TPU v7x, 512 devices: a whole 4x4x16 slice. The times are simulated.
512 devices in a mesh: region: 64 (over z, y), depth: 8 (over x, core).
Axes of the slice: x: 4, y: 4, z: 16, core: 2. Of those that a mesh axis runs over, the one named last changes fastest.
Arguments:
- adjoint_seed: float32 [64, 16, 8192], P('depth', None, 'region'), may hold values from -6 to 6
- column_lengths: int32 [8192], P('region'), may hold values from 1 to 64
- lateral_tiles: bfloat16 [384, 8192, 128], P('depth', 'region'), may hold values from -0.0546875 to 0.0546875
- lateral_rows: int32 [384, 64], P('depth', 'region'), may hold values from 0 to 7
- lateral_sides: int32 [384, 64], P('depth', 'region'), may hold values from 0 to 2
- lateral_targets: int32 [384, 64], P('depth', 'region'), may hold values from 0 to 7
- lateral_counts: int32 [8, 64], P('depth', 'region'), may hold values from 12 to 48, as said below
- vertical_tiles: bfloat16 [128, 8192, 128], P('depth', 'region'), may hold values from -0.09375 to 0.09375
- vertical_rows: int32 [128, 64], P('depth', 'region'), may hold values from 0 to 7
- vertical_peers: int32 [128, 64], P('depth', 'region'), may hold values from 0 to 7
- vertical_targets: int32 [128, 64], P('depth', 'region'), may hold values from 0 to 7
Outputs:
- adjoint: float32 [64, 16, 8192], P('depth', None, 'region')
Inputs may be any that keep to these rules, and one draw needn't show every extreme that they name: `lateral_counts`: some device uses all 48 slots in every draw.
All inputs are finite; a program needn't handle non-finite values.
Results may differ from a plain program's by a relative error of at most 0.0075.
Values may be sent and summed in bfloat16 or wider, within the bound.
No kernel may reach another device: no remote copies, remote signals or barrier semaphores. Data moves between devices by JAX's collectives and lax.ppermute only.
A program may use at most 64 MiB of HBM per device.

v0:
```python
import jax
import jax.numpy as jnp
from jax import lax
from jax.sharding import PartitionSpec as P

STEPS = 12


def passed_along(value, axis, by):
    devices = lax.axis_size(axis)
    return lax.ppermute(value, axis, [(i, (i + by) % devices) for i in range(devices)])


def partial_sums(adjoint, picker, tile_set, placer):
    rounded = adjoint.astype(jnp.bfloat16)
    picked = jnp.einsum("kb,btc->ktc", picker, rounded, preferred_element_type=jnp.float32).astype(
        jnp.bfloat16
    )
    product = jnp.einsum("ktc,kce->kte", picked, tile_set, preferred_element_type=jnp.float32)
    summed = jnp.einsum("kj,kte->jte", placer, product, precision=lax.Precision.HIGHEST)
    return summed.astype(jnp.bfloat16)


def local(
    adjoint_seed,
    column_lengths,
    lateral_tiles,
    lateral_rows,
    lateral_sides,
    lateral_targets,
    lateral_counts,
    vertical_tiles,
    vertical_rows,
    vertical_peers,
    vertical_targets,
):
    levels_here = adjoint_seed.shape[0]
    tracer_count = adjoint_seed.shape[1]
    tile_cells = adjoint_seed.shape[2]
    depth_count = lax.axis_size("depth")
    levels = lax.axis_index("depth") * levels_here + jnp.arange(levels_here, dtype=jnp.int32)
    wet_mask = (levels[:, None] < column_lengths[None, :]).astype(jnp.float32)[:, None, :]
    level_ids = jnp.arange(levels_here, dtype=jnp.int32)
    lateral_slots = lateral_tiles.shape[0]
    in_use = jnp.arange(lateral_slots, dtype=jnp.int32) < lateral_counts[0, 0]
    lateral_picker = (lateral_rows[:, 0][:, None] == level_ids[None, :]).astype(jnp.bfloat16)
    lateral_target = lateral_sides[:, 0] * levels_here + lateral_targets[:, 0]
    lateral_ids = jnp.arange(3 * levels_here, dtype=jnp.int32)
    lateral_placer = ((lateral_target[:, None] == lateral_ids[None, :]) & in_use[:, None]).astype(
        jnp.float32
    )
    vertical_picker = (vertical_rows[:, 0][:, None] == level_ids[None, :]).astype(jnp.bfloat16)
    vertical_target = vertical_peers[:, 0] * levels_here + vertical_targets[:, 0]
    vertical_ids = jnp.arange(depth_count * levels_here, dtype=jnp.int32)
    vertical_placer = (vertical_target[:, None] == vertical_ids[None, :]).astype(jnp.float32)

    def advance(step_index, adjoint):
        partial_value = partial_sums(adjoint, vertical_picker, vertical_tiles, vertical_placer)
        returned = lax.all_to_all(partial_value, "depth", split_axis=0, concat_axis=0, tiled=True)
        incoming = jnp.sum(
            returned.astype(jnp.float32).reshape(
                depth_count, levels_here, tracer_count, tile_cells
            ),
            axis=0,
        )
        adjoint = wet_mask * (adjoint + incoming)
        lateral = partial_sums(adjoint, lateral_picker, lateral_tiles, lateral_placer).reshape(
            3, levels_here, tracer_count, tile_cells
        )
        from_left = passed_along(lateral[2], "region", 1)
        from_right = passed_along(lateral[0], "region", -1)
        incoming = (
            lateral[1].astype(jnp.float32)
            + from_left.astype(jnp.float32)
            + from_right.astype(jnp.float32)
        )
        return wet_mask * (adjoint + incoming)

    adjoint = wet_mask * adjoint_seed
    return lax.fori_loop(0, STEPS, advance, adjoint)


def solution(mesh):
    return jax.shard_map(
        local,
        mesh=mesh,
        in_specs=(
            P("depth", None, "region"),
            P("region"),
            P("depth", "region", None),
            P("depth", "region"),
            P("depth", "region"),
            P("depth", "region"),
            P("depth", "region"),
            P("depth", "region", None),
            P("depth", "region"),
            P("depth", "region"),
            P("depth", "region"),
        ),
        out_specs=P("depth", None, "region"),
        check_vma=False,
    )
```

profile of v0, /device:TPU:1, one launch (start us, length us, event | category | flops | bytes accessed | tf_op | source)
XLA Modules:
  0.0 342.9 jit_solution(18200345843055934057)
XLA Ops:
  3.6 338.6 %while.11 = (s32[]{:T(128)}, f32[8,16,128]{2,0,1:T(8,128)S(1)}, bf16[16,128,128]{2,1,0:T(8,128)(2,1)}, bf16[48,128,128]{2,1,0:T(8,128)(2,1)}, s32[128]{0:T(128)}...) while((s32[]{:T(128)}, f32[8,16,128]{2,0,1:T(8,128)S(1)}, ...), condition=%wide.region_2.0_spmd.clone, body=%wide.region_0.0_spmd.clone.sunk | while | flops 89907584 | bytes 12861577 | solution.py:80
  7.5 10.2 %all-to-all-start = ((bf16[64,16,128]{2,1,0:T(8,128)(2,1)}), bf16[64,16,128]{2,1,0:T(8,128)(2,1)S(1)}, u32[]{:S(2)}, u32[]{:S(2)}) async-start(bf16[64,16,128]{2,1,0:T(8,128)(2,1)} %copy.55), calls=%async_computation | async-start | bytes 524288 | tf_op jit(solution)/shard_map/while/body/eval_jaxpr/all_to_all | solution.py:59
  17.8 6.4 %all-to-all-done = bf16[64,16,128]{2,1,0:T(8,128)(2,1)S(1)} async-done(((bf16[64,16,128]{2,1,0:T(8,128)(2,1)}), bf16[64,16,128]{2,1,0:T(8,128)(2,1)S(1)}, u32[]{:S(2)}, u32[]{:S(2)}) %all-to-all-start) | async-done | bytes 262176 | tf_op jit(solution)/shard_map/while/body/eval_jaxpr/all_to_all | solution.py:59
  25.5 9.2 %collective-permute-start = (bf16[8,16,128]{2,0,1:T(8,128)(2,1)S(1)}, bf16[8,16,128]{2,0,1:T(8,128)(2,1)S(1)}, u32[]{:S(2)}, u32[]{:S(2)}) collective-permute-start(bf16[8,16,128]{2,0,1:T(8,128)(2,1)S(1)} %get-tuple-element.181), channel_id=1, source_target_pairs={{0,504},{8,0},{16,8},{24,16},{32,24},{40,32},{48,40},{56,48},{64,5... | collective-permute-start | bytes 98312 | tf_op jit(solution)/shard_map/while/body/eval_jaxpr/ppermute | solution.py:11
  36.7 6.0 %collective-permute-done.1 = bf16[8,16,128]{2,0,1:T(8,128)(2,1)S(1)} collective-permute-done((bf16[8,16,128]{2,0,1:T(8,128)(2,1)S(1)}, bf16[8,16,128]{2,0,1:T(8,128)(2,1)S(1)}, u32[]{:S(2)}, u32[]{:S(2)}) %collective-permute-start.1) | collective-permute-done | bytes 32800 | tf_op jit(solution)/shard_map/while/body/eval_jaxpr/ppermute | solution.py:11
  46.6 5.8 %all-to-all-start = ((bf16[64,16,128]{2,1,0:T(8,128)(2,1)}), bf16[64,16,128]{2,1,0:T(8,128)(2,1)S(1)}, u32[]{:S(2)}, u32[]{:S(2)}) async-start(bf16[64,16,128]{2,1,0:T(8,128)(2,1)} %copy.55), calls=%async_computation | async-start | bytes 524288 | tf_op jit(solution)/shard_map/while/body/eval_jaxpr/all_to_all | solution.py:59
  52.5 6.4 %all-to-all-done = bf16[64,16,128]{2,1,0:T(8,128)(2,1)S(1)} async-done(((bf16[64,16,128]{2,1,0:T(8,128)(2,1)}), bf16[64,16,128]{2,1,0:T(8,128)(2,1)S(1)}, u32[]{:S(2)}, u32[]{:S(2)}) %all-to-all-start) | async-done | bytes 262176 | tf_op jit(solution)/shard_map/while/body/eval_jaxpr/all_to_all | solution.py:59
  74.1 5.5 %all-to-all-start = ((bf16[64,16,128]{2,1,0:T(8,128)(2,1)}), bf16[64,16,128]{2,1,0:T(8,128)(2,1)S(1)}, u32[]{:S(2)}, u32[]{:S(2)}) async-start(bf16[64,16,128]{2,1,0:T(8,128)(2,1)} %copy.55), calls=%async_computation | async-start | bytes 524288 | tf_op jit(solution)/shard_map/while/body/eval_jaxpr/all_to_all | solution.py:59
  79.7 6.4 %all-to-all-done = bf16[64,16,128]{2,1,0:T(8,128)(2,1)S(1)} async-done(((bf16[64,16,128]{2,1,0:T(8,128)(2,1)}), bf16[64,16,128]{2,1,0:T(8,128)(2,1)S(1)}, u32[]{:S(2)}, u32[]{:S(2)}) %all-to-all-start) | async-done | bytes 262176 | tf_op jit(solution)/shard_map/while/body/eval_jaxpr/all_to_all | solution.py:59
  101.3 5.5 %all-to-all-start = ((bf16[64,16,128]{2,1,0:T(8,128)(2,1)}), bf16[64,16,128]{2,1,0:T(8,128)(2,1)S(1)}, u32[]{:S(2)}, u32[]{:S(2)}) async-start(bf16[64,16,128]{2,1,0:T(8,128)(2,1)} %copy.55), calls=%async_computation | async-start | bytes 524288 | tf_op jit(solution)/shard_map/while/body/eval_jaxpr/all_to_all | solution.py:59
  106.9 6.4 %all-to-all-done = bf16[64,16,128]{2,1,0:T(8,128)(2,1)S(1)} async-done(((bf16[64,16,128]{2,1,0:T(8,128)(2,1)}), bf16[64,16,128]{2,1,0:T(8,128)(2,1)S(1)}, u32[]{:S(2)}, u32[]{:S(2)}) %all-to-all-start) | async-done | bytes 262176 | tf_op jit(solution)/shard_map/while/body/eval_jaxpr/all_to_all | solution.py:59
  128.5 5.5 %all-to-all-start = ((bf16[64,16,128]{2,1,0:T(8,128)(2,1)}), bf16[64,16,128]{2,1,0:T(8,128)(2,1)S(1)}, u32[]{:S(2)}, u32[]{:S(2)}) async-start(bf16[64,16,128]{2,1,0:T(8,128)(2,1)} %copy.55), calls=%async_computation | async-start | bytes 524288 | tf_op jit(solution)/shard_map/while/body/eval_jaxpr/all_to_all | solution.py:59
  134.1 6.4 %all-to-all-done = bf16[64,16,128]{2,1,0:T(8,128)(2,1)S(1)} async-done(((bf16[64,16,128]{2,1,0:T(8,128)(2,1)}), bf16[64,16,128]{2,1,0:T(8,128)(2,1)S(1)}, u32[]{:S(2)}, u32[]{:S(2)}) %all-to-all-start) | async-done | bytes 262176 | tf_op jit(solution)/shard_map/while/body/eval_jaxpr/all_to_all | solution.py:59
  155.7 5.5 %all-to-all-start = ((bf16[64,16,128]{2,1,0:T(8,128)(2,1)}), bf16[64,16,128]{2,1,0:T(8,128)(2,1)S(1)}, u32[]{:S(2)}, u32[]{:S(2)}) async-start(bf16[64,16,128]{2,1,0:T(8,128)(2,1)} %copy.55), calls=%async_computation | async-start | bytes 524288 | tf_op jit(solution)/shard_map/while/body/eval_jaxpr/all_to_all | solution.py:59
  161.3 6.4 %all-to-all-done = bf16[64,16,128]{2,1,0:T(8,128)(2,1)S(1)} async-done(((bf16[64,16,128]{2,1,0:T(8,128)(2,1)}), bf16[64,16,128]{2,1,0:T(8,128)(2,1)S(1)}, u32[]{:S(2)}, u32[]{:S(2)}) %all-to-all-start) | async-done | bytes 262176 | tf_op jit(solution)/shard_map/while/body/eval_jaxpr/all_to_all | solution.py:59
  182.9 5.5 %all-to-all-start = ((bf16[64,16,128]{2,1,0:T(8,128)(2,1)}), bf16[64,16,128]{2,1,0:T(8,128)(2,1)S(1)}, u32[]{:S(2)}, u32[]{:S(2)}) async-start(bf16[64,16,128]{2,1,0:T(8,128)(2,1)} %copy.55), calls=%async_computation | async-start | bytes 524288 | tf_op jit(solution)/shard_map/while/body/eval_jaxpr/all_to_all | solution.py:59
  188.5 6.4 %all-to-all-done = bf16[64,16,128]{2,1,0:T(8,128)(2,1)S(1)} async-done(((bf16[64,16,128]{2,1,0:T(8,128)(2,1)}), bf16[64,16,128]{2,1,0:T(8,128)(2,1)S(1)}, u32[]{:S(2)}, u32[]{:S(2)}) %all-to-all-start) | async-done | bytes 262176 | tf_op jit(solution)/shard_map/while/body/eval_jaxpr/all_to_all | solution.py:59
  210.1 5.5 %all-to-all-start = ((bf16[64,16,128]{2,1,0:T(8,128)(2,1)}), bf16[64,16,128]{2,1,0:T(8,128)(2,1)S(1)}, u32[]{:S(2)}, u32[]{:S(2)}) async-start(bf16[64,16,128]{2,1,0:T(8,128)(2,1)} %copy.55), calls=%async_computation | async-start | bytes 524288 | tf_op jit(solution)/shard_map/while/body/eval_jaxpr/all_to_all | solution.py:59
  215.7 6.4 %all-to-all-done = bf16[64,16,128]{2,1,0:T(8,128)(2,1)S(1)} async-done(((bf16[64,16,128]{2,1,0:T(8,128)(2,1)}), bf16[64,16,128]{2,1,0:T(8,128)(2,1)S(1)}, u32[]{:S(2)}, u32[]{:S(2)}) %all-to-all-start) | async-done | bytes 262176 | tf_op jit(solution)/shard_map/while/body/eval_jaxpr/all_to_all | solution.py:59
  237.3 5.5 %all-to-all-start = ((bf16[64,16,128]{2,1,0:T(8,128)(2,1)}), bf16[64,16,128]{2,1,0:T(8,128)(2,1)S(1)}, u32[]{:S(2)}, u32[]{:S(2)}) async-start(bf16[64,16,128]{2,1,0:T(8,128)(2,1)} %copy.55), calls=%async_computation | async-start | bytes 524288 | tf_op jit(solution)/shard_map/while/body/eval_jaxpr/all_to_all | solution.py:59
  242.9 6.4 %all-to-all-done = bf16[64,16,128]{2,1,0:T(8,128)(2,1)S(1)} async-done(((bf16[64,16,128]{2,1,0:T(8,128)(2,1)}), bf16[64,16,128]{2,1,0:T(8,128)(2,1)S(1)}, u32[]{:S(2)}, u32[]{:S(2)}) %all-to-all-start) | async-done | bytes 262176 | tf_op jit(solution)/shard_map/while/body/eval_jaxpr/all_to_all | solution.py:59
  270.1 6.4 %all-to-all-done = bf16[64,16,128]{2,1,0:T(8,128)(2,1)S(1)} async-done(((bf16[64,16,128]{2,1,0:T(8,128)(2,1)}), bf16[64,16,128]{2,1,0:T(8,128)(2,1)S(1)}, u32[]{:S(2)}, u32[]{:S(2)}) %all-to-all-start) | async-done | bytes 262176 | tf_op jit(solution)/shard_map/while/body/eval_jaxpr/all_to_all | solution.py:59
  297.3 6.4 %all-to-all-done = bf16[64,16,128]{2,1,0:T(8,128)(2,1)S(1)} async-done(((bf16[64,16,128]{2,1,0:T(8,128)(2,1)}), bf16[64,16,128]{2,1,0:T(8,128)(2,1)S(1)}, u32[]{:S(2)}, u32[]{:S(2)}) %all-to-all-start) | async-done | bytes 262176 | tf_op jit(solution)/shard_map/while/body/eval_jaxpr/all_to_all | solution.py:59
  324.5 6.4 %all-to-all-done = bf16[64,16,128]{2,1,0:T(8,128)(2,1)S(1)} async-done(((bf16[64,16,128]{2,1,0:T(8,128)(2,1)}), bf16[64,16,128]{2,1,0:T(8,128)(2,1)S(1)}, u32[]{:S(2)}, u32[]{:S(2)}) %all-to-all-start) | async-done | bytes 262176 | tf_op jit(solution)/shard_map/while/body/eval_jaxpr/all_to_all | solution.py:59
  (260 shorter events, 193.8 us)
Async XLA Ops:
  7.5 16.7 %all-to-all-start = ((bf16[64,16,128]{2,1,0:T(8,128)(2,1)}), bf16[64,16,128]{2,1,0:T(8,128)(2,1)S(1)}, u32[]{:S(2)}, u32[]{:S(2)}) async-start(bf16[64,16,128]{2,1,0:T(8,128)(2,1)} %copy.55), calls=%async_computation | async-start | bytes 524288 | tf_op jit(solution)/shard_map/while/body/eval_jaxpr/all_to_all | solution.py:59
  25.5 11.1 %collective-permute-start = (bf16[8,16,128]{2,0,1:T(8,128)(2,1)S(1)}, bf16[8,16,128]{2,0,1:T(8,128)(2,1)S(1)}, u32[]{:S(2)}, u32[]{:S(2)}) collective-permute-start(bf16[8,16,128]{2,0,1:T(8,128)(2,1)S(1)} %get-tuple-element.181), channel_id=1, source_target_pairs={{0,504},{8,0},{16,8},{24,16},{32,24},{40,32},{48,40},{56,48},{64,5... | collective-permute-start | bytes 98312 | tf_op jit(solution)/shard_map/while/body/eval_jaxpr/ppermute | solution.py:11
  46.6 12.3 %all-to-all-start = ((bf16[64,16,128]{2,1,0:T(8,128)(2,1)}), bf16[64,16,128]{2,1,0:T(8,128)(2,1)S(1)}, u32[]{:S(2)}, u32[]{:S(2)}) async-start(bf16[64,16,128]{2,1,0:T(8,128)(2,1)} %copy.55), calls=%async_computation | async-start | bytes 524288 | tf_op jit(solution)/shard_map/while/body/eval_jaxpr/all_to_all | solution.py:59
  62.2 8.0 %collective-permute-start.1 = (bf16[8,16,128]{2,0,1:T(8,128)(2,1)S(1)}, bf16[8,16,128]{2,0,1:T(8,128)(2,1)S(1)}, u32[]{:S(2)}, u32[]{:S(2)}) collective-permute-start(bf16[8,16,128]{2,0,1:T(8,128)(2,1)S(1)} %get-tuple-element.182), channel_id=1, source_target_pairs={{0,8},{8,16},{16,24},{24,32},{32,40},{40,48},{48,56},{56,64},{64,7... | collective-permute-start | bytes 98312 | tf_op jit(solution)/shard_map/while/body/eval_jaxpr/ppermute | solution.py:11
  74.1 12.0 %all-to-all-start = ((bf16[64,16,128]{2,1,0:T(8,128)(2,1)}), bf16[64,16,128]{2,1,0:T(8,128)(2,1)S(1)}, u32[]{:S(2)}, u32[]{:S(2)}) async-start(bf16[64,16,128]{2,1,0:T(8,128)(2,1)} %copy.55), calls=%async_computation | async-start | bytes 524288 | tf_op jit(solution)/shard_map/while/body/eval_jaxpr/all_to_all | solution.py:59
  89.4 8.0 %collective-permute-start.1 = (bf16[8,16,128]{2,0,1:T(8,128)(2,1)S(1)}, bf16[8,16,128]{2,0,1:T(8,128)(2,1)S(1)}, u32[]{:S(2)}, u32[]{:S(2)}) collective-permute-start(bf16[8,16,128]{2,0,1:T(8,128)(2,1)S(1)} %get-tuple-element.182), channel_id=1, source_target_pairs={{0,8},{8,16},{16,24},{24,32},{32,40},{40,48},{48,56},{56,64},{64,7... | collective-permute-start | bytes 98312 | tf_op jit(solution)/shard_map/while/body/eval_jaxpr/ppermute | solution.py:11
  101.3 12.0 %all-to-all-start = ((bf16[64,16,128]{2,1,0:T(8,128)(2,1)}), bf16[64,16,128]{2,1,0:T(8,128)(2,1)S(1)}, u32[]{:S(2)}, u32[]{:S(2)}) async-start(bf16[64,16,128]{2,1,0:T(8,128)(2,1)} %copy.55), calls=%async_computation | async-start | bytes 524288 | tf_op jit(solution)/shard_map/while/body/eval_jaxpr/all_to_all | solution.py:59
  116.6 8.0 %collective-permute-start.1 = (bf16[8,16,128]{2,0,1:T(8,128)(2,1)S(1)}, bf16[8,16,128]{2,0,1:T(8,128)(2,1)S(1)}, u32[]{:S(2)}, u32[]{:S(2)}) collective-permute-start(bf16[8,16,128]{2,0,1:T(8,128)(2,1)S(1)} %get-tuple-element.182), channel_id=1, source_target_pairs={{0,8},{8,16},{16,24},{24,32},{32,40},{40,48},{48,56},{56,64},{64,7... | collective-permute-start | bytes 98312 | tf_op jit(solution)/shard_map/while/body/eval_jaxpr/ppermute | solution.py:11
  128.5 12.0 %all-to-all-start = ((bf16[64,16,128]{2,1,0:T(8,128)(2,1)}), bf16[64,16,128]{2,1,0:T(8,128)(2,1)S(1)}, u32[]{:S(2)}, u32[]{:S(2)}) async-start(bf16[64,16,128]{2,1,0:T(8,128)(2,1)} %copy.55), calls=%async_computation | async-start | bytes 524288 | tf_op jit(solution)/shard_map/while/body/eval_jaxpr/all_to_all | solution.py:59
  143.8 8.0 %collective-permute-start.1 = (bf16[8,16,128]{2,0,1:T(8,128)(2,1)S(1)}, bf16[8,16,128]{2,0,1:T(8,128)(2,1)S(1)}, u32[]{:S(2)}, u32[]{:S(2)}) collective-permute-start(bf16[8,16,128]{2,0,1:T(8,128)(2,1)S(1)} %get-tuple-element.182), channel_id=1, source_target_pairs={{0,8},{8,16},{16,24},{24,32},{32,40},{40,48},{48,56},{56,64},{64,7... | collective-permute-start | bytes 98312 | tf_op jit(solution)/shard_map/while/body/eval_jaxpr/ppermute | solution.py:11
  155.7 12.0 %all-to-all-start = ((bf16[64,16,128]{2,1,0:T(8,128)(2,1)}), bf16[64,16,128]{2,1,0:T(8,128)(2,1)S(1)}, u32[]{:S(2)}, u32[]{:S(2)}) async-start(bf16[64,16,128]{2,1,0:T(8,128)(2,1)} %copy.55), calls=%async_computation | async-start | bytes 524288 | tf_op jit(solution)/shard_map/while/body/eval_jaxpr/all_to_all | solution.py:59
  171.0 8.0 %collective-permute-start.1 = (bf16[8,16,128]{2,0,1:T(8,128)(2,1)S(1)}, bf16[8,16,128]{2,0,1:T(8,128)(2,1)S(1)}, u32[]{:S(2)}, u32[]{:S(2)}) collective-permute-start(bf16[8,16,128]{2,0,1:T(8,128)(2,1)S(1)} %get-tuple-element.182), channel_id=1, source_target_pairs={{0,8},{8,16},{16,24},{24,32},{32,40},{40,48},{48,56},{56,64},{64,7... | collective-permute-start | bytes 98312 | tf_op jit(solution)/shard_map/while/body/eval_jaxpr/ppermute | solution.py:11
  182.9 12.0 %all-to-all-start = ((bf16[64,16,128]{2,1,0:T(8,128)(2,1)}), bf16[64,16,128]{2,1,0:T(8,128)(2,1)S(1)}, u32[]{:S(2)}, u32[]{:S(2)}) async-start(bf16[64,16,128]{2,1,0:T(8,128)(2,1)} %copy.55), calls=%async_computation | async-start | bytes 524288 | tf_op jit(solution)/shard_map/while/body/eval_jaxpr/all_to_all | solution.py:59
  198.2 8.0 %collective-permute-start.1 = (bf16[8,16,128]{2,0,1:T(8,128)(2,1)S(1)}, bf16[8,16,128]{2,0,1:T(8,128)(2,1)S(1)}, u32[]{:S(2)}, u32[]{:S(2)}) collective-permute-start(bf16[8,16,128]{2,0,1:T(8,128)(2,1)S(1)} %get-tuple-element.182), channel_id=1, source_target_pairs={{0,8},{8,16},{16,24},{24,32},{32,40},{40,48},{48,56},{56,64},{64,7... | collective-permute-start | bytes 98312 | tf_op jit(solution)/shard_map/while/body/eval_jaxpr/ppermute | solution.py:11
  210.1 12.0 %all-to-all-start = ((bf16[64,16,128]{2,1,0:T(8,128)(2,1)}), bf16[64,16,128]{2,1,0:T(8,128)(2,1)S(1)}, u32[]{:S(2)}, u32[]{:S(2)}) async-start(bf16[64,16,128]{2,1,0:T(8,128)(2,1)} %copy.55), calls=%async_computation | async-start | bytes 524288 | tf_op jit(solution)/shard_map/while/body/eval_jaxpr/all_to_all | solution.py:59
  225.4 8.0 %collective-permute-start.1 = (bf16[8,16,128]{2,0,1:T(8,128)(2,1)S(1)}, bf16[8,16,128]{2,0,1:T(8,128)(2,1)S(1)}, u32[]{:S(2)}, u32[]{:S(2)}) collective-permute-start(bf16[8,16,128]{2,0,1:T(8,128)(2,1)S(1)} %get-tuple-element.182), channel_id=1, source_target_pairs={{0,8},{8,16},{16,24},{24,32},{32,40},{40,48},{48,56},{56,64},{64,7... | collective-permute-start | bytes 98312 | tf_op jit(solution)/shard_map/while/body/eval_jaxpr/ppermute | solution.py:11
  237.3 12.0 %all-to-all-start = ((bf16[64,16,128]{2,1,0:T(8,128)(2,1)}), bf16[64,16,128]{2,1,0:T(8,128)(2,1)S(1)}, u32[]{:S(2)}, u32[]{:S(2)}) async-start(bf16[64,16,128]{2,1,0:T(8,128)(2,1)} %copy.55), calls=%async_computation | async-start | bytes 524288 | tf_op jit(solution)/shard_map/while/body/eval_jaxpr/all_to_all | solution.py:59
  252.6 8.0 %collective-permute-start.1 = (bf16[8,16,128]{2,0,1:T(8,128)(2,1)S(1)}, bf16[8,16,128]{2,0,1:T(8,128)(2,1)S(1)}, u32[]{:S(2)}, u32[]{:S(2)}) collective-permute-start(bf16[8,16,128]{2,0,1:T(8,128)(2,1)S(1)} %get-tuple-element.182), channel_id=1, source_target_pairs={{0,8},{8,16},{16,24},{24,32},{32,40},{40,48},{48,56},{56,64},{64,7... | collective-permute-start | bytes 98312 | tf_op jit(solution)/shard_map/while/body/eval_jaxpr/ppermute | solution.py:11
  264.5 12.0 %all-to-all-start = ((bf16[64,16,128]{2,1,0:T(8,128)(2,1)}), bf16[64,16,128]{2,1,0:T(8,128)(2,1)S(1)}, u32[]{:S(2)}, u32[]{:S(2)}) async-start(bf16[64,16,128]{2,1,0:T(8,128)(2,1)} %copy.55), calls=%async_computation | async-start | bytes 524288 | tf_op jit(solution)/shard_map/while/body/eval_jaxpr/all_to_all | solution.py:59
  279.8 8.0 %collective-permute-start.1 = (bf16[8,16,128]{2,0,1:T(8,128)(2,1)S(1)}, bf16[8,16,128]{2,0,1:T(8,128)(2,1)S(1)}, u32[]{:S(2)}, u32[]{:S(2)}) collective-permute-start(bf16[8,16,128]{2,0,1:T(8,128)(2,1)S(1)} %get-tuple-element.182), channel_id=1, source_target_pairs={{0,8},{8,16},{16,24},{24,32},{32,40},{40,48},{48,56},{56,64},{64,7... | collective-permute-start | bytes 98312 | tf_op jit(solution)/shard_map/while/body/eval_jaxpr/ppermute | solution.py:11
  291.7 12.0 %all-to-all-start = ((bf16[64,16,128]{2,1,0:T(8,128)(2,1)}), bf16[64,16,128]{2,1,0:T(8,128)(2,1)S(1)}, u32[]{:S(2)}, u32[]{:S(2)}) async-start(bf16[64,16,128]{2,1,0:T(8,128)(2,1)} %copy.55), calls=%async_computation | async-start | bytes 524288 | tf_op jit(solution)/shard_map/while/body/eval_jaxpr/all_to_all | solution.py:59
  307.0 8.0 %collective-permute-start.1 = (bf16[8,16,128]{2,0,1:T(8,128)(2,1)S(1)}, bf16[8,16,128]{2,0,1:T(8,128)(2,1)S(1)}, u32[]{:S(2)}, u32[]{:S(2)}) collective-permute-start(bf16[8,16,128]{2,0,1:T(8,128)(2,1)S(1)} %get-tuple-element.182), channel_id=1, source_target_pairs={{0,8},{8,16},{16,24},{24,32},{32,40},{40,48},{48,56},{56,64},{64,7... | collective-permute-start | bytes 98312 | tf_op jit(solution)/shard_map/while/body/eval_jaxpr/ppermute | solution.py:11
  318.9 12.0 %all-to-all-start = ((bf16[64,16,128]{2,1,0:T(8,128)(2,1)}), bf16[64,16,128]{2,1,0:T(8,128)(2,1)S(1)}, u32[]{:S(2)}, u32[]{:S(2)}) async-start(bf16[64,16,128]{2,1,0:T(8,128)(2,1)} %copy.55), calls=%async_computation | async-start | bytes 524288 | tf_op jit(solution)/shard_map/while/body/eval_jaxpr/all_to_all | solution.py:59
  334.2 8.0 %collective-permute-start.1 = (bf16[8,16,128]{2,0,1:T(8,128)(2,1)S(1)}, bf16[8,16,128]{2,0,1:T(8,128)(2,1)S(1)}, u32[]{:S(2)}, u32[]{:S(2)}) collective-permute-start(bf16[8,16,128]{2,0,1:T(8,128)(2,1)S(1)} %get-tuple-element.182), channel_id=1, source_target_pairs={{0,8},{8,16},{16,24},{24,32},{32,40},{40,48},{48,56},{56,64},{64,7... | collective-permute-start | bytes 98312 | tf_op jit(solution)/shard_map/while/body/eval_jaxpr/ppermute | solution.py:11
  (48 other events, 579.2 us)
where the time goes:
time: 345 us; the launch traced here: 343 us
  starting transfers between devices  140 us (41%)
  waiting for transfers between devices  134 us (39%)
  matrix products  50.2 us (15%)
  local copies, waits for them, and re-layouts  11.5 us (3%)
  other arithmetic  4.94 us (1%)
    all_to_all x12, waiting for transfers between devices, advance(): lax.all_to_all(partial_value, 'depth', split_axis=0, concat_axis=0, tiled...  77.4 us
    all_to_all x12, starting transfers between devices, advance(): lax.all_to_all(partial_value, 'depth', split_axis=0, concat_axis=0, tiled...  70.9 us
    ppermute x24, starting transfers between devices, passed_along(): lax.ppermute(value, axis, [(i, (i + by) % devices) for i in range(devices)])  69.2 us
    ppermute x24, waiting for transfers between devices, passed_along(): lax.ppermute(value, axis, [(i, (i + by) % devices) for i in range(devices)])  56.7 us
    dot_general x24, matrix products, partial_sums(): jnp.einsum('ktc,kce->kte', picked, tile_set, preferred_element_type=jnp.f...  21.6 us
    dot_general x24, matrix products, partial_sums(): jnp.einsum('kb,btc->ktc', picker, rounded, preferred_element_type=jnp.flo...  14.8 us
    dot_general x24, matrix products, partial_sums(): jnp.einsum('kj,kte->jte', placer, product, precision=lax.Precision.HIGHEST)  13.9 us
    convert_element_type x12, local copies, waits for them, and re-layouts, partial_sums(): return summed.astype(jnp.bfloat16)  10.5 us
  transfers between devices with their start and end apart: 36, of which 24 were waited for; matrix products, arithmetic and copies ran while one was open for 0% of the time, Pallas kernels for 0%

commit v1 on v0

v1 whole, which is shorter than its diff:
```python
import functools

import jax
import jax.numpy as jnp
from jax import lax
from jax.experimental import pallas as pl
from jax.experimental.pallas import tpu as pltpu
from jax.sharding import PartitionSpec as P

STEPS = 12
GROUPS = 8
PAIR = 2
BF = jnp.bfloat16
F32 = jnp.float32


def passed_along(value, axis, by):
    devices = lax.axis_size(axis)
    return lax.ppermute(value, axis, [(i, (i + by) % devices) for i in range(devices)])


def dot(a, b):
    return jnp.dot(a, b, preferred_element_type=F32)


def placed(rows, pick_left, pick_right, tiles, place, width):
    left = dot(pick_left, rows).astype(BF)
    right = dot(pick_right, rows).astype(BF)
    slots = tiles.shape[0]
    span = 4 * width
    parts = []
    for at in range(0, slots, 4):
        part = slice(at * width, at * width + span)
        lhs = jnp.concatenate([left[part], right[part]], axis=1)
        upper = jnp.concatenate([tiles[at], tiles[at + 2]], axis=1)
        lower = jnp.concatenate([tiles[at + 1], tiles[at + 3]], axis=1)
        out = dot(lhs, jnp.concatenate([upper, lower], axis=0))
        parts.append(out[: 2 * width, :128])
        parts.append(out[2 * width :, 128:])
    product = jnp.concatenate(parts, axis=0)
    high = product.astype(BF)
    low = (product - high.astype(F32)).astype(BF)
    return dot(place, high) + dot(place, low)


def vertical_kernel(base, from_left, from_right, wet, pick_left, pick_right, place, tiles, adjoint, partial):
    value = base[...] + from_left[...].astype(F32) + from_right[...].astype(F32)
    value = wet[...] * value
    adjoint[...] = value
    partial[...] = placed(value.astype(BF), pick_left[...], pick_right[...], tiles, place[...], 16).astype(BF)


def first_kernel(seed, wet, pick_left, pick_right, place, tiles, adjoint, partial):
    value = wet[...] * seed[...]
    adjoint[...] = value
    partial[...] = placed(value.astype(BF), pick_left[...], pick_right[...], tiles, place[...], 16).astype(BF)


def lateral_kernel(adjoint, returned, wet, pick_left, pick_right, place, tiles, base, to_left, to_right):
    value = adjoint[...]
    for peer in range(GROUPS):
        value = value + returned[128 * peer : 128 * (peer + 1)].astype(F32)
    value = wet[...] * value
    partial = placed(value.astype(BF), pick_left[...], pick_right[...], tiles, place[...], 16).astype(BF)
    to_left[...] = partial[:128]
    to_right[...] = partial[256:]
    base[...] = value + partial[128:256].astype(F32)


def call(body, outs, *args):
    specs = [pl.BlockSpec(memory_space=pltpu.VMEM) for _ in args]
    return pl.pallas_call(
        body,
        out_shape=[jax.ShapeDtypeStruct(shape, kind) for shape, kind in outs],
        in_specs=specs,
        out_specs=[pl.BlockSpec(memory_space=pltpu.VMEM) for _ in outs],
        compiler_params=pltpu.CompilerParams(vmem_limit_bytes=24 * 1024 * 1024),
    )(*args)


def split_rows(field):
    levels, tracers, cells = field.shape
    shaped = field.reshape(levels, GROUPS, tracers // GROUPS, cells)
    return shaped.transpose(1, 0, 2, 3).reshape(levels * tracers, cells)


def join_rows(rows, levels, tracers):
    shaped = rows.reshape(GROUPS, levels, tracers // GROUPS, rows.shape[1])
    return shaped.transpose(1, 0, 2, 3).reshape(levels, tracers, rows.shape[1])


def level_pickers(slot_rows):
    slots = slot_rows.shape[0]
    row = jnp.arange(slots * 16, dtype=jnp.int32)
    wanted = (row % 16 // PAIR) * 16 + jnp.repeat(slot_rows, 16) * PAIR + row % PAIR
    hit = wanted[:, None] == jnp.arange(128, dtype=jnp.int32)[None, :]
    even = (row // 16 % 2 == 0)[:, None]
    return (hit & even).astype(BF), (hit & ~even).astype(BF)


def level_placer(slot_blocks, slot_levels, in_use, blocks):
    slots = slot_blocks.shape[0]
    row = jnp.arange(slots * 16, dtype=jnp.int32)
    wanted = (
        jnp.repeat(slot_blocks, 16) * 128
        + (row % 16 // PAIR) * 16
        + jnp.repeat(slot_levels, 16) * PAIR
        + row % PAIR
    )
    wanted = jnp.where(jnp.repeat(in_use, 16), wanted, -1)
    return (jnp.arange(blocks * 128, dtype=jnp.int32)[:, None] == wanted[None, :]).astype(BF)


def local(
    adjoint_seed,
    column_lengths,
    lateral_tiles,
    lateral_rows,
    lateral_sides,
    lateral_targets,
    lateral_counts,
    vertical_tiles,
    vertical_rows,
    vertical_peers,
    vertical_targets,
):
    levels_here, tracers, cells = adjoint_seed.shape
    row = jnp.arange(levels_here * tracers, dtype=jnp.int32)
    level_of_row = lax.axis_index("depth") * levels_here + row % 16 // PAIR
    wet = (level_of_row[:, None] < column_lengths[None, :]).astype(F32)

    lateral_slots = lateral_tiles.shape[0]
    in_use = jnp.arange(lateral_slots, dtype=jnp.int32) < lateral_counts[0, 0]
    lateral = (
        *level_pickers(lateral_rows[:, 0]),
        level_placer(lateral_sides[:, 0], lateral_targets[:, 0], in_use, 3),
        lateral_tiles,
    )
    vertical = (
        *level_pickers(vertical_rows[:, 0]),
        level_placer(
            vertical_peers[:, 0],
            vertical_targets[:, 0],
            jnp.ones(vertical_tiles.shape[0], jnp.bool_),
            GROUPS,
        ),
        vertical_tiles,
    )
    shape = (levels_here * tracers, cells)
    state_and_partial = [(shape, F32), ((GROUPS * shape[0], cells), BF)]
    adjoint, partial = call(first_kernel, state_and_partial, split_rows(adjoint_seed), wet, *vertical)
    for step in range(STEPS):
        returned = lax.all_to_all(partial, "depth", split_axis=0, concat_axis=0, tiled=True)
        base, to_left, to_right = call(
            lateral_kernel, [(shape, F32), (shape, BF), (shape, BF)], adjoint, returned, wet, *lateral
        )
        from_left = passed_along(to_right, "region", 1)
        from_right = passed_along(to_left, "region", -1)
        if step < STEPS - 1:
            adjoint, partial = call(
                vertical_kernel, state_and_partial, base, from_left, from_right, wet, *vertical
            )
        else:
            adjoint = wet * (base + from_left.astype(F32) + from_right.astype(F32))
    return join_rows(adjoint, levels_here, tracers)


def solution(mesh):
    return jax.shard_map(
        local,
        mesh=mesh,
        in_specs=(
            P("depth", None, "region"),
            P("region"),
            P("depth", "region", None),
            P("depth", "region"),
            P("depth", "region"),
            P("depth", "region"),
            P("depth", "region"),
            P("depth", "region", None),
            P("depth", "region"),
            P("depth", "region"),
            P("depth", "region"),
        ),
        out_specs=P("depth", None, "region"),
        check_vma=False,
    )
```

time: 345 us -> 290 us (0.84)
  blocking collectives: 0 us -> 119 us
  waiting for transfers between devices: 134 us -> 15.7 us
  matrix products: 50.2 us -> 0 us
  Pallas kernels: 0 us -> 20.9 us
  starting transfers between devices: 140 us -> 122 us
  local copies, waits for them, and re-layouts: 11.5 us -> 4.41 us
    all_to_all x0 -> x11, blocking collectives: none -> 119 us  [local(): lax.all_to_all(partial, 'depth', split_axis=0, concat_axis=0, tiled=True)]
    all_to_all x12 -> x1, waiting for transfers between devices: 77.4 us -> 3.73 us  [local(): lax.all_to_all(partial, 'depth', split_axis=0, concat_axis=0, tiled=True)]
    all_to_all x12 -> x1, starting transfers between devices: 70.9 us -> 10.9 us  [local(): lax.all_to_all(partial, 'depth', split_axis=0, concat_axis=0, tiled=True)]
    dot_general x72 -> x0, matrix products: 50.2 us -> none  [the longest x24 21.6 us: partial_sums(): jnp.einsum('ktc,kce->kte', picked, tile_set, preferred_element_type=jnp.f...]
    ppermute x24, waiting for transfers between devices: 56.7 us -> 11.9 us  [passed_along(): lax.ppermute(value, axis, [(i, (i + by) % devices) for i in range(devices)])]
    ppermute x24, starting transfers between devices: 69.2 us -> 112 us  [passed_along(): lax.ppermute(value, axis, [(i, (i + by) % devices) for i in range(devices)])]
    pallas_call x0 -> x24, Pallas kernels: none -> 20.9 us  [call(): pl.pallas_call(body, out_shape=[jax.ShapeDtypeStruct(shape, kind) for sha...]
    convert_element_type x12 -> x0, local copies, waits for them, and re-layouts: 10.5 us -> none  [partial_sums(): return summed.astype(jnp.bfloat16)]
  transfers between devices with their start and end apart: 36 -> 25, of which waited for: 24 -> 13; matrix products, arithmetic and copies ran while one was open for 0% -> 1% of each run, Pallas kernels for 0% -> 0%
where the time goes in v1:
time: 290 us; the launch traced here: 288 us
  starting transfers between devices  122 us (42%)
  blocking collectives  119 us (41%)
  Pallas kernels  20.9 us (7%)
  waiting for transfers between devices  15.7 us (5%)
  other arithmetic  4.8 us (2%)
  local copies, waits for them, and re-layouts  4.41 us (2%)
    all_to_all x11, blocking collectives, local(): lax.all_to_all(partial, 'depth', split_axis=0, concat_axis=0, tiled=True)  119 us
    ppermute x24, starting transfers between devices, passed_along(): lax.ppermute(value, axis, [(i, (i + by) % devices) for i in range(devices)])  112 us
    pallas_call x24, Pallas kernels, call(): pl.pallas_call(body, out_shape=[jax.ShapeDtypeStruct(shape, kind) for sha...  20.9 us
    ppermute x24, waiting for transfers between devices, passed_along(): lax.ppermute(value, axis, [(i, (i + by) % devices) for i in range(devices)])  11.9 us
    all_to_all x1, starting transfers between devices, local(): lax.all_to_all(partial, 'depth', split_axis=0, concat_axis=0, tiled=True)  10.9 us
  transfers between devices with their start and end apart: 25, of which 13 were waited for; matrix products, arithmetic and copies ran while one was open for 1% of the time, Pallas kernels for 0%

profile of v1, /device:TPU:1, one launch (start us, length us, event | category | flops | bytes accessed | tf_op | source)
XLA Modules:
  0.0 288.3 jit_solution(13292445614448242541)
XLA Ops:
  6.1 10.9 %all-to-all-start = ((bf16[8,128,128]{2,1,0:T(8,128)(2,1)}), bf16[8,128,128]{2,1,0:T(8,128)(2,1)}, u32[]{:S(2)}, u32[]{:S(2)}) async-start(bf16[8,128,128]{2,1,0:T(8,128)(2,1)} %bitcast.6), calls=%async_computation | async-start | bytes 524288 | tf_op jit(solution)/shard_map/all_to_all | solution.py:153
  29.2 8.6 %collective-permute-start.1 = (bf16[128,128]{1,0:T(8,128)(2,1)S(1)}, bf16[128,128]{1,0:T(8,128)(2,1)S(1)}, u32[]{:S(2)}, u32[]{:S(2)}) collective-permute-start(bf16[128,128]{1,0:T(8,128)(2,1)S(1)} %get-tuple-element.69), channel_id=1, source_target_pairs={{0,504},{8,0},{16,8},{24,16},{32,24},{40,32},{48,40},{56,48},{64,5... | collective-permute-start | bytes 98312 | tf_op jit(solution)/shard_map/ppermute | solution.py:19
  39.5 10.8 %all_to_all.132 = bf16[8,128,128]{2,1,0:T(8,128)(2,1)S(1)} all-to-all(bf16[8,128,128]{2,1,0:T(8,128)(2,1)S(1)} %bitcast.59), channel_id=1, replica_groups=mesh['region'=64,'depth'=8] {'depth'}, dimensions={0} | all-to-all | bytes 524288 | tf_op jit(solution)/shard_map/all_to_all | solution.py:153
  53.1 7.3 %collective-permute-start.3 = (bf16[128,128]{1,0:T(8,128)(2,1)S(1)}, bf16[128,128]{1,0:T(8,128)(2,1)S(1)}, u32[]{:S(2)}, u32[]{:S(2)}) collective-permute-start(bf16[128,128]{1,0:T(8,128)(2,1)S(1)} %get-tuple-element.74), channel_id=1, source_target_pairs={{0,504},{8,0},{16,8},{24,16},{32,24},{40,32},{48,40},{56,48},{64,5... | collective-permute-start | bytes 98312 | tf_op jit(solution)/shard_map/ppermute | solution.py:19
  62.1 10.8 %all_to_all.133 = bf16[8,128,128]{2,1,0:T(8,128)(2,1)S(1)} all-to-all(bf16[8,128,128]{2,1,0:T(8,128)(2,1)S(1)} %bitcast.60), channel_id=1, replica_groups=mesh['region'=64,'depth'=8] {'depth'}, dimensions={0} | all-to-all | bytes 524288 | tf_op jit(solution)/shard_map/all_to_all | solution.py:153
  75.7 7.3 %collective-permute-start.5 = (bf16[128,128]{1,0:T(8,128)(2,1)S(1)}, bf16[128,128]{1,0:T(8,128)(2,1)S(1)}, u32[]{:S(2)}, u32[]{:S(2)}) collective-permute-start(bf16[128,128]{1,0:T(8,128)(2,1)S(1)} %get-tuple-element.79), channel_id=1, source_target_pairs={{0,504},{8,0},{16,8},{24,16},{32,24},{40,32},{48,40},{56,48},{64,5... | collective-permute-start | bytes 98312 | tf_op jit(solution)/shard_map/ppermute | solution.py:19
  84.8 10.8 %all_to_all.134 = bf16[8,128,128]{2,1,0:T(8,128)(2,1)S(1)} all-to-all(bf16[8,128,128]{2,1,0:T(8,128)(2,1)S(1)} %bitcast.61), channel_id=1, replica_groups=mesh['region'=64,'depth'=8] {'depth'}, dimensions={0} | all-to-all | bytes 524288 | tf_op jit(solution)/shard_map/all_to_all | solution.py:153
  98.4 7.3 %collective-permute-start.7 = (bf16[128,128]{1,0:T(8,128)(2,1)S(1)}, bf16[128,128]{1,0:T(8,128)(2,1)S(1)}, u32[]{:S(2)}, u32[]{:S(2)}) collective-permute-start(bf16[128,128]{1,0:T(8,128)(2,1)S(1)} %get-tuple-element.84), channel_id=1, source_target_pairs={{0,504},{8,0},{16,8},{24,16},{32,24},{40,32},{48,40},{56,48},{64,5... | collective-permute-start | bytes 98312 | tf_op jit(solution)/shard_map/ppermute | solution.py:19
  107.4 10.8 %all_to_all.135 = bf16[8,128,128]{2,1,0:T(8,128)(2,1)S(1)} all-to-all(bf16[8,128,128]{2,1,0:T(8,128)(2,1)S(1)} %bitcast.62), channel_id=1, replica_groups=mesh['region'=64,'depth'=8] {'depth'}, dimensions={0} | all-to-all | bytes 524288 | tf_op jit(solution)/shard_map/all_to_all | solution.py:153
  121.0 7.3 %collective-permute-start.9 = (bf16[128,128]{1,0:T(8,128)(2,1)S(1)}, bf16[128,128]{1,0:T(8,128)(2,1)S(1)}, u32[]{:S(2)}, u32[]{:S(2)}) collective-permute-start(bf16[128,128]{1,0:T(8,128)(2,1)S(1)} %get-tuple-element.89), channel_id=1, source_target_pairs={{0,504},{8,0},{16,8},{24,16},{32,24},{40,32},{48,40},{56,48},{64,5... | collective-permute-start | bytes 98312 | tf_op jit(solution)/shard_map/ppermute | solution.py:19
  130.0 10.8 %all_to_all.136 = bf16[8,128,128]{2,1,0:T(8,128)(2,1)S(1)} all-to-all(bf16[8,128,128]{2,1,0:T(8,128)(2,1)S(1)} %bitcast.63), channel_id=1, replica_groups=mesh['region'=64,'depth'=8] {'depth'}, dimensions={0} | all-to-all | bytes 524288 | tf_op jit(solution)/shard_map/all_to_all | solution.py:153
  143.6 7.3 %collective-permute-start.11 = (bf16[128,128]{1,0:T(8,128)(2,1)S(1)}, bf16[128,128]{1,0:T(8,128)(2,1)S(1)}, u32[]{:S(2)}, u32[]{:S(2)}) collective-permute-start(bf16[128,128]{1,0:T(8,128)(2,1)S(1)} %get-tuple-element.94), channel_id=1, source_target_pairs={{0,504},{8,0},{16,8},{24,16},{32,24},{40,32},{48,40},{56,48},{64,5... | collective-permute-start | bytes 98312 | tf_op jit(solution)/shard_map/ppermute | solution.py:19
  152.6 10.8 %all_to_all.137 = bf16[8,128,128]{2,1,0:T(8,128)(2,1)S(1)} all-to-all(bf16[8,128,128]{2,1,0:T(8,128)(2,1)S(1)} %bitcast.64), channel_id=1, replica_groups=mesh['region'=64,'depth'=8] {'depth'}, dimensions={0} | all-to-all | bytes 524288 | tf_op jit(solution)/shard_map/all_to_all | solution.py:153
  166.2 7.3 %collective-permute-start.13 = (bf16[128,128]{1,0:T(8,128)(2,1)S(1)}, bf16[128,128]{1,0:T(8,128)(2,1)S(1)}, u32[]{:S(2)}, u32[]{:S(2)}) collective-permute-start(bf16[128,128]{1,0:T(8,128)(2,1)S(1)} %get-tuple-element.99), channel_id=1, source_target_pairs={{0,504},{8,0},{16,8},{24,16},{32,24},{40,32},{48,40},{56,48},{64,5... | collective-permute-start | bytes 98312 | tf_op jit(solution)/shard_map/ppermute | solution.py:19
  175.2 10.8 %all_to_all.138 = bf16[8,128,128]{2,1,0:T(8,128)(2,1)S(1)} all-to-all(bf16[8,128,128]{2,1,0:T(8,128)(2,1)S(1)} %bitcast.65), channel_id=1, replica_groups=mesh['region'=64,'depth'=8] {'depth'}, dimensions={0} | all-to-all | bytes 524288 | tf_op jit(solution)/shard_map/all_to_all | solution.py:153
  188.8 7.3 %collective-permute-start.15 = (bf16[128,128]{1,0:T(8,128)(2,1)S(1)}, bf16[128,128]{1,0:T(8,128)(2,1)S(1)}, u32[]{:S(2)}, u32[]{:S(2)}) collective-permute-start(bf16[128,128]{1,0:T(8,128)(2,1)S(1)} %get-tuple-element.104), channel_id=1, source_target_pairs={{0,504},{8,0},{16,8},{24,16},{32,24},{40,32},{48,40},{56,48},{64,5... | collective-permute-start | bytes 98312 | tf_op jit(solution)/shard_map/ppermute | solution.py:19
  197.8 10.8 %all_to_all.139 = bf16[8,128,128]{2,1,0:T(8,128)(2,1)S(1)} all-to-all(bf16[8,128,128]{2,1,0:T(8,128)(2,1)S(1)} %bitcast.66), channel_id=1, replica_groups=mesh['region'=64,'depth'=8] {'depth'}, dimensions={0} | all-to-all | bytes 524288 | tf_op jit(solution)/shard_map/all_to_all | solution.py:153
  211.5 7.3 %collective-permute-start.17 = (bf16[128,128]{1,0:T(8,128)(2,1)S(1)}, bf16[128,128]{1,0:T(8,128)(2,1)S(1)}, u32[]{:S(2)}, u32[]{:S(2)}) collective-permute-start(bf16[128,128]{1,0:T(8,128)(2,1)S(1)} %get-tuple-element.109), channel_id=1, source_target_pairs={{0,504},{8,0},{16,8},{24,16},{32,24},{40,32},{48,40},{56,48},{64,5... | collective-permute-start | bytes 98312 | tf_op jit(solution)/shard_map/ppermute | solution.py:19
  220.5 10.8 %all_to_all.140 = bf16[8,128,128]{2,1,0:T(8,128)(2,1)S(1)} all-to-all(bf16[8,128,128]{2,1,0:T(8,128)(2,1)S(1)} %bitcast.67), channel_id=1, replica_groups=mesh['region'=64,'depth'=8] {'depth'}, dimensions={0} | all-to-all | bytes 524288 | tf_op jit(solution)/shard_map/all_to_all | solution.py:153
  234.1 7.3 %collective-permute-start.19 = (bf16[128,128]{1,0:T(8,128)(2,1)S(1)}, bf16[128,128]{1,0:T(8,128)(2,1)S(1)}, u32[]{:S(2)}, u32[]{:S(2)}) collective-permute-start(bf16[128,128]{1,0:T(8,128)(2,1)S(1)} %get-tuple-element.114), channel_id=1, source_target_pairs={{0,504},{8,0},{16,8},{24,16},{32,24},{40,32},{48,40},{56,48},{64,5... | collective-permute-start | bytes 98312 | tf_op jit(solution)/shard_map/ppermute | solution.py:19
  243.1 10.8 %all_to_all.141 = bf16[8,128,128]{2,1,0:T(8,128)(2,1)S(1)} all-to-all(bf16[8,128,128]{2,1,0:T(8,128)(2,1)S(1)} %bitcast.68), channel_id=1, replica_groups=mesh['region'=64,'depth'=8] {'depth'}, dimensions={0} | all-to-all | bytes 524288 | tf_op jit(solution)/shard_map/all_to_all | solution.py:153
  256.7 7.3 %collective-permute-start.21 = (bf16[128,128]{1,0:T(8,128)(2,1)S(1)}, bf16[128,128]{1,0:T(8,128)(2,1)S(1)}, u32[]{:S(2)}, u32[]{:S(2)}) collective-permute-start(bf16[128,128]{1,0:T(8,128)(2,1)S(1)} %get-tuple-element.119), channel_id=1, source_target_pairs={{0,504},{8,0},{16,8},{24,16},{32,24},{40,32},{48,40},{56,48},{64,5... | collective-permute-start | bytes 98312 | tf_op jit(solution)/shard_map/ppermute | solution.py:19
  265.7 10.8 %all_to_all.142 = bf16[8,128,128]{2,1,0:T(8,128)(2,1)S(1)} all-to-all(bf16[8,128,128]{2,1,0:T(8,128)(2,1)S(1)} %bitcast.58), channel_id=1, replica_groups=mesh['region'=64,'depth'=8] {'depth'}, dimensions={0} | all-to-all | bytes 524288 | tf_op jit(solution)/shard_map/all_to_all | solution.py:153
  279.3 7.3 %collective-permute-start.23 = (bf16[128,128]{1,0:T(8,128)(2,1)S(1)}, bf16[128,128]{1,0:T(8,128)(2,1)S(1)}, u32[]{:S(2)}, u32[]{:S(2)}) collective-permute-start(bf16[128,128]{1,0:T(8,128)(2,1)S(1)} %get-tuple-element.124), channel_id=1, source_target_pairs={{0,504},{8,0},{16,8},{24,16},{32,24},{40,32},{48,40},{56,48},{64,5... | collective-permute-start | bytes 98312 | tf_op jit(solution)/shard_map/ppermute | solution.py:19
  (119 shorter events, 68.8 us)
Async XLA Ops:
  6.1 17.6 %all-to-all-start = ((bf16[8,128,128]{2,1,0:T(8,128)(2,1)}), bf16[8,128,128]{2,1,0:T(8,128)(2,1)}, u32[]{:S(2)}, u32[]{:S(2)}) async-start(bf16[8,128,128]{2,1,0:T(8,128)(2,1)} %bitcast.6), calls=%async_computation | async-start | bytes 524288 | tf_op jit(solution)/shard_map/all_to_all | solution.py:153
  27.3 10.5 %collective-permute-start = (bf16[128,128]{1,0:T(8,128)(2,1)S(1)}, bf16[128,128]{1,0:T(8,128)(2,1)S(1)}, u32[]{:S(2)}, u32[]{:S(2)}) collective-permute-start(bf16[128,128]{1,0:T(8,128)(2,1)S(1)} %get-tuple-element.68), channel_id=1, source_target_pairs={{0,8},{8,16},{16,24},{24,32},{32,40},{40,48},{48,56},{56,64},{64,7... | collective-permute-start | bytes 98312 | tf_op jit(solution)/shard_map/ppermute | solution.py:19
  29.2 9.6 %collective-permute-start.1 = (bf16[128,128]{1,0:T(8,128)(2,1)S(1)}, bf16[128,128]{1,0:T(8,128)(2,1)S(1)}, u32[]{:S(2)}, u32[]{:S(2)}) collective-permute-start(bf16[128,128]{1,0:T(8,128)(2,1)S(1)} %get-tuple-element.69), channel_id=1, source_target_pairs={{0,504},{8,0},{16,8},{24,16},{32,24},{40,32},{48,40},{56,48},{64,5... | collective-permute-start | bytes 98312 | tf_op jit(solution)/shard_map/ppermute | solution.py:19
  51.2 9.2 %collective-permute-start.2 = (bf16[128,128]{1,0:T(8,128)(2,1)S(1)}, bf16[128,128]{1,0:T(8,128)(2,1)S(1)}, u32[]{:S(2)}, u32[]{:S(2)}) collective-permute-start(bf16[128,128]{1,0:T(8,128)(2,1)S(1)} %get-tuple-element.73), channel_id=1, source_target_pairs={{0,8},{8,16},{16,24},{24,32},{32,40},{40,48},{48,56},{56,64},{64,7... | collective-permute-start | bytes 98312 | tf_op jit(solution)/shard_map/ppermute | solution.py:19
  53.1 8.3 %collective-permute-start.3 = (bf16[128,128]{1,0:T(8,128)(2,1)S(1)}, bf16[128,128]{1,0:T(8,128)(2,1)S(1)}, u32[]{:S(2)}, u32[]{:S(2)}) collective-permute-start(bf16[128,128]{1,0:T(8,128)(2,1)S(1)} %get-tuple-element.74), channel_id=1, source_target_pairs={{0,504},{8,0},{16,8},{24,16},{32,24},{40,32},{48,40},{56,48},{64,5... | collective-permute-start | bytes 98312 | tf_op jit(solution)/shard_map/ppermute | solution.py:19
  73.8 9.2 %collective-permute-start.4 = (bf16[128,128]{1,0:T(8,128)(2,1)S(1)}, bf16[128,128]{1,0:T(8,128)(2,1)S(1)}, u32[]{:S(2)}, u32[]{:S(2)}) collective-permute-start(bf16[128,128]{1,0:T(8,128)(2,1)S(1)} %get-tuple-element.78), channel_id=1, source_target_pairs={{0,8},{8,16},{16,24},{24,32},{32,40},{40,48},{48,56},{56,64},{64,7... | collective-permute-start | bytes 98312 | tf_op jit(solution)/shard_map/ppermute | solution.py:19
  75.7 8.3 %collective-permute-start.5 = (bf16[128,128]{1,0:T(8,128)(2,1)S(1)}, bf16[128,128]{1,0:T(8,128)(2,1)S(1)}, u32[]{:S(2)}, u32[]{:S(2)}) collective-permute-start(bf16[128,128]{1,0:T(8,128)(2,1)S(1)} %get-tuple-element.79), channel_id=1, source_target_pairs={{0,504},{8,0},{16,8},{24,16},{32,24},{40,32},{48,40},{56,48},{64,5... | collective-permute-start | bytes 98312 | tf_op jit(solution)/shard_map/ppermute | solution.py:19
  96.4 9.2 %collective-permute-start.6 = (bf16[128,128]{1,0:T(8,128)(2,1)S(1)}, bf16[128,128]{1,0:T(8,128)(2,1)S(1)}, u32[]{:S(2)}, u32[]{:S(2)}) collective-permute-start(bf16[128,128]{1,0:T(8,128)(2,1)S(1)} %get-tuple-element.83), channel_id=1, source_target_pairs={{0,8},{8,16},{16,24},{24,32},{32,40},{40,48},{48,56},{56,64},{64,7... | collective-permute-start | bytes 98312 | tf_op jit(solution)/shard_map/ppermute | solution.py:19
  98.4 8.3 %collective-permute-start.7 = (bf16[128,128]{1,0:T(8,128)(2,1)S(1)}, bf16[128,128]{1,0:T(8,128)(2,1)S(1)}, u32[]{:S(2)}, u32[]{:S(2)}) collective-permute-start(bf16[128,128]{1,0:T(8,128)(2,1)S(1)} %get-tuple-element.84), channel_id=1, source_target_pairs={{0,504},{8,0},{16,8},{24,16},{32,24},{40,32},{48,40},{56,48},{64,5... | collective-permute-start | bytes 98312 | tf_op jit(solution)/shard_map/ppermute | solution.py:19
  119.1 9.2 %collective-permute-start.8 = (bf16[128,128]{1,0:T(8,128)(2,1)S(1)}, bf16[128,128]{1,0:T(8,128)(2,1)S(1)}, u32[]{:S(2)}, u32[]{:S(2)}) collective-permute-start(bf16[128,128]{1,0:T(8,128)(2,1)S(1)} %get-tuple-element.88), channel_id=1, source_target_pairs={{0,8},{8,16},{16,24},{24,32},{32,40},{40,48},{48,56},{56,64},{64,7... | collective-permute-start | bytes 98312 | tf_op jit(solution)/shard_map/ppermute | solution.py:19
  121.0 8.3 %collective-permute-start.9 = (bf16[128,128]{1,0:T(8,128)(2,1)S(1)}, bf16[128,128]{1,0:T(8,128)(2,1)S(1)}, u32[]{:S(2)}, u32[]{:S(2)}) collective-permute-start(bf16[128,128]{1,0:T(8,128)(2,1)S(1)} %get-tuple-element.89), channel_id=1, source_target_pairs={{0,504},{8,0},{16,8},{24,16},{32,24},{40,32},{48,40},{56,48},{64,5... | collective-permute-start | bytes 98312 | tf_op jit(solution)/shard_map/ppermute | solution.py:19
  141.7 9.2 %collective-permute-start.10 = (bf16[128,128]{1,0:T(8,128)(2,1)S(1)}, bf16[128,128]{1,0:T(8,128)(2,1)S(1)}, u32[]{:S(2)}, u32[]{:S(2)}) collective-permute-start(bf16[128,128]{1,0:T(8,128)(2,1)S(1)} %get-tuple-element.93), channel_id=1, source_target_pairs={{0,8},{8,16},{16,24},{24,32},{32,40},{40,48},{48,56},{56,64},{64,7... | collective-permute-start | bytes 98312 | tf_op jit(solution)/shard_map/ppermute | solution.py:19
  143.6 8.3 %collective-permute-start.11 = (bf16[128,128]{1,0:T(8,128)(2,1)S(1)}, bf16[128,128]{1,0:T(8,128)(2,1)S(1)}, u32[]{:S(2)}, u32[]{:S(2)}) collective-permute-start(bf16[128,128]{1,0:T(8,128)(2,1)S(1)} %get-tuple-element.94), channel_id=1, source_target_pairs={{0,504},{8,0},{16,8},{24,16},{32,24},{40,32},{48,40},{56,48},{64,5... | collective-permute-start | bytes 98312 | tf_op jit(solution)/shard_map/ppermute | solution.py:19
  164.3 9.2 %collective-permute-start.12 = (bf16[128,128]{1,0:T(8,128)(2,1)S(1)}, bf16[128,128]{1,0:T(8,128)(2,1)S(1)}, u32[]{:S(2)}, u32[]{:S(2)}) collective-permute-start(bf16[128,128]{1,0:T(8,128)(2,1)S(1)} %get-tuple-element.98), channel_id=1, source_target_pairs={{0,8},{8,16},{16,24},{24,32},{32,40},{40,48},{48,56},{56,64},{64,7... | collective-permute-start | bytes 98312 | tf_op jit(solution)/shard_map/ppermute | solution.py:19
  166.2 8.3 %collective-permute-start.13 = (bf16[128,128]{1,0:T(8,128)(2,1)S(1)}, bf16[128,128]{1,0:T(8,128)(2,1)S(1)}, u32[]{:S(2)}, u32[]{:S(2)}) collective-permute-start(bf16[128,128]{1,0:T(8,128)(2,1)S(1)} %get-tuple-element.99), channel_id=1, source_target_pairs={{0,504},{8,0},{16,8},{24,16},{32,24},{40,32},{48,40},{56,48},{64,5... | collective-permute-start | bytes 98312 | tf_op jit(solution)/shard_map/ppermute | solution.py:19
  186.9 9.2 %collective-permute-start.14 = (bf16[128,128]{1,0:T(8,128)(2,1)S(1)}, bf16[128,128]{1,0:T(8,128)(2,1)S(1)}, u32[]{:S(2)}, u32[]{:S(2)}) collective-permute-start(bf16[128,128]{1,0:T(8,128)(2,1)S(1)} %get-tuple-element.103), channel_id=1, source_target_pairs={{0,8},{8,16},{16,24},{24,32},{32,40},{40,48},{48,56},{56,64},{64,7... | collective-permute-start | bytes 98312 | tf_op jit(solution)/shard_map/ppermute | solution.py:19
  188.8 8.3 %collective-permute-start.15 = (bf16[128,128]{1,0:T(8,128)(2,1)S(1)}, bf16[128,128]{1,0:T(8,128)(2,1)S(1)}, u32[]{:S(2)}, u32[]{:S(2)}) collective-permute-start(bf16[128,128]{1,0:T(8,128)(2,1)S(1)} %get-tuple-element.104), channel_id=1, source_target_pairs={{0,504},{8,0},{16,8},{24,16},{32,24},{40,32},{48,40},{56,48},{64,5... | collective-permute-start | bytes 98312 | tf_op jit(solution)/shard_map/ppermute | solution.py:19
  209.5 9.2 %collective-permute-start.16 = (bf16[128,128]{1,0:T(8,128)(2,1)S(1)}, bf16[128,128]{1,0:T(8,128)(2,1)S(1)}, u32[]{:S(2)}, u32[]{:S(2)}) collective-permute-start(bf16[128,128]{1,0:T(8,128)(2,1)S(1)} %get-tuple-element.108), channel_id=1, source_target_pairs={{0,8},{8,16},{16,24},{24,32},{32,40},{40,48},{48,56},{56,64},{64,7... | collective-permute-start | bytes 98312 | tf_op jit(solution)/shard_map/ppermute | solution.py:19
  211.5 8.3 %collective-permute-start.17 = (bf16[128,128]{1,0:T(8,128)(2,1)S(1)}, bf16[128,128]{1,0:T(8,128)(2,1)S(1)}, u32[]{:S(2)}, u32[]{:S(2)}) collective-permute-start(bf16[128,128]{1,0:T(8,128)(2,1)S(1)} %get-tuple-element.109), channel_id=1, source_target_pairs={{0,504},{8,0},{16,8},{24,16},{32,24},{40,32},{48,40},{56,48},{64,5... | collective-permute-start | bytes 98312 | tf_op jit(solution)/shard_map/ppermute | solution.py:19
  232.1 9.2 %collective-permute-start.18 = (bf16[128,128]{1,0:T(8,128)(2,1)S(1)}, bf16[128,128]{1,0:T(8,128)(2,1)S(1)}, u32[]{:S(2)}, u32[]{:S(2)}) collective-permute-start(bf16[128,128]{1,0:T(8,128)(2,1)S(1)} %get-tuple-element.113), channel_id=1, source_target_pairs={{0,8},{8,16},{16,24},{24,32},{32,40},{40,48},{48,56},{56,64},{64,7... | collective-permute-start | bytes 98312 | tf_op jit(solution)/shard_map/ppermute | solution.py:19
  234.1 8.3 %collective-permute-start.19 = (bf16[128,128]{1,0:T(8,128)(2,1)S(1)}, bf16[128,128]{1,0:T(8,128)(2,1)S(1)}, u32[]{:S(2)}, u32[]{:S(2)}) collective-permute-start(bf16[128,128]{1,0:T(8,128)(2,1)S(1)} %get-tuple-element.114), channel_id=1, source_target_pairs={{0,504},{8,0},{16,8},{24,16},{32,24},{40,32},{48,40},{56,48},{64,5... | collective-permute-start | bytes 98312 | tf_op jit(solution)/shard_map/ppermute | solution.py:19
  254.8 9.2 %collective-permute-start.20 = (bf16[128,128]{1,0:T(8,128)(2,1)S(1)}, bf16[128,128]{1,0:T(8,128)(2,1)S(1)}, u32[]{:S(2)}, u32[]{:S(2)}) collective-permute-start(bf16[128,128]{1,0:T(8,128)(2,1)S(1)} %get-tuple-element.118), channel_id=1, source_target_pairs={{0,8},{8,16},{16,24},{24,32},{32,40},{40,48},{48,56},{56,64},{64,7... | collective-permute-start | bytes 98312 | tf_op jit(solution)/shard_map/ppermute | solution.py:19
  256.7 8.3 %collective-permute-start.21 = (bf16[128,128]{1,0:T(8,128)(2,1)S(1)}, bf16[128,128]{1,0:T(8,128)(2,1)S(1)}, u32[]{:S(2)}, u32[]{:S(2)}) collective-permute-start(bf16[128,128]{1,0:T(8,128)(2,1)S(1)} %get-tuple-element.119), channel_id=1, source_target_pairs={{0,504},{8,0},{16,8},{24,16},{32,24},{40,32},{48,40},{56,48},{64,5... | collective-permute-start | bytes 98312 | tf_op jit(solution)/shard_map/ppermute | solution.py:19
  277.4 9.2 %collective-permute-start.22 = (bf16[128,128]{1,0:T(8,128)(2,1)S(1)}, bf16[128,128]{1,0:T(8,128)(2,1)S(1)}, u32[]{:S(2)}, u32[]{:S(2)}) collective-permute-start(bf16[128,128]{1,0:T(8,128)(2,1)S(1)} %get-tuple-element.123), channel_id=1, source_target_pairs={{0,8},{8,16},{16,24},{24,32},{32,40},{40,48},{48,56},{56,64},{64,7... | collective-permute-start | bytes 98312 | tf_op jit(solution)/shard_map/ppermute | solution.py:19
  (12 other events, 125.9 us)

commit v2 on v1

--- a/solution.py
+++ b/solution.py
@@ -8,6 +8,7 @@
 from jax.sharding import PartitionSpec as P
 
 STEPS = 12
+LEVEL_STEPS = 4
 GROUPS = 8
 PAIR = 2
 BF = jnp.bfloat16
@@ -67,13 +68,89 @@
     base[...] = value + partial[128:256].astype(F32)
 
 
-def call(body, outs, *args):
+def placed_pairs(rows, pick_left, pick_right, tiles, first, slots, place, left, right, product):
+    left[...] = dot(pick_left[...], rows).astype(BF)
+    right[...] = dot(pick_right[...], rows).astype(BF)
+    upper_rows = lax.broadcasted_iota(jnp.int32, (8, 128), 0) < 4
+    blocks = tiles.shape[0] // GROUPS
+
+    def of_depth(depth, carry):
+        for octet in range(slots // 8):
+            at = pl.ds(pl.multiple_of((depth * (slots // 8) + octet) * 16, 16), 16)
+            lhs = jnp.concatenate([left[at], right[at]], axis=1)
+            kept = []
+            for quad in range(2):
+                tile = depth * blocks + first + octet * 8 + quad * 4
+                upper = jnp.concatenate([tiles[tile], tiles[tile + 2]], axis=1)
+                lower = jnp.concatenate([tiles[tile + 1], tiles[tile + 3]], axis=1)
+                out = dot(lhs, jnp.concatenate([upper, lower], axis=0))[8 * quad : 8 * quad + 8]
+                kept.append(jnp.where(upper_rows, out[:, :128], out[:, 128:]))
+            product[at] = jnp.concatenate(kept, axis=0)
+        return carry
+
+    lax.fori_loop(0, GROUPS, of_depth, 0)
+    high = product[...].astype(BF)
+    low = (product[...] - high.astype(F32)).astype(BF)
+    return dot(place[...], high) + dot(place[...], low)
+
+
+def tracer_step(
+    value,
+    wet,
+    v_left,
+    v_right,
+    v_place,
+    l_left,
+    l_right,
+    l_place,
+    tiles,
+    base,
+    to_left,
+    to_right,
+    left,
+    right,
+    product,
+):
+    lateral_slots, vertical_slots = l_place.shape[1] // (GROUPS * PAIR), v_place.shape[1] // (GROUPS * PAIR)
+    value = wet[...] * value
+    part = slice(0, v_place.shape[1])
+    value = value + placed_pairs(
+        value.astype(BF),
+        v_left,
+        v_right,
+        tiles,
+        lateral_slots,
+        vertical_slots,
+        v_place,
+        left.at[part],
+        right.at[part],
+        product.at[part],
+    )
+    value = wet[...] * value
+    partial = placed_pairs(
+        value.astype(BF), l_left, l_right, tiles, 0, lateral_slots, l_place, left, right, product
+    )
+    to_left[...] = partial[:128].astype(BF)
+    to_right[...] = partial[256:].astype(BF)
+    base[...] = value + partial[128:256]
+
+
+def tracer_first_kernel(base, *refs):
+    tracer_step(base[...], *refs)
+
+
+def tracer_kernel(base, from_left, from_right, *refs):
+    tracer_step(base[...] + from_left[...].astype(F32) + from_right[...].astype(F32), *refs)
+
+
+def call(body, outs, *args, scratch=()):
     specs = [pl.BlockSpec(memory_space=pltpu.VMEM) for _ in args]
     return pl.pallas_call(
         body,
         out_shape=[jax.ShapeDtypeStruct(shape, kind) for shape, kind in outs],
         in_specs=specs,
         out_specs=[pl.BlockSpec(memory_space=pltpu.VMEM) for _ in outs],
+        scratch_shapes=scratch,
         compiler_params=pltpu.CompilerParams(vmem_limit_bytes=24 * 1024 * 1024),
     )(*args)
 
@@ -109,6 +186,29 @@
     )
     wanted = jnp.where(jnp.repeat(in_use, 16), wanted, -1)
     return (jnp.arange(blocks * 128, dtype=jnp.int32)[:, None] == wanted[None, :]).astype(BF)
+
+
+def tracer_pickers(slot_rows):
+    depths, slots = slot_rows.shape
+    row = jnp.arange(depths * slots * PAIR, dtype=jnp.int32)
+    wanted = (row // (slots * PAIR) * 8 + jnp.repeat(slot_rows.reshape(-1), PAIR)) * PAIR + row % PAIR
+    hit = wanted[:, None] == jnp.arange(128, dtype=jnp.int32)[None, :]
+    even = (row // PAIR % 2 == 0)[:, None]
+    return (hit & even).astype(BF), (hit & ~even).astype(BF)
+
+
+def tracer_placer(blocks, count):
+    pair = jnp.arange(blocks.shape[0] * PAIR, dtype=jnp.int32) % PAIR
+    wanted = jnp.repeat(blocks, PAIR) * PAIR + pair
+    return (jnp.arange(count * PAIR, dtype=jnp.int32)[:, None] == wanted[None, :]).astype(BF)
+
+
+def gather_tiles(lateral_tiles, lateral_rows, lateral_blocks, vertical_tiles, vertical_rows, vertical_blocks):
+    lists = [lateral_rows, lateral_blocks, vertical_rows, vertical_blocks]
+    lists = jnp.stack([jnp.pad(entry, (0, 128 - entry.shape[0])) for entry in lists]).astype(BF)
+    lists = jnp.pad(lists, ((0, 128 - lists.shape[0]), (0, 0)))
+    own = jnp.concatenate([lateral_tiles, vertical_tiles, lists[None]], axis=0)
+    return lax.all_gather(own, "depth", axis=0, tiled=True)
 
 
 def local(
@@ -125,6 +225,18 @@
     vertical_targets,
 ):
     levels_here, tracers, cells = adjoint_seed.shape
+    gathered = gather_tiles(
+        lateral_tiles,
+        lateral_rows[:, 0],
+        jnp.where(
+            jnp.arange(lateral_tiles.shape[0], dtype=jnp.int32) < lateral_counts[0, 0],
+            lateral_sides[:, 0] * levels_here + lateral_targets[:, 0],
+            -1,
+        ),
+        vertical_tiles,
+        vertical_rows[:, 0],
+        vertical_peers[:, 0] * levels_here + vertical_targets[:, 0],
+    )
     row = jnp.arange(levels_here * tracers, dtype=jnp.int32)
     level_of_row = lax.axis_index("depth") * levels_here + row % 16 // PAIR
     wet = (level_of_row[:, None] < column_lengths[None, :]).astype(F32)
@@ -149,19 +261,48 @@
     shape = (levels_here * tracers, cells)
     state_and_partial = [(shape, F32), ((GROUPS * shape[0], cells), BF)]
     adjoint, partial = call(first_kernel, state_and_partial, split_rows(adjoint_seed), wet, *vertical)
-    for step in range(STEPS):
+    exchanged = [(shape, F32), (shape, BF), (shape, BF)]
+    for step in range(LEVEL_STEPS):
         returned = lax.all_to_all(partial, "depth", split_axis=0, concat_axis=0, tiled=True)
-        base, to_left, to_right = call(
-            lateral_kernel, [(shape, F32), (shape, BF), (shape, BF)], adjoint, returned, wet, *lateral
-        )
+        base, to_left, to_right = call(lateral_kernel, exchanged, adjoint, returned, wet, *lateral)
         from_left = passed_along(to_right, "region", 1)
         from_right = passed_along(to_left, "region", -1)
-        if step < STEPS - 1:
+        if step < LEVEL_STEPS - 1:
             adjoint, partial = call(
                 vertical_kernel, state_and_partial, base, from_left, from_right, wet, *vertical
             )
+
+    vertical_slots = vertical_tiles.shape[0]
+    per_depth = lateral_slots + vertical_slots + 1
+    lists = gathered.reshape(GROUPS, per_depth, 128, 128)[:, -1, :4].astype(jnp.int32)
+    level = jnp.arange(shape[0], dtype=jnp.int32) // PAIR
+    lateral_blocks = lists[:, 1, :lateral_slots]
+    lateral_level = jnp.arange(GROUPS, dtype=jnp.int32)[:, None] * levels_here + lateral_blocks % levels_here
+    lateral_blocks = jnp.where(
+        lateral_blocks < 0, -1, lateral_blocks // levels_here * (GROUPS * levels_here) + lateral_level
+    )
+    constants = (
+        (level[:, None] < column_lengths[None, :]).astype(F32),
+        *tracer_pickers(lists[:, 2, :vertical_slots]),
+        tracer_placer(lists[:, 3, :vertical_slots].reshape(-1), GROUPS * levels_here),
+        *tracer_pickers(lists[:, 0, :lateral_slots]),
+        tracer_placer(lateral_blocks.reshape(-1), 3 * GROUPS * levels_here),
+        gathered,
+    )
+    rows = GROUPS * lateral_slots * PAIR
+    scratch = (pltpu.VMEM((rows, 128), BF), pltpu.VMEM((rows, 128), BF), pltpu.VMEM((rows, 128), F32))
+    value = base + from_left.astype(F32) + from_right.astype(F32)
+    value = lax.all_to_all(value, "depth", split_axis=0, concat_axis=0, tiled=True)
+    for step in range(LEVEL_STEPS, STEPS):
+        if step == LEVEL_STEPS:
+            received, body = (value,), tracer_first_kernel
         else:
-            adjoint = wet * (base + from_left.astype(F32) + from_right.astype(F32))
+            received, body = (base, from_left, from_right), tracer_kernel
+        base, to_left, to_right = call(body, exchanged, *received, *constants, scratch=scratch)
+        from_left = passed_along(to_right, "region", 1)
+        from_right = passed_along(to_left, "region", -1)
+    value = base + from_left.astype(F32) + from_right.astype(F32)
+    adjoint = wet * lax.all_to_all(value, "depth", split_axis=0, concat_axis=0, tiled=True)
     return join_rows(adjoint, levels_here, tracers)
 
 

time: 290 us -> 307 us (1.059)
  blocking collectives: 119 us -> 28 us
  Pallas kernels: 20.9 us -> 49.1 us
  waiting for transfers between devices: 15.7 us -> 42.4 us
  starting transfers between devices: 122 us -> 144 us
  between operations: 1.29 us -> 14.7 us
  local copies, waits for them, and re-layouts: 4.41 us -> 15.9 us
  other arithmetic: 4.8 us -> 11.2 us
    all_to_all x11 -> x2, blocking collectives: 119 us -> 28 us  [local(): lax.all_to_all(partial, 'depth', split_axis=0, concat_axis=0, tiled=True)]
    pallas_call x24 -> x16, Pallas kernels: 20.9 us -> 49.1 us  [call(): pl.pallas_call(body, out_shape=[jax.ShapeDtypeStruct(shape, kind) for sha...]
    all_to_all x0 -> x2, starting transfers between devices: none -> 19.4 us  [local(): lax.all_to_all(value, 'depth', split_axis=0, concat_axis=0, tiled=True)]
    unnamed x22 -> x36, local copies, waits for them, and re-layouts: 1.81 us -> 12.6 us
    all_to_all x1 -> x2, waiting for transfers between devices: 3.73 us -> 14.2 us  [local(): lax.all_to_all(partial, 'depth', split_axis=0, concat_axis=0, tiled=True)]
    ppermute x24, waiting for transfers between devices: 11.9 us -> 21.7 us  [passed_along(): lax.ppermute(value, axis, [(i, (i + by) % devices) for i in range(devices)])]
    all_to_all x0 -> x2, waiting for transfers between devices: none -> 6.49 us  [local(): lax.all_to_all(value, 'depth', split_axis=0, concat_axis=0, tiled=True)]
    all_to_all x1 -> x2, starting transfers between devices: 10.9 us -> 15.9 us  [local(): lax.all_to_all(partial, 'depth', split_axis=0, concat_axis=0, tiled=True)]
  transfers between devices with their start and end apart: 25 -> 29, of which waited for: 13 -> 16; matrix products, arithmetic and copies ran while one was open for 1% -> 2% of each run, Pallas kernels for 0% -> 3%
where the time goes in v2:
time: 307 us; the launch traced here: 306 us
  starting transfers between devices  144 us (47%)
  Pallas kernels  49.1 us (16%)
  waiting for transfers between devices  42.4 us (14%)
  blocking collectives  28 us (9%)
  local copies, waits for them, and re-layouts  15.9 us (5%)
  between operations  14.7 us (5%)
  other arithmetic  11.2 us (4%)
    ppermute x24, starting transfers between devices, passed_along(): lax.ppermute(value, axis, [(i, (i + by) % devices) for i in range(devices)])  109 us
    pallas_call x16, Pallas kernels, call(): pl.pallas_call(body, out_shape=[jax.ShapeDtypeStruct(shape, kind) for sha...  49.1 us
    all_to_all x2, blocking collectives, local(): lax.all_to_all(partial, 'depth', split_axis=0, concat_axis=0, tiled=True)  28 us
    ppermute x24, waiting for transfers between devices, passed_along(): lax.ppermute(value, axis, [(i, (i + by) % devices) for i in range(devices)])  21.7 us
    all_to_all x2, starting transfers between devices, local(): lax.all_to_all(value, 'depth', split_axis=0, concat_axis=0, tiled=True)  19.4 us
    all_to_all x2, starting transfers between devices, local(): lax.all_to_all(partial, 'depth', split_axis=0, concat_axis=0, tiled=True)  15.9 us
    all_to_all x2, waiting for transfers between devices, local(): lax.all_to_all(partial, 'depth', split_axis=0, concat_axis=0, tiled=True)  14.2 us
    unnamed x36, local copies, waits for them, and re-layouts  12.6 us
  transfers between devices with their start and end apart: 29, of which 16 were waited for; matrix products, arithmetic and copies ran while one was open for 2% of the time, Pallas kernels for 3%

profile of v2, /device:TPU:1, one launch (start us, length us, event | category | flops | bytes accessed | tf_op | source)
XLA Modules:
  0.0 305.6 jit_solution(10599835350212073228)
XLA Ops:
  17.6 10.8 %all-to-all-start = ((bf16[8,128,128]{2,1,0:T(8,128)(2,1)}), bf16[8,128,128]{2,1,0:T(8,128)(2,1)}, u32[]{:S(2)}, u32[]{:S(2)}) async-start(bf16[8,128,128]{2,1,0:T(8,128)(2,1)} %bitcast.6), calls=%async_computation | async-start | bytes 524288 | tf_op jit(solution)/shard_map/all_to_all | solution.py:266
  40.7 8.6 %collective-permute-start.1 = (bf16[128,128]{1,0:T(8,128)(2,1)S(1)}, bf16[128,128]{1,0:T(8,128)(2,1)S(1)}, u32[]{:S(2)}, u32[]{:S(2)}) collective-permute-start(bf16[128,128]{1,0:T(8,128)(2,1)S(1)} %get-tuple-element.53), channel_id=1, source_target_pairs={{0,504},{8,0},{16,8},{24,16},{32,24},{40,32},{48,40},{56,48},{64,5... | collective-permute-start | bytes 98312 | tf_op jit(solution)/shard_map/ppermute | solution.py:20
  51.0 14.0 %all_to_all.67 = bf16[8,128,128]{2,1,0:T(8,128)(2,1)S(1)} all-to-all(bf16[8,128,128]{2,1,0:T(8,128)(2,1)S(1)} %bitcast.75), channel_id=1, replica_groups=mesh['region'=64,'depth'=8] {'depth'}, dimensions={0} | all-to-all | bytes 524288 | tf_op jit(solution)/shard_map/all_to_all | solution.py:266
  67.8 7.3 %collective-permute-start.3 = (bf16[128,128]{1,0:T(8,128)(2,1)S(1)}, bf16[128,128]{1,0:T(8,128)(2,1)S(1)}, u32[]{:S(2)}, u32[]{:S(2)}) collective-permute-start(bf16[128,128]{1,0:T(8,128)(2,1)S(1)} %get-tuple-element.58), channel_id=1, source_target_pairs={{0,504},{8,0},{16,8},{24,16},{32,24},{40,32},{48,40},{56,48},{64,5... | collective-permute-start | bytes 98312 | tf_op jit(solution)/shard_map/ppermute | solution.py:20
  76.8 13.9 %all_to_all.68 = bf16[8,128,128]{2,1,0:T(8,128)(2,1)S(1)} all-to-all(bf16[8,128,128]{2,1,0:T(8,128)(2,1)S(1)} %bitcast.76), channel_id=1, replica_groups=mesh['region'=64,'depth'=8] {'depth'}, dimensions={0} | all-to-all | bytes 524288 | tf_op jit(solution)/shard_map/all_to_all | solution.py:266
  93.6 7.3 %collective-permute-start.5 = (bf16[128,128]{1,0:T(8,128)(2,1)S(1)}, bf16[128,128]{1,0:T(8,128)(2,1)S(1)}, u32[]{:S(2)}, u32[]{:S(2)}) collective-permute-start(bf16[128,128]{1,0:T(8,128)(2,1)S(1)} %get-tuple-element.63), channel_id=1, source_target_pairs={{0,504},{8,0},{16,8},{24,16},{32,24},{40,32},{48,40},{56,48},{64,5... | collective-permute-start | bytes 98312 | tf_op jit(solution)/shard_map/ppermute | solution.py:20
  109.0 9.7 %all-to-all-done.3 = bf16[8,128,128]{2,1,0:T(8,128)(2,1)S(1)} async-done(((bf16[8,128,128]{2,1,0:T(8,128)(2,1)}), bf16[8,128,128]{2,1,0:T(8,128)(2,1)S(1)}, u32[]{:S(2)}, u32[]{:S(2)}) %all-to-all-start.3) | async-done | bytes 262176 | tf_op jit(solution)/shard_map/all_to_all | solution.py:266
  121.5 7.2 %collective-permute-start.7 = (bf16[128,128]{1,0:T(8,128)(2,1)S(1)}, bf16[128,128]{1,0:T(8,128)(2,1)S(1)}, u32[]{:S(2)}, u32[]{:S(2)}) collective-permute-start(bf16[128,128]{1,0:T(8,128)(2,1)S(1)} %get-tuple-element.68), channel_id=1, source_target_pairs={{0,504},{8,0},{16,8},{24,16},{32,24},{40,32},{48,40},{56,48},{64,5... | collective-permute-start | bytes 98312 | tf_op jit(solution)/shard_map/ppermute | solution.py:20
  130.8 5.9 %collective-permute-done.6 = bf16[128,128]{1,0:T(8,128)(2,1)S(1)} collective-permute-done((bf16[128,128]{1,0:T(8,128)(2,1)S(1)}, bf16[128,128]{1,0:T(8,128)(2,1)S(1)}, u32[]{:S(2)}, u32[]{:S(2)}) %collective-permute-start.6) | collective-permute-done | bytes 32800 | tf_op jit(solution)/shard_map/ppermute | solution.py:20
  137.3 5.6 %all-to-all-start.4 = ((f32[8,16,128]{2,1,0:T(8,128)}), f32[8,16,128]{2,1,0:T(8,128)S(1)}, u32[]{:S(2)}, u32[]{:S(2)}) async-start(f32[8,16,128]{2,1,0:T(8,128)} %bitcast.18), calls=%async_computation.4 | async-start | bytes 131072 | tf_op jit(solution)/shard_map/all_to_all | solution.py:295
  147.8 5.8 %copy-done = bf16[520,128,128]{2,1,0:T(8,128)(2,1)S(1)} copy-done((bf16[520,128,128]{2,1,0:T(8,128)(2,1)S(1)}, bf16[520,128,128]{2,1,0:T(8,128)(2,1)}, u32[]{:S(2)}) %copy-start) | copy-done | bytes 17039384
  160.7 6.7 %collective-permute-start.9 = (bf16[128,128]{1,0:T(8,128)(2,1)S(1)}, bf16[128,128]{1,0:T(8,128)(2,1)S(1)}, u32[]{:S(2)}, u32[]{:S(2)}) collective-permute-start(bf16[128,128]{1,0:T(8,128)(2,1)S(1)} %get-tuple-element.71), channel_id=1, source_target_pairs={{0,504},{8,0},{16,8},{24,16},{32,24},{40,32},{48,40},{56,48},{64,5... | collective-permute-start | bytes 98312 | tf_op jit(solution)/shard_map/ppermute | solution.py:20
  175.5 7.1 %collective-permute-start.11 = (bf16[128,128]{1,0:T(8,128)(2,1)S(1)}, bf16[128,128]{1,0:T(8,128)(2,1)S(1)}, u32[]{:S(2)}, u32[]{:S(2)}) collective-permute-start(bf16[128,128]{1,0:T(8,128)(2,1)S(1)} %get-tuple-element.74), channel_id=1, source_target_pairs={{0,504},{8,0},{16,8},{24,16},{32,24},{40,32},{48,40},{56,48},{64,5... | collective-permute-start | bytes 98312 | tf_op jit(solution)/shard_map/ppermute | solution.py:20
  190.5 7.0 %collective-permute-start.13 = (bf16[128,128]{1,0:T(8,128)(2,1)S(1)}, bf16[128,128]{1,0:T(8,128)(2,1)S(1)}, u32[]{:S(2)}, u32[]{:S(2)}) collective-permute-start(bf16[128,128]{1,0:T(8,128)(2,1)S(1)} %get-tuple-element.77), channel_id=1, source_target_pairs={{0,504},{8,0},{16,8},{24,16},{32,24},{40,32},{48,40},{56,48},{64,5... | collective-permute-start | bytes 98312 | tf_op jit(solution)/shard_map/ppermute | solution.py:20
  205.5 7.0 %collective-permute-start.15 = (bf16[128,128]{1,0:T(8,128)(2,1)S(1)}, bf16[128,128]{1,0:T(8,128)(2,1)S(1)}, u32[]{:S(2)}, u32[]{:S(2)}) collective-permute-start(bf16[128,128]{1,0:T(8,128)(2,1)S(1)} %get-tuple-element.80), channel_id=1, source_target_pairs={{0,504},{8,0},{16,8},{24,16},{32,24},{40,32},{48,40},{56,48},{64,5... | collective-permute-start | bytes 98312 | tf_op jit(solution)/shard_map/ppermute | solution.py:20
  213.5 5.1 %shard_map.121 = (f32[128,128]{1,0:T(8,128)S(1)}, bf16[128,128]{1,0:T(8,128)(2,1)S(1)}, bf16[128,128]{1,0:T(8,128)(2,1)S(1)}) custom-call(f32[128,128]{1,0:T(8,128)S(1)} %get-tuple-element.78.base, bf16[128,128]{1,0:T(8,128)(2,1)S(1)} %collective-permute-done.14.from_left, bf16[128,128]{1,0:T(8,128)(2,1)S(1)} %collective-permute-done.15.from_right, ...), custom_call_target="tpu_custom_call" | custom-call | tf_op jit(solution)/shard_map/pallas_call | solution.py:148
  220.6 7.0 %collective-permute-start.17 = (bf16[128,128]{1,0:T(8,128)(2,1)S(1)}, bf16[128,128]{1,0:T(8,128)(2,1)S(1)}, u32[]{:S(2)}, u32[]{:S(2)}) collective-permute-start(bf16[128,128]{1,0:T(8,128)(2,1)S(1)} %get-tuple-element.83), channel_id=1, source_target_pairs={{0,504},{8,0},{16,8},{24,16},{32,24},{40,32},{48,40},{56,48},{64,5... | collective-permute-start | bytes 98312 | tf_op jit(solution)/shard_map/ppermute | solution.py:20
  228.5 5.1 %shard_map.122 = (f32[128,128]{1,0:T(8,128)S(1)}, bf16[128,128]{1,0:T(8,128)(2,1)S(1)}, bf16[128,128]{1,0:T(8,128)(2,1)S(1)}) custom-call(f32[128,128]{1,0:T(8,128)S(1)} %get-tuple-element.81.base, bf16[128,128]{1,0:T(8,128)(2,1)S(1)} %collective-permute-done.16.from_left, bf16[128,128]{1,0:T(8,128)(2,1)S(1)} %collective-permute-done.17.from_right, ...), custom_call_target="tpu_custom_call" | custom-call | tf_op jit(solution)/shard_map/pallas_call | solution.py:148
  235.6 7.0 %collective-permute-start.19 = (bf16[128,128]{1,0:T(8,128)(2,1)S(1)}, bf16[128,128]{1,0:T(8,128)(2,1)S(1)}, u32[]{:S(2)}, u32[]{:S(2)}) collective-permute-start(bf16[128,128]{1,0:T(8,128)(2,1)S(1)} %get-tuple-element.86), channel_id=1, source_target_pairs={{0,504},{8,0},{16,8},{24,16},{32,24},{40,32},{48,40},{56,48},{64,5... | collective-permute-start | bytes 98312 | tf_op jit(solution)/shard_map/ppermute | solution.py:20
  243.5 5.1 %shard_map.123 = (f32[128,128]{1,0:T(8,128)S(1)}, bf16[128,128]{1,0:T(8,128)(2,1)S(1)}, bf16[128,128]{1,0:T(8,128)(2,1)S(1)}) custom-call(f32[128,128]{1,0:T(8,128)S(1)} %get-tuple-element.84.base, bf16[128,128]{1,0:T(8,128)(2,1)S(1)} %collective-permute-done.18.from_left, bf16[128,128]{1,0:T(8,128)(2,1)S(1)} %collective-permute-done.19.from_right, ...), custom_call_target="tpu_custom_call" | custom-call | tf_op jit(solution)/shard_map/pallas_call | solution.py:148
  250.6 7.0 %collective-permute-start.21 = (bf16[128,128]{1,0:T(8,128)(2,1)S(1)}, bf16[128,128]{1,0:T(8,128)(2,1)S(1)}, u32[]{:S(2)}, u32[]{:S(2)}) collective-permute-start(bf16[128,128]{1,0:T(8,128)(2,1)S(1)} %get-tuple-element.89), channel_id=1, source_target_pairs={{0,504},{8,0},{16,8},{24,16},{32,24},{40,32},{48,40},{56,48},{64,5... | collective-permute-start | bytes 98312 | tf_op jit(solution)/shard_map/ppermute | solution.py:20
  263.7 7.0 %collective-permute-start.23 = (bf16[128,128]{1,0:T(8,128)(2,1)S(1)}, bf16[128,128]{1,0:T(8,128)(2,1)S(1)}, u32[]{:S(2)}, u32[]{:S(2)}) collective-permute-start(bf16[128,128]{1,0:T(8,128)(2,1)S(1)} %get-tuple-element.92), channel_id=1, source_target_pairs={{0,504},{8,0},{16,8},{24,16},{32,24},{40,32},{48,40},{56,48},{64,5... | collective-permute-start | bytes 98312 | tf_op jit(solution)/shard_map/ppermute | solution.py:20
  272.6 6.0 %collective-permute-done.22 = bf16[128,128]{1,0:T(8,128)(2,1)S(1)} collective-permute-done((bf16[128,128]{1,0:T(8,128)(2,1)S(1)}, bf16[128,128]{1,0:T(8,128)(2,1)S(1)}, u32[]{:S(2)}, u32[]{:S(2)}) %collective-permute-start.22) | collective-permute-done | bytes 32800 | tf_op jit(solution)/shard_map/ppermute | solution.py:20
  279.3 13.8 %all-to-all-start.5 = ((f32[8,16,128]{2,1,0:T(8,128)}), f32[8,16,128]{2,1,0:T(8,128)S(1)}, u32[]{:S(2)}, u32[]{:S(2)}) async-start(f32[8,16,128]{2,1,0:T(8,128)} %bitcast.32), calls=%async_computation.5 | async-start | bytes 131072 | tf_op jit(solution)/shard_map/all_to_all | solution.py:305
  (161 shorter events, 103.9 us)
Async XLA Ops:
  6.5 136.4 %all-gather.2.cloned.1.call-start = ((), (), s32[]{:S(2)}) async-start(), calls=%async_computation.6 | async-start | bytes 19169280 | tf_op jit(solution)/shard_map/all_gather | solution.py:211
  17.6 17.4 %all-to-all-start = ((bf16[8,128,128]{2,1,0:T(8,128)(2,1)}), bf16[8,128,128]{2,1,0:T(8,128)(2,1)}, u32[]{:S(2)}, u32[]{:S(2)}) async-start(bf16[8,128,128]{2,1,0:T(8,128)(2,1)} %bitcast.6), calls=%async_computation | async-start | bytes 524288 | tf_op jit(solution)/shard_map/all_to_all | solution.py:266
  38.7 10.5 %collective-permute-start = (bf16[128,128]{1,0:T(8,128)(2,1)S(1)}, bf16[128,128]{1,0:T(8,128)(2,1)S(1)}, u32[]{:S(2)}, u32[]{:S(2)}) collective-permute-start(bf16[128,128]{1,0:T(8,128)(2,1)S(1)} %get-tuple-element.52), channel_id=1, source_target_pairs={{0,8},{8,16},{16,24},{24,32},{32,40},{40,48},{48,56},{56,64},{64,7... | collective-permute-start | bytes 98312 | tf_op jit(solution)/shard_map/ppermute | solution.py:20
  40.7 9.6 %collective-permute-start.1 = (bf16[128,128]{1,0:T(8,128)(2,1)S(1)}, bf16[128,128]{1,0:T(8,128)(2,1)S(1)}, u32[]{:S(2)}, u32[]{:S(2)}) collective-permute-start(bf16[128,128]{1,0:T(8,128)(2,1)S(1)} %get-tuple-element.53), channel_id=1, source_target_pairs={{0,504},{8,0},{16,8},{24,16},{32,24},{40,32},{48,40},{56,48},{64,5... | collective-permute-start | bytes 98312 | tf_op jit(solution)/shard_map/ppermute | solution.py:20
  65.9 9.2 %collective-permute-start.2 = (bf16[128,128]{1,0:T(8,128)(2,1)S(1)}, bf16[128,128]{1,0:T(8,128)(2,1)S(1)}, u32[]{:S(2)}, u32[]{:S(2)}) collective-permute-start(bf16[128,128]{1,0:T(8,128)(2,1)S(1)} %get-tuple-element.57), channel_id=1, source_target_pairs={{0,8},{8,16},{16,24},{24,32},{32,40},{40,48},{48,56},{56,64},{64,7... | collective-permute-start | bytes 98312 | tf_op jit(solution)/shard_map/ppermute | solution.py:20
  67.8 8.3 %collective-permute-start.3 = (bf16[128,128]{1,0:T(8,128)(2,1)S(1)}, bf16[128,128]{1,0:T(8,128)(2,1)S(1)}, u32[]{:S(2)}, u32[]{:S(2)}) collective-permute-start(bf16[128,128]{1,0:T(8,128)(2,1)S(1)} %get-tuple-element.58), channel_id=1, source_target_pairs={{0,504},{8,0},{16,8},{24,16},{32,24},{40,32},{48,40},{56,48},{64,5... | collective-permute-start | bytes 98312 | tf_op jit(solution)/shard_map/ppermute | solution.py:20
  91.7 9.2 %collective-permute-start.4 = (bf16[128,128]{1,0:T(8,128)(2,1)S(1)}, bf16[128,128]{1,0:T(8,128)(2,1)S(1)}, u32[]{:S(2)}, u32[]{:S(2)}) collective-permute-start(bf16[128,128]{1,0:T(8,128)(2,1)S(1)} %get-tuple-element.62), channel_id=1, source_target_pairs={{0,8},{8,16},{16,24},{24,32},{32,40},{40,48},{48,56},{56,64},{64,7... | collective-permute-start | bytes 98312 | tf_op jit(solution)/shard_map/ppermute | solution.py:20
  93.6 8.3 %collective-permute-start.5 = (bf16[128,128]{1,0:T(8,128)(2,1)S(1)}, bf16[128,128]{1,0:T(8,128)(2,1)S(1)}, u32[]{:S(2)}, u32[]{:S(2)}) collective-permute-start(bf16[128,128]{1,0:T(8,128)(2,1)S(1)} %get-tuple-element.63), channel_id=1, source_target_pairs={{0,504},{8,0},{16,8},{24,16},{32,24},{40,32},{48,40},{56,48},{64,5... | collective-permute-start | bytes 98312 | tf_op jit(solution)/shard_map/ppermute | solution.py:20
  103.9 14.9 %all-to-all-start.3 = ((bf16[8,128,128]{2,1,0:T(8,128)(2,1)}), bf16[8,128,128]{2,1,0:T(8,128)(2,1)S(1)}, u32[]{:S(2)}, u32[]{:S(2)}) async-start(bf16[8,128,128]{2,1,0:T(8,128)(2,1)} %bitcast.74), calls=%async_computation.3 | async-start | bytes 524288 | tf_op jit(solution)/shard_map/all_to_all | solution.py:266
  121.5 9.3 %collective-permute-start.7 = (bf16[128,128]{1,0:T(8,128)(2,1)S(1)}, bf16[128,128]{1,0:T(8,128)(2,1)S(1)}, u32[]{:S(2)}, u32[]{:S(2)}) collective-permute-start(bf16[128,128]{1,0:T(8,128)(2,1)S(1)} %get-tuple-element.68), channel_id=1, source_target_pairs={{0,504},{8,0},{16,8},{24,16},{32,24},{40,32},{48,40},{56,48},{64,5... | collective-permute-start | bytes 98312 | tf_op jit(solution)/shard_map/ppermute | solution.py:20
  128.7 8.0 %collective-permute-start.6 = (bf16[128,128]{1,0:T(8,128)(2,1)S(1)}, bf16[128,128]{1,0:T(8,128)(2,1)S(1)}, u32[]{:S(2)}, u32[]{:S(2)}) collective-permute-start(bf16[128,128]{1,0:T(8,128)(2,1)S(1)} %get-tuple-element.67), channel_id=1, source_target_pairs={{0,8},{8,16},{16,24},{24,32},{32,40},{40,48},{48,56},{56,64},{64,7... | collective-permute-start | bytes 98312 | tf_op jit(solution)/shard_map/ppermute | solution.py:20
  137.3 10.5 %all-to-all-start.4 = ((f32[8,16,128]{2,1,0:T(8,128)}), f32[8,16,128]{2,1,0:T(8,128)S(1)}, u32[]{:S(2)}, u32[]{:S(2)}) async-start(f32[8,16,128]{2,1,0:T(8,128)} %bitcast.18), calls=%async_computation.4 | async-start | bytes 131072 | tf_op jit(solution)/shard_map/all_to_all | solution.py:295
  158.8 8.6 %collective-permute-start.8 = (bf16[128,128]{1,0:T(8,128)(2,1)S(1)}, bf16[128,128]{1,0:T(8,128)(2,1)S(1)}, u32[]{:S(2)}, u32[]{:S(2)}) collective-permute-start(bf16[128,128]{1,0:T(8,128)(2,1)S(1)} %get-tuple-element.70), channel_id=1, source_target_pairs={{0,8},{8,16},{16,24},{24,32},{32,40},{40,48},{48,56},{56,64},{64,7... | collective-permute-start | bytes 98312 | tf_op jit(solution)/shard_map/ppermute | solution.py:20
  173.5 9.1 %collective-permute-start.10 = (bf16[128,128]{1,0:T(8,128)(2,1)S(1)}, bf16[128,128]{1,0:T(8,128)(2,1)S(1)}, u32[]{:S(2)}, u32[]{:S(2)}) collective-permute-start(bf16[128,128]{1,0:T(8,128)(2,1)S(1)} %get-tuple-element.73), channel_id=1, source_target_pairs={{0,8},{8,16},{16,24},{24,32},{32,40},{40,48},{48,56},{56,64},{64,7... | collective-permute-start | bytes 98312 | tf_op jit(solution)/shard_map/ppermute | solution.py:20
  175.5 8.0 %collective-permute-start.11 = (bf16[128,128]{1,0:T(8,128)(2,1)S(1)}, bf16[128,128]{1,0:T(8,128)(2,1)S(1)}, u32[]{:S(2)}, u32[]{:S(2)}) collective-permute-start(bf16[128,128]{1,0:T(8,128)(2,1)S(1)} %get-tuple-element.74), channel_id=1, source_target_pairs={{0,504},{8,0},{16,8},{24,16},{32,24},{40,32},{48,40},{56,48},{64,5... | collective-permute-start | bytes 98312 | tf_op jit(solution)/shard_map/ppermute | solution.py:20
  188.6 8.9 %collective-permute-start.12 = (bf16[128,128]{1,0:T(8,128)(2,1)S(1)}, bf16[128,128]{1,0:T(8,128)(2,1)S(1)}, u32[]{:S(2)}, u32[]{:S(2)}) collective-permute-start(bf16[128,128]{1,0:T(8,128)(2,1)S(1)} %get-tuple-element.76), channel_id=1, source_target_pairs={{0,8},{8,16},{16,24},{24,32},{32,40},{40,48},{48,56},{56,64},{64,7... | collective-permute-start | bytes 98312 | tf_op jit(solution)/shard_map/ppermute | solution.py:20
  203.6 8.9 %collective-permute-start.14 = (bf16[128,128]{1,0:T(8,128)(2,1)S(1)}, bf16[128,128]{1,0:T(8,128)(2,1)S(1)}, u32[]{:S(2)}, u32[]{:S(2)}) collective-permute-start(bf16[128,128]{1,0:T(8,128)(2,1)S(1)} %get-tuple-element.79), channel_id=1, source_target_pairs={{0,8},{8,16},{16,24},{24,32},{32,40},{40,48},{48,56},{56,64},{64,7... | collective-permute-start | bytes 98312 | tf_op jit(solution)/shard_map/ppermute | solution.py:20
  205.5 8.0 %collective-permute-start.15 = (bf16[128,128]{1,0:T(8,128)(2,1)S(1)}, bf16[128,128]{1,0:T(8,128)(2,1)S(1)}, u32[]{:S(2)}, u32[]{:S(2)}) collective-permute-start(bf16[128,128]{1,0:T(8,128)(2,1)S(1)} %get-tuple-element.80), channel_id=1, source_target_pairs={{0,504},{8,0},{16,8},{24,16},{32,24},{40,32},{48,40},{56,48},{64,5... | collective-permute-start | bytes 98312 | tf_op jit(solution)/shard_map/ppermute | solution.py:20
  218.6 8.9 %collective-permute-start.16 = (bf16[128,128]{1,0:T(8,128)(2,1)S(1)}, bf16[128,128]{1,0:T(8,128)(2,1)S(1)}, u32[]{:S(2)}, u32[]{:S(2)}) collective-permute-start(bf16[128,128]{1,0:T(8,128)(2,1)S(1)} %get-tuple-element.82), channel_id=1, source_target_pairs={{0,8},{8,16},{16,24},{24,32},{32,40},{40,48},{48,56},{56,64},{64,7... | collective-permute-start | bytes 98312 | tf_op jit(solution)/shard_map/ppermute | solution.py:20
  233.7 8.9 %collective-permute-start.18 = (bf16[128,128]{1,0:T(8,128)(2,1)S(1)}, bf16[128,128]{1,0:T(8,128)(2,1)S(1)}, u32[]{:S(2)}, u32[]{:S(2)}) collective-permute-start(bf16[128,128]{1,0:T(8,128)(2,1)S(1)} %get-tuple-element.85), channel_id=1, source_target_pairs={{0,8},{8,16},{16,24},{24,32},{32,40},{40,48},{48,56},{56,64},{64,7... | collective-permute-start | bytes 98312 | tf_op jit(solution)/shard_map/ppermute | solution.py:20
  248.7 8.9 %collective-permute-start.20 = (bf16[128,128]{1,0:T(8,128)(2,1)S(1)}, bf16[128,128]{1,0:T(8,128)(2,1)S(1)}, u32[]{:S(2)}, u32[]{:S(2)}) collective-permute-start(bf16[128,128]{1,0:T(8,128)(2,1)S(1)} %get-tuple-element.88), channel_id=1, source_target_pairs={{0,8},{8,16},{16,24},{24,32},{32,40},{40,48},{48,56},{56,64},{64,7... | collective-permute-start | bytes 98312 | tf_op jit(solution)/shard_map/ppermute | solution.py:20
  263.7 8.9 %collective-permute-start.23 = (bf16[128,128]{1,0:T(8,128)(2,1)S(1)}, bf16[128,128]{1,0:T(8,128)(2,1)S(1)}, u32[]{:S(2)}, u32[]{:S(2)}) collective-permute-start(bf16[128,128]{1,0:T(8,128)(2,1)S(1)} %get-tuple-element.92), channel_id=1, source_target_pairs={{0,504},{8,0},{16,8},{24,16},{32,24},{40,32},{48,40},{56,48},{64,5... | collective-permute-start | bytes 98312 | tf_op jit(solution)/shard_map/ppermute | solution.py:20
  270.7 8.0 %collective-permute-start.22 = (bf16[128,128]{1,0:T(8,128)(2,1)S(1)}, bf16[128,128]{1,0:T(8,128)(2,1)S(1)}, u32[]{:S(2)}, u32[]{:S(2)}) collective-permute-start(bf16[128,128]{1,0:T(8,128)(2,1)S(1)} %get-tuple-element.91), channel_id=1, source_target_pairs={{0,8},{8,16},{16,24},{24,32},{32,40},{40,48},{48,56},{56,64},{64,7... | collective-permute-start | bytes 98312 | tf_op jit(solution)/shard_map/ppermute | solution.py:20
  279.3 18.7 %all-to-all-start.5 = ((f32[8,16,128]{2,1,0:T(8,128)}), f32[8,16,128]{2,1,0:T(8,128)S(1)}, u32[]{:S(2)}, u32[]{:S(2)}) async-start(f32[8,16,128]{2,1,0:T(8,128)} %bitcast.32), calls=%async_computation.5 | async-start | bytes 131072 | tf_op jit(solution)/shard_map/all_to_all | solution.py:305
  (23 other events, 137.8 us)
Sparse Core Ops, SparseCore 0:
  13.4 107.7 all-gather.1

commit v3 on v0

v3 whole, which is shorter than its diff:
```python
import jax
import jax.numpy as jnp
from jax import lax
from jax.experimental import pallas as pl
from jax.experimental.pallas import tpu as pltpu
from jax.sharding import PartitionSpec as P

STEPS = 12
LEVEL_STEPS = 4
GROUPS = 8
PAIR = 2
LEVELS = 8
TRACERS = GROUPS * PAIR
CELLS = 128
STATE = 128
LISTS = 16
BF = jnp.bfloat16
F32 = jnp.float32
I32 = jnp.int32


def dot(a, b):
    return jnp.dot(a, b, preferred_element_type=F32)


def dot_last(a, b):
    return lax.dot_general(a, b, (((1,), (1,)), ((), ())), preferred_element_type=F32)


def iota(shape, dim):
    return lax.broadcasted_iota(I32, shape, dim)


def spread(codes, slots, rows):
    owner = (iota((slots * rows, CELLS), 0) // rows == iota((slots * rows, CELLS), 1)).astype(BF)
    return dot_last(owner, codes).astype(I32), dot_last(codes, owner).astype(I32)


def write_picks(wanted, rows, left, right, part=slice(None)):
    count = wanted.shape[0]
    hit = jnp.where(wanted == iota((count, STATE), 1), 1.0, 0.0)
    even = iota((count, STATE), 0) // rows % 2 == 0
    left[part] = jnp.where(even, hit, 0.0).astype(BF)
    right[part] = jnp.where(even, 0.0, hit).astype(BF)


def write_place(wanted, place, part=slice(None)):
    shape = (place.shape[0], wanted.shape[1])
    place[:, part] = jnp.where(wanted == iota(shape, 0), 1.0, 0.0).astype(BF)


def level_matrices(codes, row_of, block_of, slots, left, right, place):
    columns, rows = spread(codes, slots, TRACERS)
    tracer = iota((slots * TRACERS, 1), 0) % TRACERS
    wanted = tracer // PAIR * TRACERS + columns[:, row_of : row_of + 1] * PAIR + tracer % PAIR
    write_picks(wanted, TRACERS, left, right)
    tracer = iota((1, slots * TRACERS), 1) % TRACERS
    block = rows[block_of : block_of + 1]
    wanted = block // LEVELS * STATE + tracer // PAIR * TRACERS + block % LEVELS * PAIR + tracer % PAIR
    write_place(jnp.where(block < 0, -1, wanted), place)


def level_products(rows, left, right, place, tiles):
    rows = rows.astype(BF)
    x_left = dot(left[...], rows).astype(BF)
    x_right = dot(right[...], rows).astype(BF)
    parts = []
    for at in range(0, tiles.shape[0], 4):
        part = slice(at * TRACERS, (at + 4) * TRACERS)
        lhs = jnp.concatenate([x_left[part], x_right[part]], axis=1)
        upper = jnp.concatenate([tiles[at], tiles[at + 2]], axis=1)
        lower = jnp.concatenate([tiles[at + 1], tiles[at + 3]], axis=1)
        out = dot(lhs, jnp.concatenate([upper, lower], axis=0))
        parts += [out[: 2 * TRACERS, :CELLS], out[2 * TRACERS :, CELLS:]]
    return placed(place, jnp.concatenate(parts, axis=0))


def placed(place, product):
    high = product.astype(BF)
    low = (product - high.astype(F32)).astype(BF)
    return dot(place[...], high) + dot(place[...], low)


def open_kernel(
    seed, lengths, l_rows, l_sides, l_targets, l_count, v_rows, v_peers, v_targets, tiles,
    adjoint, partial, wet, left, right, place, codes,
):
    l_slots, v_slots = l_rows.shape[1], v_rows.shape[1]
    codes[...] = jnp.zeros(codes.shape, F32)
    odd = lax.axis_index("region") % 2
    side = jnp.where(odd == 1, 2 - l_sides[...], l_sides[...])
    used = iota((1, l_slots), 1) < l_count[...]
    codes[0:1, 0:l_slots] = l_rows[...].astype(F32)
    codes[1:2, 0:l_slots] = jnp.where(used, side * LEVELS + l_targets[...], -1).astype(F32)
    codes[2:3, 0:v_slots] = v_rows[...].astype(F32)
    codes[3:4, 0:v_slots] = (v_peers[...] * LEVELS + v_targets[...]).astype(F32)
    level = lax.axis_index("depth") * LEVELS + iota((STATE, CELLS), 0) % TRACERS // PAIR
    wet[...] = jnp.where(level < lengths[...], 1.0, 0.0)
    level_matrices(codes[...].astype(BF)[:8], 2, 3, v_slots, left, right, place)
    for group in range(GROUPS):
        for at in range(LEVELS):
            row = group * TRACERS + at * PAIR
            adjoint[row : row + PAIR] = seed[at, group * PAIR : group * PAIR + PAIR]
    value = wet[...] * adjoint[...]
    adjoint[...] = value
    sums = level_products(value, left, right, place, tiles).astype(BF)
    for peer in range(GROUPS):
        at = peer * (STATE + LISTS)
        partial[at : at + STATE] = sums[peer * STATE : (peer + 1) * STATE]
        partial[at + STATE : at + STATE + LISTS] = codes[...].astype(BF)


def lateral_lists_kernel(codes, left, right, place):
    level_matrices(codes[...].astype(BF)[:8], 0, 1, left.shape[0] // TRACERS, left, right, place)


def vertical_kernel(base, first, second, wet, left, right, place, tiles, adjoint, partial):
    value = wet[...] * (base[...] + first[...].astype(F32) + second[...].astype(F32))
    adjoint[...] = value
    partial[...] = level_products(value, left, right, place, tiles).astype(BF)


def lateral_kernel(adjoint, returned, wet, left, right, place, tiles, base, to_first, to_second):
    value = adjoint[...]
    stride = returned.shape[0] // GROUPS
    for peer in range(GROUPS):
        value = value + returned[stride * peer : stride * peer + STATE].astype(F32)
    value = wet[...] * value
    partial = level_products(value, left, right, place, tiles).astype(BF)
    to_first[...] = partial[:STATE]
    to_second[...] = partial[2 * STATE :]
    base[...] = value + partial[STATE : 2 * STATE].astype(F32)


def tracer_lists_kernel(returned, lengths, wet, v_left, v_right, v_place, l_left, l_right, l_place):
    level = iota((STATE, CELLS), 0) // PAIR
    wet[...] = jnp.where(level < lengths[...], 1.0, 0.0)
    l_rows, v_rows = l_left.shape[0] // GROUPS, v_left.shape[0] // GROUPS
    stride = STATE + LISTS
    for depth in range(GROUPS):
        codes = returned[depth * stride + STATE : (depth + 1) * stride][:8]
        for rows, row_of, left, right in ((l_rows, 0, l_left, l_right), (v_rows, 2, v_left, v_right)):
            columns, lines = spread(codes, rows // PAIR, PAIR)
            part = slice(depth * rows, (depth + 1) * rows)
            wanted = (depth * LEVELS + columns[:, row_of : row_of + 1]) * PAIR + iota((rows, 1), 0) % PAIR
            write_picks(wanted, PAIR, left, right, part)
            block = lines[row_of + 1 : row_of + 2]
            pair = iota((1, rows), 1) % PAIR
            if row_of == 0:
                wanted = block // LEVELS * STATE + (depth * LEVELS + block % LEVELS) * PAIR + pair
                wanted = jnp.where(block < 0, -1, wanted)
                write_place(wanted, l_place.at[depth])
            else:
                write_place(block * PAIR + pair, v_place.at[depth])


def tracer_products(rows, left, right, place, tiles, first, slots):
    rows = rows.astype(BF)
    x_left = dot(left[...], rows).astype(BF)
    x_right = dot(right[...], rows).astype(BF)
    upper_rows = iota((8, CELLS), 0) < 2 * PAIR
    blocks = tiles.shape[0] // GROUPS
    total = None
    for depth in range(GROUPS):
        parts = []
        for octet in range(slots // 8):
            at = (depth * slots + octet * 8) * PAIR
            part = slice(at, at + 8 * PAIR)
            lhs = jnp.concatenate([x_left[part], x_right[part]], axis=1)
            for quad in range(2):
                tile = depth * blocks + first + octet * 8 + quad * 4
                upper = jnp.concatenate([tiles[tile], tiles[tile + 2]], axis=1)
                lower = jnp.concatenate([tiles[tile + 1], tiles[tile + 3]], axis=1)
                out = dot(lhs, jnp.concatenate([upper, lower], axis=0))[8 * quad : 8 * quad + 8]
                parts.append(jnp.where(upper_rows, out[:, :CELLS], out[:, CELLS:]))
        sums = placed(place.at[depth], jnp.concatenate(parts, axis=0))
        total = sums if total is None else total + sums
    return total


def tracer_step(value, wet, v_left, v_right, v_place, l_left, l_right, l_place, tiles, base, to_first, to_second):
    l_slots, v_slots = l_left.shape[0] // (GROUPS * PAIR), v_left.shape[0] // (GROUPS * PAIR)
    value = wet[...] * value
    value = wet[...] * (value + tracer_products(value, v_left, v_right, v_place, tiles, l_slots, v_slots))
    partial = tracer_products(value, l_left, l_right, l_place, tiles, 0, l_slots)
    to_first[...] = partial[:STATE].astype(BF)
    to_second[...] = partial[2 * STATE :].astype(BF)
    base[...] = value + partial[STATE : 2 * STATE]


def tracer_first_kernel(value, *refs):
    tracer_step(value[...], *refs)


def tracer_kernel(base, first, second, *refs):
    tracer_step(base[...] + first[...].astype(F32) + second[...].astype(F32), *refs)


def sum_kernel(base, first, second, total):
    total[...] = base[...] + first[...].astype(F32) + second[...].astype(F32)


def close_kernel(value, wet, out):
    rows = wet[...] * value[...]
    for group in range(GROUPS):
        for at in range(LEVELS):
            row = group * TRACERS + at * PAIR
            out[at, group * PAIR : group * PAIR + PAIR] = rows[row : row + PAIR]


def call(body, outs, *args, scratch=()):
    return pl.pallas_call(
        body,
        out_shape=[jax.ShapeDtypeStruct(shape, kind) for shape, kind in outs],
        in_specs=[pl.BlockSpec(memory_space=pltpu.VMEM) for _ in args],
        out_specs=[pl.BlockSpec(memory_space=pltpu.VMEM) for _ in outs],
        scratch_shapes=scratch,
        compiler_params=pltpu.CompilerParams(vmem_limit_bytes=24 * 1024 * 1024),
    )(*args)


def swapped(to_first, to_second):
    regions = lax.axis_size("region")
    first = [(i, (i + 1) % regions if i % 2 else (i - 1) % regions) for i in range(regions)]
    second = [(i, i ^ 1) for i in range(regions)]
    from_first = lax.ppermute(to_first, "region", first)
    from_second = lax.ppermute(to_second, "region", second)
    return from_first, from_second


def to_depth(value):
    return lax.all_to_all(value, "depth", split_axis=0, concat_axis=0, tiled=True)


def local(
    adjoint_seed,
    column_lengths,
    lateral_tiles,
    lateral_rows,
    lateral_sides,
    lateral_targets,
    lateral_counts,
    vertical_tiles,
    vertical_rows,
    vertical_peers,
    vertical_targets,
):
    gathered = lax.all_gather(
        jnp.concatenate([lateral_tiles, vertical_tiles], axis=0), "depth", axis=0, tiled=True
    )
    l_slots, v_slots = lateral_tiles.shape[0], vertical_tiles.shape[0]
    lengths = column_lengths.reshape(1, CELLS)
    state = ((STATE, CELLS), F32)
    sent = ((STATE, CELLS), BF)

    def matrices(slots, blocks):
        return [((slots * TRACERS, STATE), BF)] * 2 + [((blocks * STATE, slots * TRACERS), BF)]

    adjoint, partial, wet, *vertical, codes = call(
        open_kernel,
        [state, ((GROUPS * (STATE + LISTS), CELLS), BF), state]
        + matrices(v_slots, GROUPS)
        + [((LISTS, CELLS), F32)],
        adjoint_seed,
        lengths,
        lateral_rows.reshape(1, l_slots),
        lateral_sides.reshape(1, l_slots),
        lateral_targets.reshape(1, l_slots),
        lateral_counts,
        vertical_rows.reshape(1, v_slots),
        vertical_peers.reshape(1, v_slots),
        vertical_targets.reshape(1, v_slots),
        vertical_tiles,
    )
    lateral = call(lateral_lists_kernel, matrices(l_slots, 3), codes)
    returned = first_returned = to_depth(partial)
    for step in range(LEVEL_STEPS):
        base, to_first, to_second = call(
            lateral_kernel, [state, sent, sent], adjoint, returned, wet, *lateral, lateral_tiles
        )
        received = swapped(to_first, to_second)
        if step < LEVEL_STEPS - 1:
            adjoint, partial = call(
                vertical_kernel,
                [state, ((GROUPS * STATE, CELLS), BF)],
                base,
                *received,
                wet,
                *vertical,
                vertical_tiles,
            )
            returned = to_depth(partial)

    def tracer_matrices(slots, blocks):
        rows = slots * PAIR
        return [((GROUPS * rows, STATE), BF)] * 2 + [((GROUPS, blocks * STATE, rows), BF)]

    constants = call(
        tracer_lists_kernel,
        [state] + tracer_matrices(v_slots, 1) + tracer_matrices(l_slots, 3),
        first_returned,
        lengths,
    )
    (value,) = call(sum_kernel, [state], base, *received)
    value, gathered = lax.optimization_barrier((value, gathered))
    value = to_depth(value)
    for step in range(LEVEL_STEPS, STEPS):
        if step == LEVEL_STEPS:
            arrived, body = (value,), tracer_first_kernel
        else:
            arrived, body = (base, *received), tracer_kernel
        base, to_first, to_second = call(body, [state, sent, sent], *arrived, *constants, gathered)
        received = swapped(to_first, to_second)
    (value,) = call(sum_kernel, [state], base, *received)
    (adjoint,) = call(close_kernel, [((LEVELS, TRACERS, CELLS), F32)], to_depth(value), wet)
    return adjoint


def solution(mesh):
    return jax.shard_map(
        local,
        mesh=mesh,
        in_specs=(
            P("depth", None, "region"),
            P("region"),
            P("depth", "region", None),
            P("depth", "region"),
            P("depth", "region"),
            P("depth", "region"),
            P("depth", "region"),
            P("depth", "region", None),
            P("depth", "region"),
            P("depth", "region"),
            P("depth", "region"),
        ),
        out_specs=P("depth", None, "region"),
        check_vma=False,
    )
```

time: 345 us -> 279 us (0.81)
  waiting for transfers between devices: 134 us -> 43.2 us
  blocking collectives: 0 us -> 61.1 us
  Pallas kernels: 0 us -> 52.4 us
  matrix products: 50.2 us -> 0 us
  starting transfers between devices: 140 us -> 94.5 us
  between operations: 0.68 us -> 14.6 us
    all_to_all x12 -> x2, waiting for transfers between devices: 77.4 us -> 8.77 us  [to_depth(): lax.all_to_all(value, 'depth', split_axis=0, concat_axis=0, tiled=True)]
    all_to_all x0 -> x4, blocking collectives: none -> 61.1 us  [to_depth(): lax.all_to_all(value, 'depth', split_axis=0, concat_axis=0, tiled=True)]
    all_to_all x12 -> x2, starting transfers between devices: 70.9 us -> 16.2 us  [to_depth(): lax.all_to_all(value, 'depth', split_axis=0, concat_axis=0, tiled=True)]
    pallas_call x0 -> x21, Pallas kernels: none -> 52.4 us  [call(): pl.pallas_call(body, out_shape=[jax.ShapeDtypeStruct(shape, kind) for sha...]
    dot_general x72 -> x0, matrix products: 50.2 us -> none  [the longest x24 21.6 us: partial_sums(): jnp.einsum('ktc,kce->kte', picked, tile_set, preferred_element_type=jnp.f...]
    ppermute x24, waiting for transfers between devices: 56.7 us -> 34.4 us  [the longest x12 19.8 us: swapped(): from_first = lax.ppermute(to_first, 'region', first)]
    convert_element_type x12 -> x0, local copies, waits for them, and re-layouts: 10.5 us -> none  [partial_sums(): return summed.astype(jnp.bfloat16)]
    unnamed x0 -> x36, local copies, waits for them, and re-layouts: none -> 9.1 us
  transfers between devices with their start and end apart: 36 -> 27, of which waited for: 24 -> 20; matrix products, arithmetic and copies ran while one was open for 0% -> 0% of each run, Pallas kernels for 0% -> 4%
where the time goes in v3:
time: 279 us; the launch traced here: 278 us
  starting transfers between devices  94.5 us (34%)
  blocking collectives  61.1 us (22%)
  Pallas kernels  52.4 us (19%)
  waiting for transfers between devices  43.2 us (15%)
  between operations  14.6 us (5%)
  local copies, waits for them, and re-layouts  9.1 us (3%)
  other arithmetic  3.12 us (1%)
    all_to_all x4, blocking collectives, to_depth(): lax.all_to_all(value, 'depth', split_axis=0, concat_axis=0, tiled=True)  61.1 us
    ppermute x12, starting transfers between devices, swapped(): from_first = lax.ppermute(to_first, 'region', first)  54.8 us
    pallas_call x21, Pallas kernels, call(): pl.pallas_call(body, out_shape=[jax.ShapeDtypeStruct(shape, kind) for sha...  52.4 us
    ppermute x12, starting transfers between devices, swapped(): from_second = lax.ppermute(to_second, 'region', second)  23.4 us
    ppermute x12, waiting for transfers between devices, swapped(): from_first = lax.ppermute(to_first, 'region', first)  19.8 us
    all_to_all x2, starting transfers between devices, to_depth(): lax.all_to_all(value, 'depth', split_axis=0, concat_axis=0, tiled=True)  16.2 us
    ppermute x12, waiting for transfers between devices, swapped(): from_second = lax.ppermute(to_second, 'region', second)  14.7 us
    unnamed x36, local copies, waits for them, and re-layouts  9.1 us
  transfers between devices with their start and end apart: 27, of which 20 were waited for; matrix products, arithmetic and copies ran while one was open for 0% of the time, Pallas kernels for 4%

profile of v3, /device:TPU:1, one launch (start us, length us, event | category | flops | bytes accessed | tf_op | source)
XLA Modules:
  0.0 278.0 jit_solution(2988444041831923723)
XLA Ops:
  13.2 10.8 %all-to-all-start = ((bf16[8,144,128]{2,1,0:T(8,128)(2,1)}), bf16[8,144,128]{2,1,0:T(8,128)(2,1)}, u32[]{:S(2)}, u32[]{:S(2)}) async-start(bf16[8,144,128]{2,1,0:T(8,128)(2,1)} %bitcast.7), calls=%async_computation | async-start | bytes 589824 | tf_op jit(solution)/shard_map/all_to_all | solution.py:232
  25.2 5.7 %all-to-all-done = bf16[8,144,128]{2,1,0:T(8,128)(2,1)} async-done(((bf16[8,144,128]{2,1,0:T(8,128)(2,1)}), bf16[8,144,128]{2,1,0:T(8,128)(2,1)}, u32[]{:S(2)}, u32[]{:S(2)}) %all-to-all-start) | async-done | bytes 294944 | tf_op jit(solution)/shard_map/all_to_all | solution.py:232
  34.7 8.5 %collective-permute-start = (bf16[128,128]{1,0:T(8,128)(2,1)S(1)}, bf16[128,128]{1,0:T(8,128)(2,1)S(1)}, u32[]{:S(2)}, u32[]{:S(2)}) collective-permute-start(bf16[128,128]{1,0:T(8,128)(2,1)S(1)} %get-tuple-element.74), channel_id=1, source_target_pairs={{0,504},{8,16},{16,8},{24,32},{32,24},{40,48},{48,40},{56,64},{64,... | collective-permute-start | bytes 98312 | tf_op jit(solution)/shard_map/ppermute | solution.py:226
  49.0 14.3 %all_to_all.66 = bf16[8,128,128]{2,1,0:T(8,128)(2,1)S(1)} all-to-all(bf16[8,128,128]{2,1,0:T(8,128)(2,1)S(1)} %bitcast.26), channel_id=1, replica_groups=mesh['region'=64,'depth'=8] {'depth'}, dimensions={0} | all-to-all | bytes 524288 | tf_op jit(solution)/shard_map/all_to_all | solution.py:232
  73.0 14.1 %all_to_all.67 = bf16[8,128,128]{2,1,0:T(8,128)(2,1)S(1)} all-to-all(bf16[8,128,128]{2,1,0:T(8,128)(2,1)S(1)} %bitcast.27), channel_id=1, replica_groups=mesh['region'=64,'depth'=8] {'depth'}, dimensions={0} | all-to-all | bytes 524288 | tf_op jit(solution)/shard_map/all_to_all | solution.py:232
  88.0 5.6 %collective-permute-start.4 = (bf16[128,128]{1,0:T(8,128)(2,1)S(1)}, bf16[128,128]{1,0:T(8,128)(2,1)S(1)}, u32[]{:S(2)}, u32[]{:S(2)}) collective-permute-start(bf16[128,128]{1,0:T(8,128)(2,1)S(1)} %get-tuple-element.87), channel_id=1, source_target_pairs={{0,504},{8,16},{16,8},{24,32},{32,24},{40,48},{48,40},{56,64},{64,... | collective-permute-start | bytes 98312 | tf_op jit(solution)/shard_map/ppermute | solution.py:226
  99.4 14.1 %all_to_all.68 = bf16[8,128,128]{2,1,0:T(8,128)(2,1)S(1)} all-to-all(bf16[8,128,128]{2,1,0:T(8,128)(2,1)S(1)} %bitcast.25), channel_id=1, replica_groups=mesh['region'=64,'depth'=8] {'depth'}, dimensions={0} | all-to-all | bytes 524288 | tf_op jit(solution)/shard_map/all_to_all | solution.py:232
  123.0 5.3 %all-to-all-start.4 = ((f32[8,16,128]{2,1,0:T(8,128)}), f32[8,16,128]{2,1,0:T(8,128)S(1)}, u32[]{:S(2)}, u32[]{:S(2)}) async-start(f32[8,16,128]{2,1,0:T(8,128)} %bitcast.15), calls=%async_computation.4 | async-start | bytes 131072 | tf_op jit(solution)/shard_map/all_to_all | solution.py:232
  133.2 5.8 %copy-done = bf16[512,128,128]{2,1,0:T(8,128)(2,1)S(1)} copy-done((bf16[512,128,128]{2,1,0:T(8,128)(2,1)S(1)}, bf16[512,128,128]{2,1,0:T(8,128)(2,1)}, u32[]{:S(2)}) %copy-start) | copy-done | bytes 16777240
  139.0 5.0 %shard_map.120 = (f32[128,128]{1,0:T(8,128)S(1)}, bf16[128,128]{1,0:T(8,128)(2,1)S(1)}, bf16[128,128]{1,0:T(8,128)(2,1)S(1)}) custom-call(f32[128,128]{1,0:T(8,128)S(1)} %bitcast.22, f32[128,128]{1,0:T(8,128)S(1)} %get-tuple-element.95.refs_0_, bf16[256,128]{1,0:T(8,128)(2,1)S(1)} %get-tuple-element.96.refs_1_, ...), custom_call_target="tpu_custom_call" | custom-call | tf_op jit(solution)/shard_map/pallas_call | solution.py:212
  144.0 5.6 %collective-permute-start.8 = (bf16[128,128]{1,0:T(8,128)(2,1)S(1)}, bf16[128,128]{1,0:T(8,128)(2,1)S(1)}, u32[]{:S(2)}, u32[]{:S(2)}) collective-permute-start(bf16[128,128]{1,0:T(8,128)(2,1)S(1)} %get-tuple-element.104), channel_id=1, source_target_pairs={{0,504},{8,16},{16,8},{24,32},{32,24},{40,48},{48,40},{56,64},{64,... | collective-permute-start | bytes 98312 | tf_op jit(solution)/shard_map/ppermute | solution.py:226
  154.2 5.0 %shard_map.121 = (f32[128,128]{1,0:T(8,128)S(1)}, bf16[128,128]{1,0:T(8,128)(2,1)S(1)}, bf16[128,128]{1,0:T(8,128)(2,1)S(1)}) custom-call(f32[128,128]{1,0:T(8,128)S(1)} %get-tuple-element.103.base, bf16[128,128]{1,0:T(8,128)(2,1)S(1)} %collective-permute-done.8.first, bf16[128,128]{1,0:T(8,128)(2,1)S(1)} %collective-permute-done.9.second, ...), custom_call_target="tpu_custom_call" | custom-call | tf_op jit(solution)/shard_map/pallas_call | solution.py:212
  159.3 3.3 %collective-permute-start.10 = (bf16[128,128]{1,0:T(8,128)(2,1)S(1)}, bf16[128,128]{1,0:T(8,128)(2,1)S(1)}, u32[]{:S(2)}, u32[]{:S(2)}) collective-permute-start(bf16[128,128]{1,0:T(8,128)(2,1)S(1)} %get-tuple-element.107), channel_id=1, source_target_pairs={{0,504},{8,16},{16,8},{24,32},{32,24},{40,48},{48,40},{56,64},{64,... | collective-permute-start | bytes 98312 | tf_op jit(solution)/shard_map/ppermute | solution.py:226
  167.3 5.0 %shard_map.122 = (f32[128,128]{1,0:T(8,128)S(1)}, bf16[128,128]{1,0:T(8,128)(2,1)S(1)}, bf16[128,128]{1,0:T(8,128)(2,1)S(1)}) custom-call(f32[128,128]{1,0:T(8,128)S(1)} %get-tuple-element.106.base, bf16[128,128]{1,0:T(8,128)(2,1)S(1)} %collective-permute-done.10.first, bf16[128,128]{1,0:T(8,128)(2,1)S(1)} %collective-permute-done.11.second, ...), custom_call_target="tpu_custom_call" | custom-call | tf_op jit(solution)/shard_map/pallas_call | solution.py:212
  172.3 5.6 %collective-permute-start.12 = (bf16[128,128]{1,0:T(8,128)(2,1)S(1)}, bf16[128,128]{1,0:T(8,128)(2,1)S(1)}, u32[]{:S(2)}, u32[]{:S(2)}) collective-permute-start(bf16[128,128]{1,0:T(8,128)(2,1)S(1)} %get-tuple-element.110), channel_id=1, source_target_pairs={{0,504},{8,16},{16,8},{24,32},{32,24},{40,48},{48,40},{56,64},{64,... | collective-permute-start | bytes 98312 | tf_op jit(solution)/shard_map/ppermute | solution.py:226
  182.8 5.0 %shard_map.123 = (f32[128,128]{1,0:T(8,128)S(1)}, bf16[128,128]{1,0:T(8,128)(2,1)S(1)}, bf16[128,128]{1,0:T(8,128)(2,1)S(1)}) custom-call(f32[128,128]{1,0:T(8,128)S(1)} %get-tuple-element.109.base, bf16[128,128]{1,0:T(8,128)(2,1)S(1)} %collective-permute-done.12.first, bf16[128,128]{1,0:T(8,128)(2,1)S(1)} %collective-permute-done.13.second, ...), custom_call_target="tpu_custom_call" | custom-call | tf_op jit(solution)/shard_map/pallas_call | solution.py:212
  195.9 5.0 %shard_map.124 = (f32[128,128]{1,0:T(8,128)S(1)}, bf16[128,128]{1,0:T(8,128)(2,1)S(1)}, bf16[128,128]{1,0:T(8,128)(2,1)S(1)}) custom-call(f32[128,128]{1,0:T(8,128)S(1)} %get-tuple-element.112.base, bf16[128,128]{1,0:T(8,128)(2,1)S(1)} %collective-permute-done.14.first, bf16[128,128]{1,0:T(8,128)(2,1)S(1)} %collective-permute-done.15.second, ...), custom_call_target="tpu_custom_call" | custom-call | tf_op jit(solution)/shard_map/pallas_call | solution.py:212
  200.9 5.3 %collective-permute-start.16 = (bf16[128,128]{1,0:T(8,128)(2,1)S(1)}, bf16[128,128]{1,0:T(8,128)(2,1)S(1)}, u32[]{:S(2)}, u32[]{:S(2)}) collective-permute-start(bf16[128,128]{1,0:T(8,128)(2,1)S(1)} %get-tuple-element.116), channel_id=1, source_target_pairs={{0,504},{8,16},{16,8},{24,32},{32,24},{40,48},{48,40},{56,64},{64,... | collective-permute-start | bytes 98312 | tf_op jit(solution)/shard_map/ppermute | solution.py:226
  210.9 5.0 %shard_map.125 = (f32[128,128]{1,0:T(8,128)S(1)}, bf16[128,128]{1,0:T(8,128)(2,1)S(1)}, bf16[128,128]{1,0:T(8,128)(2,1)S(1)}) custom-call(f32[128,128]{1,0:T(8,128)S(1)} %get-tuple-element.115.base, bf16[128,128]{1,0:T(8,128)(2,1)S(1)} %collective-permute-done.16.first, bf16[128,128]{1,0:T(8,128)(2,1)S(1)} %collective-permute-done.17.second, ...), custom_call_target="tpu_custom_call" | custom-call | tf_op jit(solution)/shard_map/pallas_call | solution.py:212
  215.9 3.3 %collective-permute-start.18 = (bf16[128,128]{1,0:T(8,128)(2,1)S(1)}, bf16[128,128]{1,0:T(8,128)(2,1)S(1)}, u32[]{:S(2)}, u32[]{:S(2)}) collective-permute-start(bf16[128,128]{1,0:T(8,128)(2,1)S(1)} %get-tuple-element.119), channel_id=1, source_target_pairs={{0,504},{8,16},{16,8},{24,32},{32,24},{40,48},{48,40},{56,64},{64,... | collective-permute-start | bytes 98312 | tf_op jit(solution)/shard_map/ppermute | solution.py:226
  223.9 5.0 %shard_map.126 = (f32[128,128]{1,0:T(8,128)S(1)}, bf16[128,128]{1,0:T(8,128)(2,1)S(1)}, bf16[128,128]{1,0:T(8,128)(2,1)S(1)}) custom-call(f32[128,128]{1,0:T(8,128)S(1)} %get-tuple-element.118.base, bf16[128,128]{1,0:T(8,128)(2,1)S(1)} %collective-permute-done.18.first, bf16[128,128]{1,0:T(8,128)(2,1)S(1)} %collective-permute-done.19.second, ...), custom_call_target="tpu_custom_call" | custom-call | tf_op jit(solution)/shard_map/pallas_call | solution.py:212
  228.9 5.3 %collective-permute-start.20 = (bf16[128,128]{1,0:T(8,128)(2,1)S(1)}, bf16[128,128]{1,0:T(8,128)(2,1)S(1)}, u32[]{:S(2)}, u32[]{:S(2)}) collective-permute-start(bf16[128,128]{1,0:T(8,128)(2,1)S(1)} %get-tuple-element.122), channel_id=1, source_target_pairs={{0,504},{8,16},{16,8},{24,32},{32,24},{40,48},{48,40},{56,64},{64,... | collective-permute-start | bytes 98312 | tf_op jit(solution)/shard_map/ppermute | solution.py:226
  238.9 5.0 %shard_map.127 = (f32[128,128]{1,0:T(8,128)S(1)}, bf16[128,128]{1,0:T(8,128)(2,1)S(1)}, bf16[128,128]{1,0:T(8,128)(2,1)S(1)}) custom-call(f32[128,128]{1,0:T(8,128)S(1)} %get-tuple-element.121.base, bf16[128,128]{1,0:T(8,128)(2,1)S(1)} %collective-permute-done.20.first, bf16[128,128]{1,0:T(8,128)(2,1)S(1)} %collective-permute-done.21.second, ...), custom_call_target="tpu_custom_call" | custom-call | tf_op jit(solution)/shard_map/pallas_call | solution.py:212
  251.9 18.6 %all_to_all.69 = f32[8,16,128]{2,1,0:T(8,128)S(1)} all-to-all(f32[8,16,128]{2,1,0:T(8,128)S(1)} %bitcast.23), channel_id=1, replica_groups=mesh['region'=64,'depth'=8] {'depth'}, dimensions={0} | all-to-all | bytes 131072 | tf_op jit(solution)/shard_map/all_to_all | solution.py:232
  (93 shorter events, 92.0 us)
Async XLA Ops:
  6.5 116.4 %all-gather.2.cloned.1.call-start = ((), (), s32[]{:S(2)}) async-start(), calls=%async_computation.6 | async-start | bytes 18874368 | tf_op jit(solution)/shard_map/all_gather | solution.py:248
  13.2 17.8 %all-to-all-start = ((bf16[8,144,128]{2,1,0:T(8,128)(2,1)}), bf16[8,144,128]{2,1,0:T(8,128)(2,1)}, u32[]{:S(2)}, u32[]{:S(2)}) async-start(bf16[8,144,128]{2,1,0:T(8,128)(2,1)} %bitcast.7), calls=%async_computation | async-start | bytes 589824 | tf_op jit(solution)/shard_map/all_to_all | solution.py:232
  34.7 10.5 %collective-permute-start = (bf16[128,128]{1,0:T(8,128)(2,1)S(1)}, bf16[128,128]{1,0:T(8,128)(2,1)S(1)}, u32[]{:S(2)}, u32[]{:S(2)}) collective-permute-start(bf16[128,128]{1,0:T(8,128)(2,1)S(1)} %get-tuple-element.74), channel_id=1, source_target_pairs={{0,504},{8,16},{16,8},{24,32},{32,24},{40,48},{48,40},{56,64},{64,... | collective-permute-start | bytes 98312 | tf_op jit(solution)/shard_map/ppermute | solution.py:226
  43.2 5.1 %collective-permute-start.1 = (bf16[128,128]{1,0:T(8,128)(2,1)S(1)}, bf16[128,128]{1,0:T(8,128)(2,1)S(1)}, u32[]{:S(2)}, u32[]{:S(2)}) collective-permute-start(bf16[128,128]{1,0:T(8,128)(2,1)S(1)} %get-tuple-element.75), channel_id=1, source_target_pairs={{0,8},{8,0},{16,24},{24,16},{32,40},{40,32},{48,56},{56,48},{64,72... | collective-permute-start | bytes 98312 | tf_op jit(solution)/shard_map/ppermute | solution.py:227
  64.2 8.0 %collective-permute-start.2 = (bf16[128,128]{1,0:T(8,128)(2,1)S(1)}, bf16[128,128]{1,0:T(8,128)(2,1)S(1)}, u32[]{:S(2)}, u32[]{:S(2)}) collective-permute-start(bf16[128,128]{1,0:T(8,128)(2,1)S(1)} %get-tuple-element.82), channel_id=1, source_target_pairs={{0,504},{8,16},{16,8},{24,32},{32,24},{40,48},{48,40},{56,64},{64,... | collective-permute-start | bytes 98312 | tf_op jit(solution)/shard_map/ppermute | solution.py:226
  67.2 5.1 %collective-permute-start.3 = (bf16[128,128]{1,0:T(8,128)(2,1)S(1)}, bf16[128,128]{1,0:T(8,128)(2,1)S(1)}, u32[]{:S(2)}, u32[]{:S(2)}) collective-permute-start(bf16[128,128]{1,0:T(8,128)(2,1)S(1)} %get-tuple-element.83), channel_id=1, source_target_pairs={{0,8},{8,0},{16,24},{24,16},{32,40},{40,32},{48,56},{56,48},{64,72... | collective-permute-start | bytes 98312 | tf_op jit(solution)/shard_map/ppermute | solution.py:227
  88.0 8.0 %collective-permute-start.4 = (bf16[128,128]{1,0:T(8,128)(2,1)S(1)}, bf16[128,128]{1,0:T(8,128)(2,1)S(1)}, u32[]{:S(2)}, u32[]{:S(2)}) collective-permute-start(bf16[128,128]{1,0:T(8,128)(2,1)S(1)} %get-tuple-element.87), channel_id=1, source_target_pairs={{0,504},{8,16},{16,8},{24,32},{32,24},{40,48},{48,40},{56,64},{64,... | collective-permute-start | bytes 98312 | tf_op jit(solution)/shard_map/ppermute | solution.py:226
  93.6 5.1 %collective-permute-start.5 = (bf16[128,128]{1,0:T(8,128)(2,1)S(1)}, bf16[128,128]{1,0:T(8,128)(2,1)S(1)}, u32[]{:S(2)}, u32[]{:S(2)}) collective-permute-start(bf16[128,128]{1,0:T(8,128)(2,1)S(1)} %get-tuple-element.88), channel_id=1, source_target_pairs={{0,8},{8,0},{16,24},{24,16},{32,40},{40,32},{48,56},{56,48},{64,72... | collective-permute-start | bytes 98312 | tf_op jit(solution)/shard_map/ppermute | solution.py:227
  114.4 8.0 %collective-permute-start.6 = (bf16[128,128]{1,0:T(8,128)(2,1)S(1)}, bf16[128,128]{1,0:T(8,128)(2,1)S(1)}, u32[]{:S(2)}, u32[]{:S(2)}) collective-permute-start(bf16[128,128]{1,0:T(8,128)(2,1)S(1)} %get-tuple-element.92), channel_id=1, source_target_pairs={{0,504},{8,16},{16,8},{24,32},{32,24},{40,48},{48,40},{56,64},{64,... | collective-permute-start | bytes 98312 | tf_op jit(solution)/shard_map/ppermute | solution.py:226
  117.4 4.9 %collective-permute-start.7 = (bf16[128,128]{1,0:T(8,128)(2,1)S(1)}, bf16[128,128]{1,0:T(8,128)(2,1)S(1)}, u32[]{:S(2)}, u32[]{:S(2)}) collective-permute-start(bf16[128,128]{1,0:T(8,128)(2,1)S(1)} %get-tuple-element.93), channel_id=1, source_target_pairs={{0,8},{8,0},{16,24},{24,16},{32,40},{40,32},{48,56},{56,48},{64,72... | collective-permute-start | bytes 98312 | tf_op jit(solution)/shard_map/ppermute | solution.py:227
  123.0 10.2 %all-to-all-start.4 = ((f32[8,16,128]{2,1,0:T(8,128)}), f32[8,16,128]{2,1,0:T(8,128)S(1)}, u32[]{:S(2)}, u32[]{:S(2)}) async-start(f32[8,16,128]{2,1,0:T(8,128)} %bitcast.15), calls=%async_computation.4 | async-start | bytes 131072 | tf_op jit(solution)/shard_map/all_to_all | solution.py:232
  144.0 8.0 %collective-permute-start.8 = (bf16[128,128]{1,0:T(8,128)(2,1)S(1)}, bf16[128,128]{1,0:T(8,128)(2,1)S(1)}, u32[]{:S(2)}, u32[]{:S(2)}) collective-permute-start(bf16[128,128]{1,0:T(8,128)(2,1)S(1)} %get-tuple-element.104), channel_id=1, source_target_pairs={{0,504},{8,16},{16,8},{24,32},{32,24},{40,48},{48,40},{56,64},{64,... | collective-permute-start | bytes 98312 | tf_op jit(solution)/shard_map/ppermute | solution.py:226
  159.3 8.0 %collective-permute-start.10 = (bf16[128,128]{1,0:T(8,128)(2,1)S(1)}, bf16[128,128]{1,0:T(8,128)(2,1)S(1)}, u32[]{:S(2)}, u32[]{:S(2)}) collective-permute-start(bf16[128,128]{1,0:T(8,128)(2,1)S(1)} %get-tuple-element.107), channel_id=1, source_target_pairs={{0,504},{8,16},{16,8},{24,32},{32,24},{40,48},{48,40},{56,64},{64,... | collective-permute-start | bytes 98312 | tf_op jit(solution)/shard_map/ppermute | solution.py:226
  162.6 4.7 %collective-permute-start.11 = (bf16[128,128]{1,0:T(8,128)(2,1)S(1)}, bf16[128,128]{1,0:T(8,128)(2,1)S(1)}, u32[]{:S(2)}, u32[]{:S(2)}) collective-permute-start(bf16[128,128]{1,0:T(8,128)(2,1)S(1)} %get-tuple-element.108), channel_id=1, source_target_pairs={{0,8},{8,0},{16,24},{24,16},{32,40},{40,32},{48,56},{56,48},{64,72... | collective-permute-start | bytes 98312 | tf_op jit(solution)/shard_map/ppermute | solution.py:227
  172.3 8.0 %collective-permute-start.12 = (bf16[128,128]{1,0:T(8,128)(2,1)S(1)}, bf16[128,128]{1,0:T(8,128)(2,1)S(1)}, u32[]{:S(2)}, u32[]{:S(2)}) collective-permute-start(bf16[128,128]{1,0:T(8,128)(2,1)S(1)} %get-tuple-element.110), channel_id=1, source_target_pairs={{0,504},{8,16},{16,8},{24,32},{32,24},{40,48},{48,40},{56,64},{64,... | collective-permute-start | bytes 98312 | tf_op jit(solution)/shard_map/ppermute | solution.py:226
  177.9 5.0 %collective-permute-start.13 = (bf16[128,128]{1,0:T(8,128)(2,1)S(1)}, bf16[128,128]{1,0:T(8,128)(2,1)S(1)}, u32[]{:S(2)}, u32[]{:S(2)}) collective-permute-start(bf16[128,128]{1,0:T(8,128)(2,1)S(1)} %get-tuple-element.111), channel_id=1, source_target_pairs={{0,8},{8,0},{16,24},{24,16},{32,40},{40,32},{48,56},{56,48},{64,72... | collective-permute-start | bytes 98312 | tf_op jit(solution)/shard_map/ppermute | solution.py:227
  187.9 8.0 %collective-permute-start.14 = (bf16[128,128]{1,0:T(8,128)(2,1)S(1)}, bf16[128,128]{1,0:T(8,128)(2,1)S(1)}, u32[]{:S(2)}, u32[]{:S(2)}) collective-permute-start(bf16[128,128]{1,0:T(8,128)(2,1)S(1)} %get-tuple-element.113), channel_id=1, source_target_pairs={{0,504},{8,16},{16,8},{24,32},{32,24},{40,48},{48,40},{56,64},{64,... | collective-permute-start | bytes 98312 | tf_op jit(solution)/shard_map/ppermute | solution.py:226
  190.9 5.0 %collective-permute-start.15 = (bf16[128,128]{1,0:T(8,128)(2,1)S(1)}, bf16[128,128]{1,0:T(8,128)(2,1)S(1)}, u32[]{:S(2)}, u32[]{:S(2)}) collective-permute-start(bf16[128,128]{1,0:T(8,128)(2,1)S(1)} %get-tuple-element.114), channel_id=1, source_target_pairs={{0,8},{8,0},{16,24},{24,16},{32,40},{40,32},{48,56},{56,48},{64,72... | collective-permute-start | bytes 98312 | tf_op jit(solution)/shard_map/ppermute | solution.py:227
  200.9 8.0 %collective-permute-start.16 = (bf16[128,128]{1,0:T(8,128)(2,1)S(1)}, bf16[128,128]{1,0:T(8,128)(2,1)S(1)}, u32[]{:S(2)}, u32[]{:S(2)}) collective-permute-start(bf16[128,128]{1,0:T(8,128)(2,1)S(1)} %get-tuple-element.116), channel_id=1, source_target_pairs={{0,504},{8,16},{16,8},{24,32},{32,24},{40,48},{48,40},{56,64},{64,... | collective-permute-start | bytes 98312 | tf_op jit(solution)/shard_map/ppermute | solution.py:226
  215.9 8.0 %collective-permute-start.18 = (bf16[128,128]{1,0:T(8,128)(2,1)S(1)}, bf16[128,128]{1,0:T(8,128)(2,1)S(1)}, u32[]{:S(2)}, u32[]{:S(2)}) collective-permute-start(bf16[128,128]{1,0:T(8,128)(2,1)S(1)} %get-tuple-element.119), channel_id=1, source_target_pairs={{0,504},{8,16},{16,8},{24,32},{32,24},{40,48},{48,40},{56,64},{64,... | collective-permute-start | bytes 98312 | tf_op jit(solution)/shard_map/ppermute | solution.py:226
  219.2 4.7 %collective-permute-start.19 = (bf16[128,128]{1,0:T(8,128)(2,1)S(1)}, bf16[128,128]{1,0:T(8,128)(2,1)S(1)}, u32[]{:S(2)}, u32[]{:S(2)}) collective-permute-start(bf16[128,128]{1,0:T(8,128)(2,1)S(1)} %get-tuple-element.120), channel_id=1, source_target_pairs={{0,8},{8,0},{16,24},{24,16},{32,40},{40,32},{48,56},{56,48},{64,72... | collective-permute-start | bytes 98312 | tf_op jit(solution)/shard_map/ppermute | solution.py:227
  228.9 8.0 %collective-permute-start.20 = (bf16[128,128]{1,0:T(8,128)(2,1)S(1)}, bf16[128,128]{1,0:T(8,128)(2,1)S(1)}, u32[]{:S(2)}, u32[]{:S(2)}) collective-permute-start(bf16[128,128]{1,0:T(8,128)(2,1)S(1)} %get-tuple-element.122), channel_id=1, source_target_pairs={{0,504},{8,16},{16,8},{24,32},{32,24},{40,48},{48,40},{56,64},{64,... | collective-permute-start | bytes 98312 | tf_op jit(solution)/shard_map/ppermute | solution.py:226
  243.9 8.0 %collective-permute-start.22 = (bf16[128,128]{1,0:T(8,128)(2,1)S(1)}, bf16[128,128]{1,0:T(8,128)(2,1)S(1)}, u32[]{:S(2)}, u32[]{:S(2)}) collective-permute-start(bf16[128,128]{1,0:T(8,128)(2,1)S(1)} %get-tuple-element.125), channel_id=1, source_target_pairs={{0,504},{8,16},{16,8},{24,32},{32,24},{40,48},{48,40},{56,64},{64,... | collective-permute-start | bytes 98312 | tf_op jit(solution)/shard_map/ppermute | solution.py:226
  247.3 4.7 %collective-permute-start.23 = (bf16[128,128]{1,0:T(8,128)(2,1)S(1)}, bf16[128,128]{1,0:T(8,128)(2,1)S(1)}, u32[]{:S(2)}, u32[]{:S(2)}) collective-permute-start(bf16[128,128]{1,0:T(8,128)(2,1)S(1)} %get-tuple-element.126), channel_id=1, source_target_pairs={{0,8},{8,0},{16,24},{24,16},{32,40},{40,32},{48,56},{56,48},{64,72... | collective-permute-start | bytes 98312 | tf_op jit(solution)/shard_map/ppermute | solution.py:227
  (21 other events, 98.0 us)
Sparse Core Ops, SparseCore 0:
  9.9 106.7 all-gather.1

commit v4 on v3

--- a/solution.py
+++ b/solution.py
@@ -132,7 +132,7 @@
     base[...] = value + partial[STATE : 2 * STATE].astype(F32)
 
 
-def tracer_lists_kernel(returned, lengths, wet, v_left, v_right, v_place, l_left, l_right, l_place):
+def tracer_lists_kernel(returned, lengths, wet, v_left, v_right, v_place, l_left, l_right, l_place, lines_l, lines_v):
     level = iota((STATE, CELLS), 0) // PAIR
     wet[...] = jnp.where(level < lengths[...], 1.0, 0.0)
     l_rows, v_rows = l_left.shape[0] // GROUPS, v_left.shape[0] // GROUPS
@@ -149,20 +149,23 @@
             if row_of == 0:
                 wanted = block // LEVELS * STATE + (depth * LEVELS + block % LEVELS) * PAIR + pair
                 wanted = jnp.where(block < 0, -1, wanted)
-                write_place(wanted, l_place.at[depth])
             else:
-                write_place(block * PAIR + pair, v_place.at[depth])
-
-
-def tracer_products(rows, left, right, place, tiles, first, slots):
+                wanted = block * PAIR + pair
+            line = lines_l if row_of == 0 else lines_v
+            line[:, part] = jnp.broadcast_to(wanted, (8, rows))
+    write_place(lines_l[0:1], l_place)
+    write_place(lines_v[0:1], v_place)
+
+
+def tracer_products(rows, left, right, place, tiles, first, slots, scratch):
+    x_left, x_right, product = scratch
+    count = left.shape[0]
     rows = rows.astype(BF)
-    x_left = dot(left[...], rows).astype(BF)
-    x_right = dot(right[...], rows).astype(BF)
+    x_left[:count] = dot(left[...], rows).astype(BF)
+    x_right[:count] = dot(right[...], rows).astype(BF)
     upper_rows = iota((8, CELLS), 0) < 2 * PAIR
     blocks = tiles.shape[0] // GROUPS
-    total = None
     for depth in range(GROUPS):
-        parts = []
         for octet in range(slots // 8):
             at = (depth * slots + octet * 8) * PAIR
             part = slice(at, at + 8 * PAIR)
@@ -172,17 +175,15 @@
                 upper = jnp.concatenate([tiles[tile], tiles[tile + 2]], axis=1)
                 lower = jnp.concatenate([tiles[tile + 1], tiles[tile + 3]], axis=1)
                 out = dot(lhs, jnp.concatenate([upper, lower], axis=0))[8 * quad : 8 * quad + 8]
-                parts.append(jnp.where(upper_rows, out[:, :CELLS], out[:, CELLS:]))
-        sums = placed(place.at[depth], jnp.concatenate(parts, axis=0))
-        total = sums if total is None else total + sums
-    return total
-
-
-def tracer_step(value, wet, v_left, v_right, v_place, l_left, l_right, l_place, tiles, base, to_first, to_second):
+                product[at + 8 * quad : at + 8 * quad + 8] = jnp.where(upper_rows, out[:, :CELLS], out[:, CELLS:])
+    return placed(place, product[:count])
+
+
+def tracer_step(value, wet, v_left, v_right, v_place, l_left, l_right, l_place, tiles, base, to_first, to_second, *scratch):
     l_slots, v_slots = l_left.shape[0] // (GROUPS * PAIR), v_left.shape[0] // (GROUPS * PAIR)
     value = wet[...] * value
-    value = wet[...] * (value + tracer_products(value, v_left, v_right, v_place, tiles, l_slots, v_slots))
-    partial = tracer_products(value, l_left, l_right, l_place, tiles, 0, l_slots)
+    value = wet[...] * (value + tracer_products(value, v_left, v_right, v_place, tiles, l_slots, v_slots, scratch))
+    partial = tracer_products(value, l_left, l_right, l_place, tiles, 0, l_slots, scratch)
     to_first[...] = partial[:STATE].astype(BF)
     to_second[...] = partial[2 * STATE :].astype(BF)
     base[...] = value + partial[STATE : 2 * STATE]
@@ -293,14 +294,17 @@
 
     def tracer_matrices(slots, blocks):
         rows = slots * PAIR
-        return [((GROUPS * rows, STATE), BF)] * 2 + [((GROUPS, blocks * STATE, rows), BF)]
+        return [((GROUPS * rows, STATE), BF)] * 2 + [((blocks * STATE, GROUPS * rows), BF)]
 
     constants = call(
         tracer_lists_kernel,
         [state] + tracer_matrices(v_slots, 1) + tracer_matrices(l_slots, 3),
         first_returned,
         lengths,
+        scratch=[pltpu.VMEM((8, GROUPS * slots * PAIR), I32) for slots in (l_slots, v_slots)],
     )
+    rows = GROUPS * l_slots * PAIR
+    scratch = [pltpu.VMEM((rows, CELLS), kind) for kind in (BF, BF, F32)]
     (value,) = call(sum_kernel, [state], base, *received)
     value, gathered = lax.optimization_barrier((value, gathered))
     value = to_depth(value)
@@ -309,7 +313,7 @@
             arrived, body = (value,), tracer_first_kernel
         else:
             arrived, body = (base, *received), tracer_kernel
-        base, to_first, to_second = call(body, [state, sent, sent], *arrived, *constants, gathered)
+        base, to_first, to_second = call(body, [state, sent, sent], *arrived, *constants, gathered, scratch=scratch)
         received = swapped(to_first, to_second)
     (value,) = call(sum_kernel, [state], base, *received)
     (adjoint,) = call(close_kernel, [((LEVELS, TRACERS, CELLS), F32)], to_depth(value), wet)

time: 279 us -> 267 us (0.957)
  Pallas kernels: 52.4 us -> 39.3 us
    pallas_call x21, Pallas kernels: 52.4 us -> 39.3 us  [call(): pl.pallas_call(body, out_shape=[jax.ShapeDtypeStruct(shape, kind) for sha...]
where the time goes in v4:
time: 267 us; the launch traced here: 265 us
  starting transfers between devices  94.7 us (35%)
  blocking collectives  61.1 us (23%)
  waiting for transfers between devices  43.4 us (16%)
  Pallas kernels  39.3 us (15%)
  between operations  14.6 us (5%)
  local copies, waits for them, and re-layouts  9.1 us (3%)
  other arithmetic  3.12 us (1%)
    all_to_all x4, blocking collectives, to_depth(): lax.all_to_all(value, 'depth', split_axis=0, concat_axis=0, tiled=True)  61.1 us
    ppermute x12, starting transfers between devices, swapped(): from_first = lax.ppermute(to_first, 'region', first)  55.1 us
    pallas_call x21, Pallas kernels, call(): pl.pallas_call(body, out_shape=[jax.ShapeDtypeStruct(shape, kind) for sha...  39.3 us
    ppermute x12, starting transfers between devices, swapped(): from_second = lax.ppermute(to_second, 'region', second)  23.4 us
    ppermute x12, waiting for transfers between devices, swapped(): from_first = lax.ppermute(to_first, 'region', first)  19.7 us
    all_to_all x2, starting transfers between devices, to_depth(): lax.all_to_all(value, 'depth', split_axis=0, concat_axis=0, tiled=True)  16.2 us
    ppermute x12, waiting for transfers between devices, swapped(): from_second = lax.ppermute(to_second, 'region', second)  14.7 us
    unnamed x36, local copies, waits for them, and re-layouts  9.1 us
  transfers between devices with their start and end apart: 27, of which 20 were waited for; matrix products, arithmetic and copies ran while one was open for 0% of the time, Pallas kernels for 4%

profile of v4, /device:TPU:1, one launch (start us, length us, event | category | flops | bytes accessed | tf_op | source)
XLA Modules:
  0.0 265.3 jit_solution(8602355114504504873)
XLA Ops:
  13.2 10.8 %all-to-all-start = ((bf16[8,144,128]{2,1,0:T(8,128)(2,1)}), bf16[8,144,128]{2,1,0:T(8,128)(2,1)}, u32[]{:S(2)}, u32[]{:S(2)}) async-start(bf16[8,144,128]{2,1,0:T(8,128)(2,1)} %bitcast.7), calls=%async_computation | async-start | bytes 589824 | tf_op jit(solution)/shard_map/all_to_all | solution.py:233
  25.2 5.7 %all-to-all-done = bf16[8,144,128]{2,1,0:T(8,128)(2,1)} async-done(((bf16[8,144,128]{2,1,0:T(8,128)(2,1)}), bf16[8,144,128]{2,1,0:T(8,128)(2,1)}, u32[]{:S(2)}, u32[]{:S(2)}) %all-to-all-start) | async-done | bytes 294944 | tf_op jit(solution)/shard_map/all_to_all | solution.py:233
  34.7 8.5 %collective-permute-start = (bf16[128,128]{1,0:T(8,128)(2,1)S(1)}, bf16[128,128]{1,0:T(8,128)(2,1)S(1)}, u32[]{:S(2)}, u32[]{:S(2)}) collective-permute-start(bf16[128,128]{1,0:T(8,128)(2,1)S(1)} %get-tuple-element.74), channel_id=1, source_target_pairs={{0,504},{8,16},{16,8},{24,32},{32,24},{40,48},{48,40},{56,64},{64,... | collective-permute-start | bytes 98312 | tf_op jit(solution)/shard_map/ppermute | solution.py:227
  49.0 14.3 %all_to_all.66 = bf16[8,128,128]{2,1,0:T(8,128)(2,1)S(1)} all-to-all(bf16[8,128,128]{2,1,0:T(8,128)(2,1)S(1)} %bitcast.26), channel_id=1, replica_groups=mesh['region'=64,'depth'=8] {'depth'}, dimensions={0} | all-to-all | bytes 524288 | tf_op jit(solution)/shard_map/all_to_all | solution.py:233
  73.0 14.1 %all_to_all.67 = bf16[8,128,128]{2,1,0:T(8,128)(2,1)S(1)} all-to-all(bf16[8,128,128]{2,1,0:T(8,128)(2,1)S(1)} %bitcast.27), channel_id=1, replica_groups=mesh['region'=64,'depth'=8] {'depth'}, dimensions={0} | all-to-all | bytes 524288 | tf_op jit(solution)/shard_map/all_to_all | solution.py:233
  88.0 5.6 %collective-permute-start.4 = (bf16[128,128]{1,0:T(8,128)(2,1)S(1)}, bf16[128,128]{1,0:T(8,128)(2,1)S(1)}, u32[]{:S(2)}, u32[]{:S(2)}) collective-permute-start(bf16[128,128]{1,0:T(8,128)(2,1)S(1)} %get-tuple-element.87), channel_id=1, source_target_pairs={{0,504},{8,16},{16,8},{24,32},{32,24},{40,48},{48,40},{56,64},{64,... | collective-permute-start | bytes 98312 | tf_op jit(solution)/shard_map/ppermute | solution.py:227
  99.4 14.1 %all_to_all.68 = bf16[8,128,128]{2,1,0:T(8,128)(2,1)S(1)} all-to-all(bf16[8,128,128]{2,1,0:T(8,128)(2,1)S(1)} %bitcast.25), channel_id=1, replica_groups=mesh['region'=64,'depth'=8] {'depth'}, dimensions={0} | all-to-all | bytes 524288 | tf_op jit(solution)/shard_map/all_to_all | solution.py:233
  123.0 5.3 %all-to-all-start.4 = ((f32[8,16,128]{2,1,0:T(8,128)}), f32[8,16,128]{2,1,0:T(8,128)S(1)}, u32[]{:S(2)}, u32[]{:S(2)}) async-start(f32[8,16,128]{2,1,0:T(8,128)} %bitcast.15), calls=%async_computation.4 | async-start | bytes 131072 | tf_op jit(solution)/shard_map/all_to_all | solution.py:233
  133.2 5.8 %copy-done = bf16[512,128,128]{2,1,0:T(8,128)(2,1)S(1)} copy-done((bf16[512,128,128]{2,1,0:T(8,128)(2,1)S(1)}, bf16[512,128,128]{2,1,0:T(8,128)(2,1)}, u32[]{:S(2)}) %copy-start) | copy-done | bytes 16777240
  139.0 3.4 %shard_map.120 = (f32[128,128]{1,0:T(8,128)S(1)}, bf16[128,128]{1,0:T(8,128)(2,1)S(1)}, bf16[128,128]{1,0:T(8,128)(2,1)S(1)}) custom-call(f32[128,128]{1,0:T(8,128)S(1)} %bitcast.22, f32[128,128]{1,0:T(8,128)S(1)} %get-tuple-element.95.refs_0_, bf16[256,128]{1,0:T(8,128)(2,1)S(1)} %get-tuple-element.96.refs_1_, ...), custom_call_target="tpu_custom_call" | custom-call | tf_op jit(solution)/shard_map/pallas_call | solution.py:213
  142.4 5.8 %collective-permute-start.8 = (bf16[128,128]{1,0:T(8,128)(2,1)S(1)}, bf16[128,128]{1,0:T(8,128)(2,1)S(1)}, u32[]{:S(2)}, u32[]{:S(2)}) collective-permute-start(bf16[128,128]{1,0:T(8,128)(2,1)S(1)} %get-tuple-element.104), channel_id=1, source_target_pairs={{0,504},{8,16},{16,8},{24,32},{32,24},{40,48},{48,40},{56,64},{64,... | collective-permute-start | bytes 98312 | tf_op jit(solution)/shard_map/ppermute | solution.py:227
  152.9 3.4 %shard_map.121 = (f32[128,128]{1,0:T(8,128)S(1)}, bf16[128,128]{1,0:T(8,128)(2,1)S(1)}, bf16[128,128]{1,0:T(8,128)(2,1)S(1)}) custom-call(f32[128,128]{1,0:T(8,128)S(1)} %get-tuple-element.103.base, bf16[128,128]{1,0:T(8,128)(2,1)S(1)} %collective-permute-done.8.first, bf16[128,128]{1,0:T(8,128)(2,1)S(1)} %collective-permute-done.9.second, ...), custom_call_target="tpu_custom_call" | custom-call | tf_op jit(solution)/shard_map/pallas_call | solution.py:213
  156.3 3.3 %collective-permute-start.10 = (bf16[128,128]{1,0:T(8,128)(2,1)S(1)}, bf16[128,128]{1,0:T(8,128)(2,1)S(1)}, u32[]{:S(2)}, u32[]{:S(2)}) collective-permute-start(bf16[128,128]{1,0:T(8,128)(2,1)S(1)} %get-tuple-element.107), channel_id=1, source_target_pairs={{0,504},{8,16},{16,8},{24,32},{32,24},{40,48},{48,40},{56,64},{64,... | collective-permute-start | bytes 98312 | tf_op jit(solution)/shard_map/ppermute | solution.py:227
  164.3 3.4 %shard_map.122 = (f32[128,128]{1,0:T(8,128)S(1)}, bf16[128,128]{1,0:T(8,128)(2,1)S(1)}, bf16[128,128]{1,0:T(8,128)(2,1)S(1)}) custom-call(f32[128,128]{1,0:T(8,128)S(1)} %get-tuple-element.106.base, bf16[128,128]{1,0:T(8,128)(2,1)S(1)} %collective-permute-done.10.first, bf16[128,128]{1,0:T(8,128)(2,1)S(1)} %collective-permute-done.11.second, ...), custom_call_target="tpu_custom_call" | custom-call | tf_op jit(solution)/shard_map/pallas_call | solution.py:213
  167.7 5.6 %collective-permute-start.12 = (bf16[128,128]{1,0:T(8,128)(2,1)S(1)}, bf16[128,128]{1,0:T(8,128)(2,1)S(1)}, u32[]{:S(2)}, u32[]{:S(2)}) collective-permute-start(bf16[128,128]{1,0:T(8,128)(2,1)S(1)} %get-tuple-element.110), channel_id=1, source_target_pairs={{0,504},{8,16},{16,8},{24,32},{32,24},{40,48},{48,40},{56,64},{64,... | collective-permute-start | bytes 98312 | tf_op jit(solution)/shard_map/ppermute | solution.py:227
  178.3 3.4 %shard_map.123 = (f32[128,128]{1,0:T(8,128)S(1)}, bf16[128,128]{1,0:T(8,128)(2,1)S(1)}, bf16[128,128]{1,0:T(8,128)(2,1)S(1)}) custom-call(f32[128,128]{1,0:T(8,128)S(1)} %get-tuple-element.109.base, bf16[128,128]{1,0:T(8,128)(2,1)S(1)} %collective-permute-done.12.first, bf16[128,128]{1,0:T(8,128)(2,1)S(1)} %collective-permute-done.13.second, ...), custom_call_target="tpu_custom_call" | custom-call | tf_op jit(solution)/shard_map/pallas_call | solution.py:213
  189.7 3.4 %shard_map.124 = (f32[128,128]{1,0:T(8,128)S(1)}, bf16[128,128]{1,0:T(8,128)(2,1)S(1)}, bf16[128,128]{1,0:T(8,128)(2,1)S(1)}) custom-call(f32[128,128]{1,0:T(8,128)S(1)} %get-tuple-element.112.base, bf16[128,128]{1,0:T(8,128)(2,1)S(1)} %collective-permute-done.14.first, bf16[128,128]{1,0:T(8,128)(2,1)S(1)} %collective-permute-done.15.second, ...), custom_call_target="tpu_custom_call" | custom-call | tf_op jit(solution)/shard_map/pallas_call | solution.py:213
  193.1 5.3 %collective-permute-start.16 = (bf16[128,128]{1,0:T(8,128)(2,1)S(1)}, bf16[128,128]{1,0:T(8,128)(2,1)S(1)}, u32[]{:S(2)}, u32[]{:S(2)}) collective-permute-start(bf16[128,128]{1,0:T(8,128)(2,1)S(1)} %get-tuple-element.116), channel_id=1, source_target_pairs={{0,504},{8,16},{16,8},{24,32},{32,24},{40,48},{48,40},{56,64},{64,... | collective-permute-start | bytes 98312 | tf_op jit(solution)/shard_map/ppermute | solution.py:227
  203.1 3.4 %shard_map.125 = (f32[128,128]{1,0:T(8,128)S(1)}, bf16[128,128]{1,0:T(8,128)(2,1)S(1)}, bf16[128,128]{1,0:T(8,128)(2,1)S(1)}) custom-call(f32[128,128]{1,0:T(8,128)S(1)} %get-tuple-element.115.base, bf16[128,128]{1,0:T(8,128)(2,1)S(1)} %collective-permute-done.16.first, bf16[128,128]{1,0:T(8,128)(2,1)S(1)} %collective-permute-done.17.second, ...), custom_call_target="tpu_custom_call" | custom-call | tf_op jit(solution)/shard_map/pallas_call | solution.py:213
  206.5 3.3 %collective-permute-start.18 = (bf16[128,128]{1,0:T(8,128)(2,1)S(1)}, bf16[128,128]{1,0:T(8,128)(2,1)S(1)}, u32[]{:S(2)}, u32[]{:S(2)}) collective-permute-start(bf16[128,128]{1,0:T(8,128)(2,1)S(1)} %get-tuple-element.119), channel_id=1, source_target_pairs={{0,504},{8,16},{16,8},{24,32},{32,24},{40,48},{48,40},{56,64},{64,... | collective-permute-start | bytes 98312 | tf_op jit(solution)/shard_map/ppermute | solution.py:227
  214.5 3.4 %shard_map.126 = (f32[128,128]{1,0:T(8,128)S(1)}, bf16[128,128]{1,0:T(8,128)(2,1)S(1)}, bf16[128,128]{1,0:T(8,128)(2,1)S(1)}) custom-call(f32[128,128]{1,0:T(8,128)S(1)} %get-tuple-element.118.base, bf16[128,128]{1,0:T(8,128)(2,1)S(1)} %collective-permute-done.18.first, bf16[128,128]{1,0:T(8,128)(2,1)S(1)} %collective-permute-done.19.second, ...), custom_call_target="tpu_custom_call" | custom-call | tf_op jit(solution)/shard_map/pallas_call | solution.py:213
  217.9 5.3 %collective-permute-start.20 = (bf16[128,128]{1,0:T(8,128)(2,1)S(1)}, bf16[128,128]{1,0:T(8,128)(2,1)S(1)}, u32[]{:S(2)}, u32[]{:S(2)}) collective-permute-start(bf16[128,128]{1,0:T(8,128)(2,1)S(1)} %get-tuple-element.122), channel_id=1, source_target_pairs={{0,504},{8,16},{16,8},{24,32},{32,24},{40,48},{48,40},{56,64},{64,... | collective-permute-start | bytes 98312 | tf_op jit(solution)/shard_map/ppermute | solution.py:227
  227.8 3.4 %shard_map.127 = (f32[128,128]{1,0:T(8,128)S(1)}, bf16[128,128]{1,0:T(8,128)(2,1)S(1)}, bf16[128,128]{1,0:T(8,128)(2,1)S(1)}) custom-call(f32[128,128]{1,0:T(8,128)S(1)} %get-tuple-element.121.base, bf16[128,128]{1,0:T(8,128)(2,1)S(1)} %collective-permute-done.20.first, bf16[128,128]{1,0:T(8,128)(2,1)S(1)} %collective-permute-done.21.second, ...), custom_call_target="tpu_custom_call" | custom-call | tf_op jit(solution)/shard_map/pallas_call | solution.py:213
  239.3 18.6 %all_to_all.69 = f32[8,16,128]{2,1,0:T(8,128)S(1)} all-to-all(f32[8,16,128]{2,1,0:T(8,128)S(1)} %bitcast.23), channel_id=1, replica_groups=mesh['region'=64,'depth'=8] {'depth'}, dimensions={0} | all-to-all | bytes 131072 | tf_op jit(solution)/shard_map/all_to_all | solution.py:233
  (93 shorter events, 92.0 us)
Async XLA Ops:
  6.5 116.4 %all-gather.2.cloned.1.call-start = ((), (), s32[]{:S(2)}) async-start(), calls=%async_computation.6 | async-start | bytes 18874368 | tf_op jit(solution)/shard_map/all_gather | solution.py:249
  13.2 17.8 %all-to-all-start = ((bf16[8,144,128]{2,1,0:T(8,128)(2,1)}), bf16[8,144,128]{2,1,0:T(8,128)(2,1)}, u32[]{:S(2)}, u32[]{:S(2)}) async-start(bf16[8,144,128]{2,1,0:T(8,128)(2,1)} %bitcast.7), calls=%async_computation | async-start | bytes 589824 | tf_op jit(solution)/shard_map/all_to_all | solution.py:233
  34.7 10.5 %collective-permute-start = (bf16[128,128]{1,0:T(8,128)(2,1)S(1)}, bf16[128,128]{1,0:T(8,128)(2,1)S(1)}, u32[]{:S(2)}, u32[]{:S(2)}) collective-permute-start(bf16[128,128]{1,0:T(8,128)(2,1)S(1)} %get-tuple-element.74), channel_id=1, source_target_pairs={{0,504},{8,16},{16,8},{24,32},{32,24},{40,48},{48,40},{56,64},{64,... | collective-permute-start | bytes 98312 | tf_op jit(solution)/shard_map/ppermute | solution.py:227
  43.2 5.1 %collective-permute-start.1 = (bf16[128,128]{1,0:T(8,128)(2,1)S(1)}, bf16[128,128]{1,0:T(8,128)(2,1)S(1)}, u32[]{:S(2)}, u32[]{:S(2)}) collective-permute-start(bf16[128,128]{1,0:T(8,128)(2,1)S(1)} %get-tuple-element.75), channel_id=1, source_target_pairs={{0,8},{8,0},{16,24},{24,16},{32,40},{40,32},{48,56},{56,48},{64,72... | collective-permute-start | bytes 98312 | tf_op jit(solution)/shard_map/ppermute | solution.py:228
  64.2 8.0 %collective-permute-start.2 = (bf16[128,128]{1,0:T(8,128)(2,1)S(1)}, bf16[128,128]{1,0:T(8,128)(2,1)S(1)}, u32[]{:S(2)}, u32[]{:S(2)}) collective-permute-start(bf16[128,128]{1,0:T(8,128)(2,1)S(1)} %get-tuple-element.82), channel_id=1, source_target_pairs={{0,504},{8,16},{16,8},{24,32},{32,24},{40,48},{48,40},{56,64},{64,... | collective-permute-start | bytes 98312 | tf_op jit(solution)/shard_map/ppermute | solution.py:227
  67.2 5.1 %collective-permute-start.3 = (bf16[128,128]{1,0:T(8,128)(2,1)S(1)}, bf16[128,128]{1,0:T(8,128)(2,1)S(1)}, u32[]{:S(2)}, u32[]{:S(2)}) collective-permute-start(bf16[128,128]{1,0:T(8,128)(2,1)S(1)} %get-tuple-element.83), channel_id=1, source_target_pairs={{0,8},{8,0},{16,24},{24,16},{32,40},{40,32},{48,56},{56,48},{64,72... | collective-permute-start | bytes 98312 | tf_op jit(solution)/shard_map/ppermute | solution.py:228
  88.0 8.0 %collective-permute-start.4 = (bf16[128,128]{1,0:T(8,128)(2,1)S(1)}, bf16[128,128]{1,0:T(8,128)(2,1)S(1)}, u32[]{:S(2)}, u32[]{:S(2)}) collective-permute-start(bf16[128,128]{1,0:T(8,128)(2,1)S(1)} %get-tuple-element.87), channel_id=1, source_target_pairs={{0,504},{8,16},{16,8},{24,32},{32,24},{40,48},{48,40},{56,64},{64,... | collective-permute-start | bytes 98312 | tf_op jit(solution)/shard_map/ppermute | solution.py:227
  93.6 5.1 %collective-permute-start.5 = (bf16[128,128]{1,0:T(8,128)(2,1)S(1)}, bf16[128,128]{1,0:T(8,128)(2,1)S(1)}, u32[]{:S(2)}, u32[]{:S(2)}) collective-permute-start(bf16[128,128]{1,0:T(8,128)(2,1)S(1)} %get-tuple-element.88), channel_id=1, source_target_pairs={{0,8},{8,0},{16,24},{24,16},{32,40},{40,32},{48,56},{56,48},{64,72... | collective-permute-start | bytes 98312 | tf_op jit(solution)/shard_map/ppermute | solution.py:228
  114.4 8.0 %collective-permute-start.6 = (bf16[128,128]{1,0:T(8,128)(2,1)S(1)}, bf16[128,128]{1,0:T(8,128)(2,1)S(1)}, u32[]{:S(2)}, u32[]{:S(2)}) collective-permute-start(bf16[128,128]{1,0:T(8,128)(2,1)S(1)} %get-tuple-element.92), channel_id=1, source_target_pairs={{0,504},{8,16},{16,8},{24,32},{32,24},{40,48},{48,40},{56,64},{64,... | collective-permute-start | bytes 98312 | tf_op jit(solution)/shard_map/ppermute | solution.py:227
  117.4 4.9 %collective-permute-start.7 = (bf16[128,128]{1,0:T(8,128)(2,1)S(1)}, bf16[128,128]{1,0:T(8,128)(2,1)S(1)}, u32[]{:S(2)}, u32[]{:S(2)}) collective-permute-start(bf16[128,128]{1,0:T(8,128)(2,1)S(1)} %get-tuple-element.93), channel_id=1, source_target_pairs={{0,8},{8,0},{16,24},{24,16},{32,40},{40,32},{48,56},{56,48},{64,72... | collective-permute-start | bytes 98312 | tf_op jit(solution)/shard_map/ppermute | solution.py:228
  123.0 10.2 %all-to-all-start.4 = ((f32[8,16,128]{2,1,0:T(8,128)}), f32[8,16,128]{2,1,0:T(8,128)S(1)}, u32[]{:S(2)}, u32[]{:S(2)}) async-start(f32[8,16,128]{2,1,0:T(8,128)} %bitcast.15), calls=%async_computation.4 | async-start | bytes 131072 | tf_op jit(solution)/shard_map/all_to_all | solution.py:233
  142.4 8.2 %collective-permute-start.8 = (bf16[128,128]{1,0:T(8,128)(2,1)S(1)}, bf16[128,128]{1,0:T(8,128)(2,1)S(1)}, u32[]{:S(2)}, u32[]{:S(2)}) collective-permute-start(bf16[128,128]{1,0:T(8,128)(2,1)S(1)} %get-tuple-element.104), channel_id=1, source_target_pairs={{0,504},{8,16},{16,8},{24,32},{32,24},{40,48},{48,40},{56,64},{64,... | collective-permute-start | bytes 98312 | tf_op jit(solution)/shard_map/ppermute | solution.py:227
  148.2 4.7 %collective-permute-start.9 = (bf16[128,128]{1,0:T(8,128)(2,1)S(1)}, bf16[128,128]{1,0:T(8,128)(2,1)S(1)}, u32[]{:S(2)}, u32[]{:S(2)}) collective-permute-start(bf16[128,128]{1,0:T(8,128)(2,1)S(1)} %get-tuple-element.105), channel_id=1, source_target_pairs={{0,8},{8,0},{16,24},{24,16},{32,40},{40,32},{48,56},{56,48},{64,72... | collective-permute-start | bytes 98312 | tf_op jit(solution)/shard_map/ppermute | solution.py:228
  156.3 8.0 %collective-permute-start.10 = (bf16[128,128]{1,0:T(8,128)(2,1)S(1)}, bf16[128,128]{1,0:T(8,128)(2,1)S(1)}, u32[]{:S(2)}, u32[]{:S(2)}) collective-permute-start(bf16[128,128]{1,0:T(8,128)(2,1)S(1)} %get-tuple-element.107), channel_id=1, source_target_pairs={{0,504},{8,16},{16,8},{24,32},{32,24},{40,48},{48,40},{56,64},{64,... | collective-permute-start | bytes 98312 | tf_op jit(solution)/shard_map/ppermute | solution.py:227
  159.7 4.7 %collective-permute-start.11 = (bf16[128,128]{1,0:T(8,128)(2,1)S(1)}, bf16[128,128]{1,0:T(8,128)(2,1)S(1)}, u32[]{:S(2)}, u32[]{:S(2)}) collective-permute-start(bf16[128,128]{1,0:T(8,128)(2,1)S(1)} %get-tuple-element.108), channel_id=1, source_target_pairs={{0,8},{8,0},{16,24},{24,16},{32,40},{40,32},{48,56},{56,48},{64,72... | collective-permute-start | bytes 98312 | tf_op jit(solution)/shard_map/ppermute | solution.py:228
  167.7 8.0 %collective-permute-start.12 = (bf16[128,128]{1,0:T(8,128)(2,1)S(1)}, bf16[128,128]{1,0:T(8,128)(2,1)S(1)}, u32[]{:S(2)}, u32[]{:S(2)}) collective-permute-start(bf16[128,128]{1,0:T(8,128)(2,1)S(1)} %get-tuple-element.110), channel_id=1, source_target_pairs={{0,504},{8,16},{16,8},{24,32},{32,24},{40,48},{48,40},{56,64},{64,... | collective-permute-start | bytes 98312 | tf_op jit(solution)/shard_map/ppermute | solution.py:227
  173.3 5.0 %collective-permute-start.13 = (bf16[128,128]{1,0:T(8,128)(2,1)S(1)}, bf16[128,128]{1,0:T(8,128)(2,1)S(1)}, u32[]{:S(2)}, u32[]{:S(2)}) collective-permute-start(bf16[128,128]{1,0:T(8,128)(2,1)S(1)} %get-tuple-element.111), channel_id=1, source_target_pairs={{0,8},{8,0},{16,24},{24,16},{32,40},{40,32},{48,56},{56,48},{64,72... | collective-permute-start | bytes 98312 | tf_op jit(solution)/shard_map/ppermute | solution.py:228
  181.7 8.0 %collective-permute-start.14 = (bf16[128,128]{1,0:T(8,128)(2,1)S(1)}, bf16[128,128]{1,0:T(8,128)(2,1)S(1)}, u32[]{:S(2)}, u32[]{:S(2)}) collective-permute-start(bf16[128,128]{1,0:T(8,128)(2,1)S(1)} %get-tuple-element.113), channel_id=1, source_target_pairs={{0,504},{8,16},{16,8},{24,32},{32,24},{40,48},{48,40},{56,64},{64,... | collective-permute-start | bytes 98312 | tf_op jit(solution)/shard_map/ppermute | solution.py:227
  184.7 5.0 %collective-permute-start.15 = (bf16[128,128]{1,0:T(8,128)(2,1)S(1)}, bf16[128,128]{1,0:T(8,128)(2,1)S(1)}, u32[]{:S(2)}, u32[]{:S(2)}) collective-permute-start(bf16[128,128]{1,0:T(8,128)(2,1)S(1)} %get-tuple-element.114), channel_id=1, source_target_pairs={{0,8},{8,0},{16,24},{24,16},{32,40},{40,32},{48,56},{56,48},{64,72... | collective-permute-start | bytes 98312 | tf_op jit(solution)/shard_map/ppermute | solution.py:228
  193.1 8.0 %collective-permute-start.16 = (bf16[128,128]{1,0:T(8,128)(2,1)S(1)}, bf16[128,128]{1,0:T(8,128)(2,1)S(1)}, u32[]{:S(2)}, u32[]{:S(2)}) collective-permute-start(bf16[128,128]{1,0:T(8,128)(2,1)S(1)} %get-tuple-element.116), channel_id=1, source_target_pairs={{0,504},{8,16},{16,8},{24,32},{32,24},{40,48},{48,40},{56,64},{64,... | collective-permute-start | bytes 98312 | tf_op jit(solution)/shard_map/ppermute | solution.py:227
  206.5 8.0 %collective-permute-start.18 = (bf16[128,128]{1,0:T(8,128)(2,1)S(1)}, bf16[128,128]{1,0:T(8,128)(2,1)S(1)}, u32[]{:S(2)}, u32[]{:S(2)}) collective-permute-start(bf16[128,128]{1,0:T(8,128)(2,1)S(1)} %get-tuple-element.119), channel_id=1, source_target_pairs={{0,504},{8,16},{16,8},{24,32},{32,24},{40,48},{48,40},{56,64},{64,... | collective-permute-start | bytes 98312 | tf_op jit(solution)/shard_map/ppermute | solution.py:227
  209.8 4.7 %collective-permute-start.19 = (bf16[128,128]{1,0:T(8,128)(2,1)S(1)}, bf16[128,128]{1,0:T(8,128)(2,1)S(1)}, u32[]{:S(2)}, u32[]{:S(2)}) collective-permute-start(bf16[128,128]{1,0:T(8,128)(2,1)S(1)} %get-tuple-element.120), channel_id=1, source_target_pairs={{0,8},{8,0},{16,24},{24,16},{32,40},{40,32},{48,56},{56,48},{64,72... | collective-permute-start | bytes 98312 | tf_op jit(solution)/shard_map/ppermute | solution.py:228
  217.9 8.0 %collective-permute-start.20 = (bf16[128,128]{1,0:T(8,128)(2,1)S(1)}, bf16[128,128]{1,0:T(8,128)(2,1)S(1)}, u32[]{:S(2)}, u32[]{:S(2)}) collective-permute-start(bf16[128,128]{1,0:T(8,128)(2,1)S(1)} %get-tuple-element.122), channel_id=1, source_target_pairs={{0,504},{8,16},{16,8},{24,32},{32,24},{40,48},{48,40},{56,64},{64,... | collective-permute-start | bytes 98312 | tf_op jit(solution)/shard_map/ppermute | solution.py:227
  231.3 8.0 %collective-permute-start.22 = (bf16[128,128]{1,0:T(8,128)(2,1)S(1)}, bf16[128,128]{1,0:T(8,128)(2,1)S(1)}, u32[]{:S(2)}, u32[]{:S(2)}) collective-permute-start(bf16[128,128]{1,0:T(8,128)(2,1)S(1)} %get-tuple-element.125), channel_id=1, source_target_pairs={{0,504},{8,16},{16,8},{24,32},{32,24},{40,48},{48,40},{56,64},{64,... | collective-permute-start | bytes 98312 | tf_op jit(solution)/shard_map/ppermute | solution.py:227
  (21 other events, 96.6 us)
Sparse Core Ops, SparseCore 0:
  9.9 106.7 all-gather.1

commit v5 on v4

--- a/solution.py
+++ b/solution.py
@@ -6,7 +6,7 @@
 from jax.sharding import PartitionSpec as P
 
 STEPS = 12
-LEVEL_STEPS = 4
+LEVEL_STEPS = 3
 GROUPS = 8
 PAIR = 2
 LEVELS = 8
@@ -60,16 +60,17 @@
     write_place(jnp.where(block < 0, -1, wanted), place)
 
 
-def level_products(rows, left, right, place, tiles):
+def level_products(rows, left, right, place, tiles, first):
     rows = rows.astype(BF)
     x_left = dot(left[...], rows).astype(BF)
     x_right = dot(right[...], rows).astype(BF)
     parts = []
-    for at in range(0, tiles.shape[0], 4):
+    for at in range(0, left.shape[0] // TRACERS, 4):
         part = slice(at * TRACERS, (at + 4) * TRACERS)
+        tile = first + at
         lhs = jnp.concatenate([x_left[part], x_right[part]], axis=1)
-        upper = jnp.concatenate([tiles[at], tiles[at + 2]], axis=1)
-        lower = jnp.concatenate([tiles[at + 1], tiles[at + 3]], axis=1)
+        upper = jnp.concatenate([tiles[tile], tiles[tile + 2]], axis=1)
+        lower = jnp.concatenate([tiles[tile + 1], tiles[tile + 3]], axis=1)
         out = dot(lhs, jnp.concatenate([upper, lower], axis=0))
         parts += [out[: 2 * TRACERS, :CELLS], out[2 * TRACERS :, CELLS:]]
     return placed(place, jnp.concatenate(parts, axis=0))
@@ -103,7 +104,7 @@
             adjoint[row : row + PAIR] = seed[at, group * PAIR : group * PAIR + PAIR]
     value = wet[...] * adjoint[...]
     adjoint[...] = value
-    sums = level_products(value, left, right, place, tiles).astype(BF)
+    sums = level_products(value, left, right, place, tiles, l_slots).astype(BF)
     for peer in range(GROUPS):
         at = peer * (STATE + LISTS)
         partial[at : at + STATE] = sums[peer * STATE : (peer + 1) * STATE]
@@ -117,7 +118,7 @@
 def vertical_kernel(base, first, second, wet, left, right, place, tiles, adjoint, partial):
     value = wet[...] * (base[...] + first[...].astype(F32) + second[...].astype(F32))
     adjoint[...] = value
-    partial[...] = level_products(value, left, right, place, tiles).astype(BF)
+    partial[...] = level_products(value, left, right, place, tiles, tiles.shape[0] - left.shape[0] // TRACERS).astype(BF)
 
 
 def lateral_kernel(adjoint, returned, wet, left, right, place, tiles, base, to_first, to_second):
@@ -126,10 +127,17 @@
     for peer in range(GROUPS):
         value = value + returned[stride * peer : stride * peer + STATE].astype(F32)
     value = wet[...] * value
-    partial = level_products(value, left, right, place, tiles).astype(BF)
+    partial = level_products(value, left, right, place, tiles, 0).astype(BF)
     to_first[...] = partial[:STATE]
     to_second[...] = partial[2 * STATE :]
     base[...] = value + partial[STATE : 2 * STATE].astype(F32)
+
+
+def depth_at(place):
+    mine = lax.axis_index("depth")
+    chip, core = mine // 2, mine % 2
+    offset = (0, 3, 1, 2)[place % 4]
+    return (chip + offset) % (GROUPS // 2) * 2 + (core if place < 4 else 1 - core)
 
 
 def tracer_lists_kernel(returned, lengths, wet, v_left, v_right, v_place, l_left, l_right, l_place, lines_l, lines_v):
@@ -137,11 +145,12 @@
     wet[...] = jnp.where(level < lengths[...], 1.0, 0.0)
     l_rows, v_rows = l_left.shape[0] // GROUPS, v_left.shape[0] // GROUPS
     stride = STATE + LISTS
-    for depth in range(GROUPS):
-        codes = returned[depth * stride + STATE : (depth + 1) * stride][:8]
+    for at in range(GROUPS):
+        depth = depth_at(at)
+        codes = returned[pl.ds(pl.multiple_of(depth * stride + STATE, LISTS), LISTS)][:8]
         for rows, row_of, left, right in ((l_rows, 0, l_left, l_right), (v_rows, 2, v_left, v_right)):
             columns, lines = spread(codes, rows // PAIR, PAIR)
-            part = slice(depth * rows, (depth + 1) * rows)
+            part = slice(at * rows, (at + 1) * rows)
             wanted = (depth * LEVELS + columns[:, row_of : row_of + 1]) * PAIR + iota((rows, 1), 0) % PAIR
             write_picks(wanted, PAIR, left, right, part)
             block = lines[row_of + 1 : row_of + 2]
@@ -179,7 +188,8 @@
     return placed(place, product[:count])
 
 
-def tracer_step(value, wet, v_left, v_right, v_place, l_left, l_right, l_place, tiles, base, to_first, to_second, *scratch):
+def tracer_step(value, wet, v_left, v_right, v_place, l_left, l_right, l_place, tiles, *refs):
+    (base, to_first, to_second), scratch = refs[:3], refs[4:]
     l_slots, v_slots = l_left.shape[0] // (GROUPS * PAIR), v_left.shape[0] // (GROUPS * PAIR)
     value = wet[...] * value
     value = wet[...] * (value + tracer_products(value, v_left, v_right, v_place, tiles, l_slots, v_slots, scratch))
@@ -190,7 +200,17 @@
 
 
 def tracer_first_kernel(value, *refs):
-    tracer_step(value[...], *refs)
+    constants, parts, (base, to_first, to_second, tiles) = refs[:7], refs[7:13], refs[13:17]
+    *scratch, done = refs[17:]
+    copies, at = [], 0
+    for index, part in enumerate(parts):
+        count = part.shape[0]
+        copies.append(pltpu.make_async_copy(part, tiles.at[pl.ds(at, count)], done.at[index]))
+        copies[-1].start()
+        at += count
+    for copy in copies:
+        copy.wait()
+    tracer_step(value[...], *constants, tiles, base, to_first, to_second, tiles, *scratch)
 
 
 def tracer_kernel(base, first, second, *refs):
@@ -209,14 +229,20 @@
             out[at, group * PAIR : group * PAIR + PAIR] = rows[row : row + PAIR]
 
 
-def call(body, outs, *args, scratch=()):
+def call(body, outs, *args, scratch=(), mebibytes=12, parts=0, kept=None):
+    aliases = {} if kept is None else {kept: len(outs) - 1}
+    spaces = [pltpu.VMEM] * (len(args) - parts) + [pl.ANY] * parts
+    shapes = [jax.ShapeDtypeStruct(shape, kind) for shape, kind in outs]
+    if parts or kept is not None:
+        shapes[-1] = pltpu.VMEM(*outs[-1])
     return pl.pallas_call(
         body,
-        out_shape=[jax.ShapeDtypeStruct(shape, kind) for shape, kind in outs],
-        in_specs=[pl.BlockSpec(memory_space=pltpu.VMEM) for _ in args],
+        out_shape=shapes,
+        input_output_aliases=aliases,
+        in_specs=[pl.BlockSpec(memory_space=space) for space in spaces],
         out_specs=[pl.BlockSpec(memory_space=pltpu.VMEM) for _ in outs],
         scratch_shapes=scratch,
-        compiler_params=pltpu.CompilerParams(vmem_limit_bytes=24 * 1024 * 1024),
+        compiler_params=pltpu.CompilerParams(vmem_limit_bytes=mebibytes * 1024 * 1024),
     )(*args)
 
 
@@ -227,6 +253,27 @@
     from_first = lax.ppermute(to_first, "region", first)
     from_second = lax.ppermute(to_second, "region", second)
     return from_first, from_second
+
+
+def join_kernel(*refs):
+    out, at = refs[-1], 0
+    for part in refs[:-1]:
+        out[at : at + part.shape[0]] = part[...]
+        at += part.shape[0]
+
+
+def joined(*parts):
+    count = sum(part.shape[0] for part in parts)
+    return call(join_kernel, [((count, CELLS, CELLS), BF)], *parts, mebibytes=20)[0]
+
+
+def from_chip(value, by):
+    depths = lax.axis_size("depth")
+    return lax.ppermute(value, "depth", [(i, (i + 2 * by) % depths) for i in range(depths)])
+
+
+def from_core(value):
+    return lax.ppermute(value, "depth", [(i, i ^ 1) for i in range(lax.axis_size("depth"))])
 
 
 def to_depth(value):
@@ -246,9 +293,9 @@
     vertical_peers,
     vertical_targets,
 ):
-    gathered = lax.all_gather(
-        jnp.concatenate([lateral_tiles, vertical_tiles], axis=0), "depth", axis=0, tiled=True
-    )
+    own = joined(lateral_tiles, vertical_tiles)
+    half = own.shape[0] // 2
+    before, after = from_chip(own, 1), from_chip(own, -1)
     l_slots, v_slots = lateral_tiles.shape[0], vertical_tiles.shape[0]
     lengths = column_lengths.reshape(1, CELLS)
     state = ((STATE, CELLS), F32)
@@ -271,26 +318,30 @@
         vertical_rows.reshape(1, v_slots),
         vertical_peers.reshape(1, v_slots),
         vertical_targets.reshape(1, v_slots),
-        vertical_tiles,
+        own,
     )
     lateral = call(lateral_lists_kernel, matrices(l_slots, 3), codes)
     returned = first_returned = to_depth(partial)
     for step in range(LEVEL_STEPS):
+        if step == LEVEL_STEPS - 1:
+            returned, opposite = lax.optimization_barrier((returned, opposite))
+            opposite = joined(*opposite)
+            swapped_opposite = from_core(opposite)
         base, to_first, to_second = call(
-            lateral_kernel, [state, sent, sent], adjoint, returned, wet, *lateral, lateral_tiles
+            lateral_kernel, [state, sent, sent], adjoint, returned, wet, *lateral, own
         )
         received = swapped(to_first, to_second)
+        if step == LEVEL_STEPS - 2:
+            received, before, after = lax.optimization_barrier((received, before, after))
+            opposite = from_chip(before[:half], 1), from_chip(after[half:], -1)
+            three = joined(own, before, after)
+            swapped_three = from_core(three)
         if step < LEVEL_STEPS - 1:
             adjoint, partial = call(
-                vertical_kernel,
-                [state, ((GROUPS * STATE, CELLS), BF)],
-                base,
-                *received,
-                wet,
-                *vertical,
-                vertical_tiles,
+                vertical_kernel, [state, ((GROUPS * STATE, CELLS), BF)], base, *received, wet, *vertical, own
             )
             returned = to_depth(partial)
+    parts = (own, before, after, opposite, swapped_three, swapped_opposite)
 
     def tracer_matrices(slots, blocks):
         rows = slots * PAIR
@@ -306,14 +357,33 @@
     rows = GROUPS * l_slots * PAIR
     scratch = [pltpu.VMEM((rows, CELLS), kind) for kind in (BF, BF, F32)]
     (value,) = call(sum_kernel, [state], base, *received)
-    value, gathered = lax.optimization_barrier((value, gathered))
     value = to_depth(value)
+    held = ((GROUPS * own.shape[0], CELLS, CELLS), BF)
+    outs = [state, sent, sent, held]
     for step in range(LEVEL_STEPS, STEPS):
         if step == LEVEL_STEPS:
-            arrived, body = (value,), tracer_first_kernel
+            base, to_first, to_second, tiles = call(
+                tracer_first_kernel,
+                outs,
+                value,
+                *constants,
+                *parts,
+                scratch=scratch + [pltpu.SemaphoreType.DMA((len(parts),))],
+                mebibytes=24,
+                parts=len(parts),
+            )
         else:
-            arrived, body = (base, *received), tracer_kernel
-        base, to_first, to_second = call(body, [state, sent, sent], *arrived, *constants, gathered, scratch=scratch)
+            base, to_first, to_second, tiles = call(
+                tracer_kernel,
+                outs,
+                base,
+                *received,
+                *constants,
+                tiles,
+                scratch=scratch,
+                mebibytes=24,
+                kept=3 + len(constants),
+            )
         received = swapped(to_first, to_second)
     (value,) = call(sum_kernel, [state], base, *received)
     (adjoint,) = call(close_kernel, [((LEVELS, TRACERS, CELLS), F32)], to_depth(value), wet)

time: 267 us -> 314 us (1.18)
  waiting for transfers between devices: 43.4 us -> 69.2 us
  starting transfers between devices: 94.7 us -> 116 us
  between operations: 14.6 us -> 1.11 us
  Pallas kernels: 39.3 us -> 51.6 us
  local copies, waits for them, and re-layouts: 9.1 us -> 16 us
    all_to_all x2, waiting for transfers between devices: 8.95 us -> 35.7 us  [to_depth(): lax.all_to_all(value, 'depth', split_axis=0, concat_axis=0, tiled=True)]
    ppermute x0 -> x6, starting transfers between devices: none -> 19.4 us  [the longest x4 12.4 us: from_chip(): lax.ppermute(value, 'depth', [(i, (i + 2 * by) % depths) for i in range(d...]
    pallas_call x21 -> x23, Pallas kernels: 39.3 us -> 51.6 us  [call(): pl.pallas_call(body, out_shape=shapes, input_output_aliases=aliases, in_s...]
    ppermute x12, starting transfers between devices: 55.1 us -> 59.6 us  [swapped(): from_first = lax.ppermute(to_first, 'region', first)]
    unnamed x36 -> x40, local copies, waits for them, and re-layouts: 9.1 us -> 13.3 us
    all_to_all x4 -> x3, blocking collectives: 61.1 us -> 58.6 us  [to_depth(): lax.all_to_all(value, 'depth', split_axis=0, concat_axis=0, tiled=True)]
  transfers between devices with their start and end apart: 27 -> 32, of which waited for: 20 -> 19; matrix products, arithmetic and copies ran while one was open for 0% -> 1% of each run, Pallas kernels for 4% -> 3%
where the time goes in v5:
time: 314 us; the launch traced here: 313 us
  starting transfers between devices  116 us (37%)
  waiting for transfers between devices  69.2 us (22%)
  blocking collectives  58.6 us (19%)
  Pallas kernels  51.6 us (16%)
  local copies, waits for them, and re-layouts  16 us (5%)
    ppermute x12, starting transfers between devices, swapped(): from_first = lax.ppermute(to_first, 'region', first)  59.6 us
    all_to_all x3, blocking collectives, to_depth(): lax.all_to_all(value, 'depth', split_axis=0, concat_axis=0, tiled=True)  58.6 us
    pallas_call x23, Pallas kernels, call(): pl.pallas_call(body, out_shape=shapes, input_output_aliases=aliases, in_s...  51.6 us
    all_to_all x2, waiting for transfers between devices, to_depth(): lax.all_to_all(value, 'depth', split_axis=0, concat_axis=0, tiled=True)  35.7 us
    ppermute x12, starting transfers between devices, swapped(): from_second = lax.ppermute(to_second, 'region', second)  23.4 us
    ppermute x12, waiting for transfers between devices, swapped(): from_first = lax.ppermute(to_first, 'region', first)  20 us
    all_to_all x2, starting transfers between devices, to_depth(): lax.all_to_all(value, 'depth', split_axis=0, concat_axis=0, tiled=True)  13.6 us
    ppermute x12, waiting for transfers between devices, swapped(): from_second = lax.ppermute(to_second, 'region', second)  13.5 us
  transfers between devices with their start and end apart: 32, of which 19 were waited for; matrix products, arithmetic and copies ran while one was open for 1% of the time, Pallas kernels for 3%

profile of v5, /device:TPU:1, one launch (start us, length us, event | category | flops | bytes accessed | tf_op | source)
XLA Modules:
  0.0 312.6 jit_solution(16621630616497753251)
XLA Ops:
  2.6 5.2 %collective-permute-start.5 = (bf16[64,128,128]{2,1,0:T(8,128)(2,1)S(1)}, bf16[64,128,128]{2,1,0:T(8,128)(2,1)}, u32[]{:S(2)}, u32[]{:S(2)}) collective-permute-start(bf16[64,128,128]{2,1,0:T(8,128)(2,1)S(1)} %shard_map.109.tiles.refs_0_.refs_7_), channel_id=1, source_target_pairs={{0,6},{1,7},{2,0},{3,1},{4,2},{5,3},{6,4},{7,5},{8,14},{9,15},{10,... | collective-permute-start | bytes 6291464 | tf_op jit(solution)/shard_map/ppermute | solution.py:272
  18.4 8.9 %all-to-all-start = ((bf16[8,144,128]{2,1,0:T(8,128)(2,1)}), bf16[8,144,128]{2,1,0:T(8,128)(2,1)S(1)}, u32[]{:S(2)}, u32[]{:S(2)}) async-start(bf16[8,144,128]{2,1,0:T(8,128)(2,1)} %bitcast.7), calls=%async_computation | async-start | bytes 589824 | tf_op jit(solution)/shard_map/all_to_all | solution.py:280
  28.6 32.5 %all-to-all-done = bf16[8,144,128]{2,1,0:T(8,128)(2,1)S(1)} async-done(((bf16[8,144,128]{2,1,0:T(8,128)(2,1)}), bf16[8,144,128]{2,1,0:T(8,128)(2,1)S(1)}, u32[]{:S(2)}, u32[]{:S(2)}) %all-to-all-start) | async-done | bytes 294944 | tf_op jit(solution)/shard_map/all_to_all | solution.py:280
  63.0 13.6 %collective-permute-start = (bf16[128,128]{1,0:T(8,128)(2,1)S(1)}, bf16[128,128]{1,0:T(8,128)(2,1)S(1)}, u32[]{:S(2)}, u32[]{:S(2)}) collective-permute-start(bf16[128,128]{1,0:T(8,128)(2,1)S(1)} %get-tuple-element.85), channel_id=1, source_target_pairs={{0,504},{8,16},{16,8},{24,32},{32,24},{40,48},{48,40},{56,64},{64,... | collective-permute-start | bytes 98312 | tf_op jit(solution)/shard_map/ppermute | solution.py:253
  83.0 11.4 %all_to_all.56 = bf16[8,128,128]{2,1,0:T(8,128)(2,1)S(1)} all-to-all(bf16[8,128,128]{2,1,0:T(8,128)(2,1)S(1)} %bitcast.25), channel_id=1, replica_groups=mesh['region'=64,'depth'=8] {'depth'}, dimensions={0} | all-to-all | bytes 524288 | tf_op jit(solution)/shard_map/all_to_all | solution.py:280
  104.2 5.3 %shard_map.120 = bf16[192,128,128]{2,1,0:T(8,128)(2,1)} custom-call(bf16[64,128,128]{2,1,0:T(8,128)(2,1)S(1)} %shard_map.109.tiles.refs_0_.refs_7_, bf16[64,128,128]{2,1,0:T(8,128)(2,1)} %collective-permute-done.4.refs_1_.refs_8_, bf16[64,128,128]{2,1,0:T(8,128)(2,1)} %collective-permute-done.5.refs_2_.refs_9_), custom_call_target="tpu_custom_call" | custom-call | tf_op jit(solution)/shard_map/pallas_call | solution.py:238
  109.6 4.1 %collective-permute-start.10 = (bf16[192,128,128]{2,1,0:T(8,128)(2,1)}, bf16[192,128,128]{2,1,0:T(8,128)(2,1)}, u32[]{:S(2)}, u32[]{:S(2)}) collective-permute-start(bf16[192,128,128]{2,1,0:T(8,128)(2,1)} %shard_map.120), channel_id=1, source_target_pairs={{0,1},{1,0},{2,3},{3,2},{4,5},{5,4},{6,7},{7,6},{8,9},{9,8},{10,11... | collective-permute-start | bytes 18874376 | tf_op jit(solution)/shard_map/ppermute | solution.py:276
  122.4 27.2 %all_to_all.57 = bf16[8,128,128]{2,1,0:T(8,128)(2,1)S(1)} all-to-all(bf16[8,128,128]{2,1,0:T(8,128)(2,1)S(1)} %bitcast.24), channel_id=1, replica_groups=mesh['region'=64,'depth'=8] {'depth'}, dimensions={0} | all-to-all | bytes 524288 | tf_op jit(solution)/shard_map/all_to_all | solution.py:280
  154.9 5.6 %collective-permute-start.8 = (bf16[128,128]{1,0:T(8,128)(2,1)S(1)}, bf16[128,128]{1,0:T(8,128)(2,1)S(1)}, u32[]{:S(2)}, u32[]{:S(2)}) collective-permute-start(bf16[128,128]{1,0:T(8,128)(2,1)S(1)} %get-tuple-element.103), channel_id=1, source_target_pairs={{0,504},{8,16},{16,8},{24,32},{32,24},{40,48},{48,40},{56,64},{64,... | collective-permute-start | bytes 98312 | tf_op jit(solution)/shard_map/ppermute | solution.py:253
  165.8 4.7 %all-to-all-start.3 = ((f32[8,16,128]{2,1,0:T(8,128)}), f32[8,16,128]{2,1,0:T(8,128)S(1)}, u32[]{:S(2)}, u32[]{:S(2)}) async-start(f32[8,16,128]{2,1,0:T(8,128)} %bitcast.13), calls=%async_computation.3 | async-start | bytes 131072 | tf_op jit(solution)/shard_map/all_to_all | solution.py:280
  175.3 8.9 %shard_map.121 = (f32[128,128]{1,0:T(8,128)S(1)}, bf16[128,128]{1,0:T(8,128)(2,1)S(1)}, bf16[128,128]{1,0:T(8,128)(2,1)S(1)}, bf16[512,128,128]{2,1,0:T(8,128)(2,1)S(1)}) custom-call(f32[128,128]{1,0:T(8,128)S(1)} %bitcast.21, f32[128,128]{1,0:T(8,128)S(1)} %get-tuple-element.105.refs_0_, bf16[256,128]{1,0:T(8,128)(2,1)S(1)} %get-tuple-element.106.refs_1_, ...), custom_call_target="tpu_custom_call" | custom-call | tf_op jit(solution)/shard_map/pallas_call | solution.py:238
  192.2 3.4 %shard_map.122 = (f32[128,128]{1,0:T(8,128)S(1)}, bf16[128,128]{1,0:T(8,128)(2,1)S(1)}, bf16[128,128]{1,0:T(8,128)(2,1)S(1)}, bf16[512,128,128]{2,1,0:T(8,128)(2,1)S(1)}) custom-call(f32[128,128]{1,0:T(8,128)S(1)} %get-tuple-element.114.base, bf16[128,128]{1,0:T(8,128)(2,1)S(1)} %collective-permute-done.12.first, ...), custom_call_target="tpu_custom_call", output_to_operand_aliasing={{3}: (10, {})} | custom-call | tf_op jit(solution)/shard_map/pallas_call | solution.py:238
  195.6 5.3 %collective-permute-start.14 = (bf16[128,128]{1,0:T(8,128)(2,1)S(1)}, bf16[128,128]{1,0:T(8,128)(2,1)S(1)}, u32[]{:S(2)}, u32[]{:S(2)}) collective-permute-start(bf16[128,128]{1,0:T(8,128)(2,1)S(1)} %get-tuple-element.119), channel_id=1, source_target_pairs={{0,504},{8,16},{16,8},{24,32},{32,24},{40,48},{48,40},{56,64},{64,... | collective-permute-start | bytes 98312 | tf_op jit(solution)/shard_map/ppermute | solution.py:253
  205.9 3.4 %shard_map.123 = (f32[128,128]{1,0:T(8,128)S(1)}, bf16[128,128]{1,0:T(8,128)(2,1)S(1)}, bf16[128,128]{1,0:T(8,128)(2,1)S(1)}, bf16[512,128,128]{2,1,0:T(8,128)(2,1)S(1)}) custom-call(f32[128,128]{1,0:T(8,128)S(1)} %get-tuple-element.118.base, bf16[128,128]{1,0:T(8,128)(2,1)S(1)} %collective-permute-done.14.first, ...), custom_call_target="tpu_custom_call", output_to_operand_aliasing={{3}: (10, {})} | custom-call | tf_op jit(solution)/shard_map/pallas_call | solution.py:238
  217.3 3.4 %shard_map.124 = (f32[128,128]{1,0:T(8,128)S(1)}, bf16[128,128]{1,0:T(8,128)(2,1)S(1)}, bf16[128,128]{1,0:T(8,128)(2,1)S(1)}, bf16[512,128,128]{2,1,0:T(8,128)(2,1)S(1)}) custom-call(f32[128,128]{1,0:T(8,128)S(1)} %get-tuple-element.122.base, bf16[128,128]{1,0:T(8,128)(2,1)S(1)} %collective-permute-done.16.first, ...), custom_call_target="tpu_custom_call", output_to_operand_aliasing={{3}: (10, {})} | custom-call | tf_op jit(solution)/shard_map/pallas_call | solution.py:238
  220.7 5.6 %collective-permute-start.18 = (bf16[128,128]{1,0:T(8,128)(2,1)S(1)}, bf16[128,128]{1,0:T(8,128)(2,1)S(1)}, u32[]{:S(2)}, u32[]{:S(2)}) collective-permute-start(bf16[128,128]{1,0:T(8,128)(2,1)S(1)} %get-tuple-element.127), channel_id=1, source_target_pairs={{0,504},{8,16},{16,8},{24,32},{32,24},{40,48},{48,40},{56,64},{64,... | collective-permute-start | bytes 98312 | tf_op jit(solution)/shard_map/ppermute | solution.py:253
  231.0 3.4 %shard_map.125 = (f32[128,128]{1,0:T(8,128)S(1)}, bf16[128,128]{1,0:T(8,128)(2,1)S(1)}, bf16[128,128]{1,0:T(8,128)(2,1)S(1)}, bf16[512,128,128]{2,1,0:T(8,128)(2,1)S(1)}) custom-call(f32[128,128]{1,0:T(8,128)S(1)} %get-tuple-element.126.base, bf16[128,128]{1,0:T(8,128)(2,1)S(1)} %collective-permute-done.18.first, ...), custom_call_target="tpu_custom_call", output_to_operand_aliasing={{3}: (10, {})} | custom-call | tf_op jit(solution)/shard_map/pallas_call | solution.py:238
  242.4 3.4 %shard_map.126 = (f32[128,128]{1,0:T(8,128)S(1)}, bf16[128,128]{1,0:T(8,128)(2,1)S(1)}, bf16[128,128]{1,0:T(8,128)(2,1)S(1)}, bf16[512,128,128]{2,1,0:T(8,128)(2,1)S(1)}) custom-call(f32[128,128]{1,0:T(8,128)S(1)} %get-tuple-element.130.base, bf16[128,128]{1,0:T(8,128)(2,1)S(1)} %collective-permute-done.20.first, ...), custom_call_target="tpu_custom_call", output_to_operand_aliasing={{3}: (10, {})} | custom-call | tf_op jit(solution)/shard_map/pallas_call | solution.py:238
  245.8 5.3 %collective-permute-start.22 = (bf16[128,128]{1,0:T(8,128)(2,1)S(1)}, bf16[128,128]{1,0:T(8,128)(2,1)S(1)}, u32[]{:S(2)}, u32[]{:S(2)}) collective-permute-start(bf16[128,128]{1,0:T(8,128)(2,1)S(1)} %get-tuple-element.135), channel_id=1, source_target_pairs={{0,504},{8,16},{16,8},{24,32},{32,24},{40,48},{48,40},{56,64},{64,... | collective-permute-start | bytes 98312 | tf_op jit(solution)/shard_map/ppermute | solution.py:253
  255.7 3.4 %shard_map.127 = (f32[128,128]{1,0:T(8,128)S(1)}, bf16[128,128]{1,0:T(8,128)(2,1)S(1)}, bf16[128,128]{1,0:T(8,128)(2,1)S(1)}, bf16[512,128,128]{2,1,0:T(8,128)(2,1)S(1)}) custom-call(f32[128,128]{1,0:T(8,128)S(1)} %get-tuple-element.134.base, bf16[128,128]{1,0:T(8,128)(2,1)S(1)} %collective-permute-done.22.first, ...), custom_call_target="tpu_custom_call", output_to_operand_aliasing={{3}: (10, {})} | custom-call | tf_op jit(solution)/shard_map/pallas_call | solution.py:238
  267.2 3.4 %shard_map.128 = (f32[128,128]{1,0:T(8,128)S(1)}, bf16[128,128]{1,0:T(8,128)(2,1)S(1)}, bf16[128,128]{1,0:T(8,128)(2,1)S(1)}, bf16[512,128,128]{2,1,0:T(8,128)(2,1)S(1)}) custom-call(f32[128,128]{1,0:T(8,128)S(1)} %get-tuple-element.138.base, bf16[128,128]{1,0:T(8,128)(2,1)S(1)} %collective-permute-done.24.first, ...), custom_call_target="tpu_custom_call", output_to_operand_aliasing={{3}: (10, {})} | custom-call | tf_op jit(solution)/shard_map/pallas_call | solution.py:238
  270.6 5.3 %collective-permute-start.26 = (bf16[128,128]{1,0:T(8,128)(2,1)S(1)}, bf16[128,128]{1,0:T(8,128)(2,1)S(1)}, u32[]{:S(2)}, u32[]{:S(2)}) collective-permute-start(bf16[128,128]{1,0:T(8,128)(2,1)S(1)} %get-tuple-element.143), channel_id=1, source_target_pairs={{0,504},{8,16},{16,8},{24,32},{32,24},{40,48},{48,40},{56,64},{64,... | collective-permute-start | bytes 98312 | tf_op jit(solution)/shard_map/ppermute | solution.py:253
  280.5 3.4 %shard_map.129 = (f32[128,128]{1,0:T(8,128)S(1)}, bf16[128,128]{1,0:T(8,128)(2,1)S(1)}, bf16[128,128]{1,0:T(8,128)(2,1)S(1)}, bf16[512,128,128]{2,1,0:T(8,128)(2,1)S(1)}) custom-call(f32[128,128]{1,0:T(8,128)S(1)} %get-tuple-element.142.base, bf16[128,128]{1,0:T(8,128)(2,1)S(1)} %collective-permute-done.26.first, ...), custom_call_target="tpu_custom_call", output_to_operand_aliasing={{3}: (10, {})} | custom-call | tf_op jit(solution)/shard_map/pallas_call | solution.py:238
  292.0 20.0 %all_to_all.58 = f32[8,16,128]{2,1,0:T(8,128)S(1)} all-to-all(f32[8,16,128]{2,1,0:T(8,128)S(1)} %bitcast.22), channel_id=1, replica_groups=mesh['region'=64,'depth'=8] {'depth'}, dimensions={0} | all-to-all | bytes 131072 | tf_op jit(solution)/shard_map/all_to_all | solution.py:280
  (108 shorter events, 115.4 us)
Async XLA Ops:
  2.6 101.6 %collective-permute-start.5 = (bf16[64,128,128]{2,1,0:T(8,128)(2,1)S(1)}, bf16[64,128,128]{2,1,0:T(8,128)(2,1)}, u32[]{:S(2)}, u32[]{:S(2)}) collective-permute-start(bf16[64,128,128]{2,1,0:T(8,128)(2,1)S(1)} %shard_map.109.tiles.refs_0_.refs_7_), channel_id=1, source_target_pairs={{0,6},{1,7},{2,0},{3,1},{4,2},{5,3},{6,4},{7,5},{8,14},{9,15},{10,... | collective-permute-start | bytes 6291464 | tf_op jit(solution)/shard_map/ppermute | solution.py:272
  7.8 96.4 %collective-permute-start.4 = (bf16[64,128,128]{2,1,0:T(8,128)(2,1)S(1)}, bf16[64,128,128]{2,1,0:T(8,128)(2,1)}, u32[]{:S(2)}, u32[]{:S(2)}) collective-permute-start(bf16[64,128,128]{2,1,0:T(8,128)(2,1)S(1)} %shard_map.109.tiles.refs_0_.refs_7_), channel_id=1, source_target_pairs={{0,2},{1,3},{2,4},{3,5},{4,6},{5,7},{6,0},{7,1},{8,10},{9,11},{10,... | collective-permute-start | bytes 6291464 | tf_op jit(solution)/shard_map/ppermute | solution.py:272
  18.4 42.6 %all-to-all-start = ((bf16[8,144,128]{2,1,0:T(8,128)(2,1)}), bf16[8,144,128]{2,1,0:T(8,128)(2,1)S(1)}, u32[]{:S(2)}, u32[]{:S(2)}) async-start(bf16[8,144,128]{2,1,0:T(8,128)(2,1)} %bitcast.7), calls=%async_computation | async-start | bytes 589824 | tf_op jit(solution)/shard_map/all_to_all | solution.py:280
  63.0 15.5 %collective-permute-start = (bf16[128,128]{1,0:T(8,128)(2,1)S(1)}, bf16[128,128]{1,0:T(8,128)(2,1)S(1)}, u32[]{:S(2)}, u32[]{:S(2)}) collective-permute-start(bf16[128,128]{1,0:T(8,128)(2,1)S(1)} %get-tuple-element.85), channel_id=1, source_target_pairs={{0,504},{8,16},{16,8},{24,32},{32,24},{40,48},{48,40},{56,64},{64,... | collective-permute-start | bytes 98312 | tf_op jit(solution)/shard_map/ppermute | solution.py:253
  96.2 8.0 %collective-permute-start.2 = (bf16[128,128]{1,0:T(8,128)(2,1)S(1)}, bf16[128,128]{1,0:T(8,128)(2,1)S(1)}, u32[]{:S(2)}, u32[]{:S(2)}) collective-permute-start(bf16[128,128]{1,0:T(8,128)(2,1)S(1)} %get-tuple-element.93), channel_id=1, source_target_pairs={{0,504},{8,16},{16,8},{24,32},{32,24},{40,48},{48,40},{56,64},{64,... | collective-permute-start | bytes 98312 | tf_op jit(solution)/shard_map/ppermute | solution.py:253
  99.3 4.9 %collective-permute-start.3 = (bf16[128,128]{1,0:T(8,128)(2,1)S(1)}, bf16[128,128]{1,0:T(8,128)(2,1)S(1)}, u32[]{:S(2)}, u32[]{:S(2)}) collective-permute-start(bf16[128,128]{1,0:T(8,128)(2,1)S(1)} %get-tuple-element.94), channel_id=1, source_target_pairs={{0,8},{8,0},{16,24},{24,16},{32,40},{40,32},{48,56},{56,48},{64,72... | collective-permute-start | bytes 98312 | tf_op jit(solution)/shard_map/ppermute | solution.py:254
  109.6 65.8 %collective-permute-start.10 = (bf16[192,128,128]{2,1,0:T(8,128)(2,1)}, bf16[192,128,128]{2,1,0:T(8,128)(2,1)}, u32[]{:S(2)}, u32[]{:S(2)}) collective-permute-start(bf16[192,128,128]{2,1,0:T(8,128)(2,1)} %shard_map.120), channel_id=1, source_target_pairs={{0,1},{1,0},{2,3},{3,2},{4,5},{5,4},{6,7},{7,6},{8,9},{9,8},{10,11... | collective-permute-start | bytes 18874376 | tf_op jit(solution)/shard_map/ppermute | solution.py:276
  116.3 33.2 %collective-permute-start.7 = (bf16[32,128,128]{2,1,0:T(8,128)(2,1)S(1)}, bf16[32,128,128]{2,1,0:T(8,128)(2,1)S(1)}, u32[]{:S(2)}, u32[]{:S(2)}) collective-permute-start(bf16[32,128,128]{2,1,0:T(8,128)(2,1)S(1)} %slice.7), channel_id=1, source_target_pairs={{0,6},{1,7},{2,0},{3,1},{4,2},{5,3},{6,4},{7,5},{8,14},{9,15},{10,... | collective-permute-start | bytes 3145736 | tf_op jit(solution)/shard_map/ppermute | solution.py:272
  119.1 30.5 %collective-permute-start.6 = (bf16[32,128,128]{2,1,0:T(8,128)(2,1)S(1)}, bf16[32,128,128]{2,1,0:T(8,128)(2,1)S(1)}, u32[]{:S(2)}, u32[]{:S(2)}) collective-permute-start(bf16[32,128,128]{2,1,0:T(8,128)(2,1)S(1)} %slice.6), channel_id=1, source_target_pairs={{0,2},{1,3},{2,4},{3,5},{4,6},{5,7},{6,0},{7,1},{8,10},{9,11},{10,... | collective-permute-start | bytes 3145736 | tf_op jit(solution)/shard_map/ppermute | solution.py:272
  151.0 24.3 %collective-permute-start.11 = (bf16[64,128,128]{2,1,0:T(8,128)(2,1)}, bf16[64,128,128]{2,1,0:T(8,128)(2,1)}, u32[]{:S(2)}, u32[]{:S(2)}) collective-permute-start(bf16[64,128,128]{2,1,0:T(8,128)(2,1)} %shard_map.119.refs_10_), channel_id=1, source_target_pairs={{0,1},{1,0},{2,3},{3,2},{4,5},{5,4},{6,7},{7,6},{8,9},{9,8},{10,11... | collective-permute-start | bytes 6291464 | tf_op jit(solution)/shard_map/ppermute | solution.py:276
  154.9 8.0 %collective-permute-start.8 = (bf16[128,128]{1,0:T(8,128)(2,1)S(1)}, bf16[128,128]{1,0:T(8,128)(2,1)S(1)}, u32[]{:S(2)}, u32[]{:S(2)}) collective-permute-start(bf16[128,128]{1,0:T(8,128)(2,1)S(1)} %get-tuple-element.103), channel_id=1, source_target_pairs={{0,504},{8,16},{16,8},{24,32},{32,24},{40,48},{48,40},{56,64},{64,... | collective-permute-start | bytes 98312 | tf_op jit(solution)/shard_map/ppermute | solution.py:253
  165.8 9.6 %all-to-all-start.3 = ((f32[8,16,128]{2,1,0:T(8,128)}), f32[8,16,128]{2,1,0:T(8,128)S(1)}, u32[]{:S(2)}, u32[]{:S(2)}) async-start(f32[8,16,128]{2,1,0:T(8,128)} %bitcast.13), calls=%async_computation.3 | async-start | bytes 131072 | tf_op jit(solution)/shard_map/all_to_all | solution.py:280
  184.2 8.0 %collective-permute-start.12 = (bf16[128,128]{1,0:T(8,128)(2,1)S(1)}, bf16[128,128]{1,0:T(8,128)(2,1)S(1)}, u32[]{:S(2)}, u32[]{:S(2)}) collective-permute-start(bf16[128,128]{1,0:T(8,128)(2,1)S(1)} %get-tuple-element.115), channel_id=1, source_target_pairs={{0,504},{8,16},{16,8},{24,32},{32,24},{40,48},{48,40},{56,64},{64,... | collective-permute-start | bytes 98312 | tf_op jit(solution)/shard_map/ppermute | solution.py:253
  187.3 5.0 %collective-permute-start.13 = (bf16[128,128]{1,0:T(8,128)(2,1)S(1)}, bf16[128,128]{1,0:T(8,128)(2,1)S(1)}, u32[]{:S(2)}, u32[]{:S(2)}) collective-permute-start(bf16[128,128]{1,0:T(8,128)(2,1)S(1)} %get-tuple-element.116), channel_id=1, source_target_pairs={{0,8},{8,0},{16,24},{24,16},{32,40},{40,32},{48,56},{56,48},{64,72... | collective-permute-start | bytes 98312 | tf_op jit(solution)/shard_map/ppermute | solution.py:254
  195.6 8.0 %collective-permute-start.14 = (bf16[128,128]{1,0:T(8,128)(2,1)S(1)}, bf16[128,128]{1,0:T(8,128)(2,1)S(1)}, u32[]{:S(2)}, u32[]{:S(2)}) collective-permute-start(bf16[128,128]{1,0:T(8,128)(2,1)S(1)} %get-tuple-element.119), channel_id=1, source_target_pairs={{0,504},{8,16},{16,8},{24,32},{32,24},{40,48},{48,40},{56,64},{64,... | collective-permute-start | bytes 98312 | tf_op jit(solution)/shard_map/ppermute | solution.py:253
  200.9 5.0 %collective-permute-start.15 = (bf16[128,128]{1,0:T(8,128)(2,1)S(1)}, bf16[128,128]{1,0:T(8,128)(2,1)S(1)}, u32[]{:S(2)}, u32[]{:S(2)}) collective-permute-start(bf16[128,128]{1,0:T(8,128)(2,1)S(1)} %get-tuple-element.120), channel_id=1, source_target_pairs={{0,8},{8,0},{16,24},{24,16},{32,40},{40,32},{48,56},{56,48},{64,72... | collective-permute-start | bytes 98312 | tf_op jit(solution)/shard_map/ppermute | solution.py:254
  209.3 8.0 %collective-permute-start.16 = (bf16[128,128]{1,0:T(8,128)(2,1)S(1)}, bf16[128,128]{1,0:T(8,128)(2,1)S(1)}, u32[]{:S(2)}, u32[]{:S(2)}) collective-permute-start(bf16[128,128]{1,0:T(8,128)(2,1)S(1)} %get-tuple-element.123), channel_id=1, source_target_pairs={{0,504},{8,16},{16,8},{24,32},{32,24},{40,48},{48,40},{56,64},{64,... | collective-permute-start | bytes 98312 | tf_op jit(solution)/shard_map/ppermute | solution.py:253
  212.3 4.9 %collective-permute-start.17 = (bf16[128,128]{1,0:T(8,128)(2,1)S(1)}, bf16[128,128]{1,0:T(8,128)(2,1)S(1)}, u32[]{:S(2)}, u32[]{:S(2)}) collective-permute-start(bf16[128,128]{1,0:T(8,128)(2,1)S(1)} %get-tuple-element.124), channel_id=1, source_target_pairs={{0,8},{8,0},{16,24},{24,16},{32,40},{40,32},{48,56},{56,48},{64,72... | collective-permute-start | bytes 98312 | tf_op jit(solution)/shard_map/ppermute | solution.py:254
  220.7 8.0 %collective-permute-start.18 = (bf16[128,128]{1,0:T(8,128)(2,1)S(1)}, bf16[128,128]{1,0:T(8,128)(2,1)S(1)}, u32[]{:S(2)}, u32[]{:S(2)}) collective-permute-start(bf16[128,128]{1,0:T(8,128)(2,1)S(1)} %get-tuple-element.127), channel_id=1, source_target_pairs={{0,504},{8,16},{16,8},{24,32},{32,24},{40,48},{48,40},{56,64},{64,... | collective-permute-start | bytes 98312 | tf_op jit(solution)/shard_map/ppermute | solution.py:253
  234.4 8.0 %collective-permute-start.20 = (bf16[128,128]{1,0:T(8,128)(2,1)S(1)}, bf16[128,128]{1,0:T(8,128)(2,1)S(1)}, u32[]{:S(2)}, u32[]{:S(2)}) collective-permute-start(bf16[128,128]{1,0:T(8,128)(2,1)S(1)} %get-tuple-element.131), channel_id=1, source_target_pairs={{0,504},{8,16},{16,8},{24,32},{32,24},{40,48},{48,40},{56,64},{64,... | collective-permute-start | bytes 98312 | tf_op jit(solution)/shard_map/ppermute | solution.py:253
  245.8 8.0 %collective-permute-start.22 = (bf16[128,128]{1,0:T(8,128)(2,1)S(1)}, bf16[128,128]{1,0:T(8,128)(2,1)S(1)}, u32[]{:S(2)}, u32[]{:S(2)}) collective-permute-start(bf16[128,128]{1,0:T(8,128)(2,1)S(1)} %get-tuple-element.135), channel_id=1, source_target_pairs={{0,504},{8,16},{16,8},{24,32},{32,24},{40,48},{48,40},{56,64},{64,... | collective-permute-start | bytes 98312 | tf_op jit(solution)/shard_map/ppermute | solution.py:253
  259.2 8.0 %collective-permute-start.24 = (bf16[128,128]{1,0:T(8,128)(2,1)S(1)}, bf16[128,128]{1,0:T(8,128)(2,1)S(1)}, u32[]{:S(2)}, u32[]{:S(2)}) collective-permute-start(bf16[128,128]{1,0:T(8,128)(2,1)S(1)} %get-tuple-element.139), channel_id=1, source_target_pairs={{0,504},{8,16},{16,8},{24,32},{32,24},{40,48},{48,40},{56,64},{64,... | collective-permute-start | bytes 98312 | tf_op jit(solution)/shard_map/ppermute | solution.py:253
  270.6 8.0 %collective-permute-start.26 = (bf16[128,128]{1,0:T(8,128)(2,1)S(1)}, bf16[128,128]{1,0:T(8,128)(2,1)S(1)}, u32[]{:S(2)}, u32[]{:S(2)}) collective-permute-start(bf16[128,128]{1,0:T(8,128)(2,1)S(1)} %get-tuple-element.143), channel_id=1, source_target_pairs={{0,504},{8,16},{16,8},{24,32},{32,24},{40,48},{48,40},{56,64},{64,... | collective-permute-start | bytes 98312 | tf_op jit(solution)/shard_map/ppermute | solution.py:253
  284.0 8.0 %collective-permute-start.28 = (bf16[128,128]{1,0:T(8,128)(2,1)S(1)}, bf16[128,128]{1,0:T(8,128)(2,1)S(1)}, u32[]{:S(2)}, u32[]{:S(2)}) collective-permute-start(bf16[128,128]{1,0:T(8,128)(2,1)S(1)} %get-tuple-element.147), channel_id=1, source_target_pairs={{0,504},{8,16},{16,8},{24,32},{32,24},{40,48},{48,40},{56,64},{64,... | collective-permute-start | bytes 98312 | tf_op jit(solution)/shard_map/ppermute | solution.py:253
  (28 other events, 380.5 us)

commit v6 on v4

--- a/solution.py
+++ b/solution.py
@@ -6,7 +6,7 @@
 from jax.sharding import PartitionSpec as P
 
 STEPS = 12
-LEVEL_STEPS = 4
+LEVEL_STEPS = 3
 GROUPS = 8
 PAIR = 2
 LEVELS = 8
@@ -306,7 +306,6 @@
     rows = GROUPS * l_slots * PAIR
     scratch = [pltpu.VMEM((rows, CELLS), kind) for kind in (BF, BF, F32)]
     (value,) = call(sum_kernel, [state], base, *received)
-    value, gathered = lax.optimization_barrier((value, gathered))
     value = to_depth(value)
     for step in range(LEVEL_STEPS, STEPS):
         if step == LEVEL_STEPS:

time: 267 us -> 266 us (level)
  blocking collectives: 61.1 us -> 49.3 us
  waiting for transfers between devices: 43.4 us -> 51.1 us
  starting transfers between devices: 94.7 us -> 99 us
    all_to_all x4 -> x3, blocking collectives: 61.1 us -> 49.3 us  [to_depth(): lax.all_to_all(value, 'depth', split_axis=0, concat_axis=0, tiled=True)]
    all_gather x1, waiting for transfers between devices: 0.01 us -> 5.78 us  [local(): lax.all_gather(jnp.concatenate([lateral_tiles, vertical_tiles], axis=0),...]
    ppermute x12, starting transfers between devices: 55.1 us -> 60.2 us  [swapped(): from_first = lax.ppermute(to_first, 'region', first)]
    pallas_call x21 -> x20, Pallas kernels: 39.3 us -> 39.1 us  [call(): pl.pallas_call(body, out_shape=[jax.ShapeDtypeStruct(shape, kind) for sha...]
  transfers between devices with their start and end apart: 27 -> 27, of which waited for: 20 -> 21; matrix products, arithmetic and copies ran while one was open for 0% -> 0% of each run, Pallas kernels for 4% -> 3%
where the time goes in v6:
time: 266 us; the launch traced here: 265 us
  starting transfers between devices  99 us (37%)
  waiting for transfers between devices  51.1 us (19%)
  blocking collectives  49.3 us (19%)
  Pallas kernels  39.1 us (15%)
  between operations  14.6 us (5%)
  local copies, waits for them, and re-layouts  8.31 us (3%)
  other arithmetic  3.13 us (1%)
    ppermute x12, starting transfers between devices, swapped(): from_first = lax.ppermute(to_first, 'region', first)  60.2 us
    all_to_all x3, blocking collectives, to_depth(): lax.all_to_all(value, 'depth', split_axis=0, concat_axis=0, tiled=True)  49.3 us
    pallas_call x20, Pallas kernels, call(): pl.pallas_call(body, out_shape=[jax.ShapeDtypeStruct(shape, kind) for sha...  39.1 us
    ppermute x12, starting transfers between devices, swapped(): from_second = lax.ppermute(to_second, 'region', second)  23.4 us
    ppermute x12, waiting for transfers between devices, swapped(): from_first = lax.ppermute(to_first, 'region', first)  17.1 us
    ppermute x12, waiting for transfers between devices, swapped(): from_second = lax.ppermute(to_second, 'region', second)  17 us
    all_to_all x2, starting transfers between devices, to_depth(): lax.all_to_all(value, 'depth', split_axis=0, concat_axis=0, tiled=True)  15.4 us
    all_to_all x2, waiting for transfers between devices, to_depth(): lax.all_to_all(value, 'depth', split_axis=0, concat_axis=0, tiled=True)  11.2 us
  transfers between devices with their start and end apart: 27, of which 21 were waited for; matrix products, arithmetic and copies ran while one was open for 0% of the time, Pallas kernels for 3%

profile of v6, /device:TPU:1, one launch (start us, length us, event | category | flops | bytes accessed | tf_op | source)
XLA Modules:
  0.0 264.6 jit_solution(13120091086599069051)
XLA Ops:
  14.0 10.2 %all-to-all-start = ((bf16[8,144,128]{2,1,0:T(8,128)(2,1)}), bf16[8,144,128]{2,1,0:T(8,128)(2,1)S(1)}, u32[]{:S(2)}, u32[]{:S(2)}) async-start(bf16[8,144,128]{2,1,0:T(8,128)(2,1)} %bitcast.7), calls=%async_computation | async-start | bytes 589824 | tf_op jit(solution)/shard_map/all_to_all | solution.py:233
  24.7 6.3 %all-to-all-done = bf16[8,144,128]{2,1,0:T(8,128)(2,1)S(1)} async-done(((bf16[8,144,128]{2,1,0:T(8,128)(2,1)}), bf16[8,144,128]{2,1,0:T(8,128)(2,1)S(1)}, u32[]{:S(2)}, u32[]{:S(2)}) %all-to-all-start) | async-done | bytes 294944 | tf_op jit(solution)/shard_map/all_to_all | solution.py:233
  32.8 9.2 %collective-permute-start = (bf16[128,128]{1,0:T(8,128)(2,1)S(1)}, bf16[128,128]{1,0:T(8,128)(2,1)S(1)}, u32[]{:S(2)}, u32[]{:S(2)}) collective-permute-start(bf16[128,128]{1,0:T(8,128)(2,1)S(1)} %get-tuple-element.70), channel_id=1, source_target_pairs={{0,504},{8,16},{16,8},{24,32},{32,24},{40,48},{48,40},{56,64},{64,... | collective-permute-start | bytes 98312 | tf_op jit(solution)/shard_map/ppermute | solution.py:227
  47.8 14.3 %all_to_all.55 = bf16[8,128,128]{2,1,0:T(8,128)(2,1)S(1)} all-to-all(bf16[8,128,128]{2,1,0:T(8,128)(2,1)S(1)} %bitcast.25), channel_id=1, replica_groups=mesh['region'=64,'depth'=8] {'depth'}, dimensions={0} | all-to-all | bytes 524288 | tf_op jit(solution)/shard_map/all_to_all | solution.py:233
  71.7 14.1 %all_to_all.56 = bf16[8,128,128]{2,1,0:T(8,128)(2,1)S(1)} all-to-all(bf16[8,128,128]{2,1,0:T(8,128)(2,1)S(1)} %bitcast.24), channel_id=1, replica_groups=mesh['region'=64,'depth'=8] {'depth'}, dimensions={0} | all-to-all | bytes 524288 | tf_op jit(solution)/shard_map/all_to_all | solution.py:233
  86.7 5.6 %collective-permute-start.4 = (bf16[128,128]{1,0:T(8,128)(2,1)S(1)}, bf16[128,128]{1,0:T(8,128)(2,1)S(1)}, u32[]{:S(2)}, u32[]{:S(2)}) collective-permute-start(bf16[128,128]{1,0:T(8,128)(2,1)S(1)} %get-tuple-element.83), channel_id=1, source_target_pairs={{0,504},{8,16},{16,8},{24,32},{32,24},{40,48},{48,40},{56,64},{64,... | collective-permute-start | bytes 98312 | tf_op jit(solution)/shard_map/ppermute | solution.py:227
  98.0 5.2 %all-to-all-start.3 = ((f32[8,16,128]{2,1,0:T(8,128)}), f32[8,16,128]{2,1,0:T(8,128)S(1)}, u32[]{:S(2)}, u32[]{:S(2)}) async-start(f32[8,16,128]{2,1,0:T(8,128)} %bitcast.13), calls=%async_computation.3 | async-start | bytes 131072 | tf_op jit(solution)/shard_map/all_to_all | solution.py:233
  103.9 4.9 %all-to-all-done.3 = f32[8,16,128]{2,1,0:T(8,128)S(1)} async-done(((f32[8,16,128]{2,1,0:T(8,128)}), f32[8,16,128]{2,1,0:T(8,128)S(1)}, u32[]{:S(2)}, u32[]{:S(2)}) %all-to-all-start.3) | async-done | bytes 65568 | tf_op jit(solution)/shard_map/all_to_all | solution.py:233
  108.8 5.8 %all-gather.2.cloned.1.call-done.refs_7_ = bf16[512,128,128]{2,1,0:T(8,128)(2,1)} async-done(((bf16[64,128,128]{2,1,0:T(8,128)(2,1)}), bf16[512,128,128]{2,1,0:T(8,128)(2,1)}) %all-gather.2.cloned.1.call-update) | async-done | bytes 16777232 | tf_op jit(solution)/shard_map/all_gather | solution.py:249
  114.6 5.8 %copy-done = bf16[512,128,128]{2,1,0:T(8,128)(2,1)S(1)} copy-done((bf16[512,128,128]{2,1,0:T(8,128)(2,1)S(1)}, bf16[512,128,128]{2,1,0:T(8,128)(2,1)}, u32[]{:S(2)}) %copy-start) | copy-done | bytes 16777240
  123.8 8.1 %collective-permute-start.6 = (bf16[128,128]{1,0:T(8,128)(2,1)S(1)}, bf16[128,128]{1,0:T(8,128)(2,1)S(1)}, u32[]{:S(2)}, u32[]{:S(2)}) collective-permute-start(bf16[128,128]{1,0:T(8,128)(2,1)S(1)} %get-tuple-element.93), channel_id=1, source_target_pairs={{0,504},{8,16},{16,8},{24,32},{32,24},{40,48},{48,40},{56,64},{64,... | collective-permute-start | bytes 98312 | tf_op jit(solution)/shard_map/ppermute | solution.py:227
  136.6 3.4 %shard_map.119 = (f32[128,128]{1,0:T(8,128)S(1)}, bf16[128,128]{1,0:T(8,128)(2,1)S(1)}, bf16[128,128]{1,0:T(8,128)(2,1)S(1)}) custom-call(f32[128,128]{1,0:T(8,128)S(1)} %get-tuple-element.92.base, bf16[128,128]{1,0:T(8,128)(2,1)S(1)} %collective-permute-done.6.first, bf16[128,128]{1,0:T(8,128)(2,1)S(1)} %collective-permute-done.7.second, ...), custom_call_target="tpu_custom_call" | custom-call | tf_op jit(solution)/shard_map/pallas_call | solution.py:213
  148.0 3.4 %shard_map.120 = (f32[128,128]{1,0:T(8,128)S(1)}, bf16[128,128]{1,0:T(8,128)(2,1)S(1)}, bf16[128,128]{1,0:T(8,128)(2,1)S(1)}) custom-call(f32[128,128]{1,0:T(8,128)S(1)} %get-tuple-element.95.base, bf16[128,128]{1,0:T(8,128)(2,1)S(1)} %collective-permute-done.8.first, bf16[128,128]{1,0:T(8,128)(2,1)S(1)} %collective-permute-done.9.second, ...), custom_call_target="tpu_custom_call" | custom-call | tf_op jit(solution)/shard_map/pallas_call | solution.py:213
  151.4 5.5 %collective-permute-start.10 = (bf16[128,128]{1,0:T(8,128)(2,1)S(1)}, bf16[128,128]{1,0:T(8,128)(2,1)S(1)}, u32[]{:S(2)}, u32[]{:S(2)}) collective-permute-start(bf16[128,128]{1,0:T(8,128)(2,1)S(1)} %get-tuple-element.99), channel_id=1, source_target_pairs={{0,504},{8,16},{16,8},{24,32},{32,24},{40,48},{48,40},{56,64},{64,... | collective-permute-start | bytes 98312 | tf_op jit(solution)/shard_map/ppermute | solution.py:227
  161.8 3.4 %shard_map.121 = (f32[128,128]{1,0:T(8,128)S(1)}, bf16[128,128]{1,0:T(8,128)(2,1)S(1)}, bf16[128,128]{1,0:T(8,128)(2,1)S(1)}) custom-call(f32[128,128]{1,0:T(8,128)S(1)} %get-tuple-element.98.base, bf16[128,128]{1,0:T(8,128)(2,1)S(1)} %collective-permute-done.10.first, bf16[128,128]{1,0:T(8,128)(2,1)S(1)} %collective-permute-done.11.second, ...), custom_call_target="tpu_custom_call" | custom-call | tf_op jit(solution)/shard_map/pallas_call | solution.py:213
  173.2 3.4 %shard_map.122 = (f32[128,128]{1,0:T(8,128)S(1)}, bf16[128,128]{1,0:T(8,128)(2,1)S(1)}, bf16[128,128]{1,0:T(8,128)(2,1)S(1)}) custom-call(f32[128,128]{1,0:T(8,128)S(1)} %get-tuple-element.101.base, bf16[128,128]{1,0:T(8,128)(2,1)S(1)} %collective-permute-done.12.first, bf16[128,128]{1,0:T(8,128)(2,1)S(1)} %collective-permute-done.13.second, ...), custom_call_target="tpu_custom_call" | custom-call | tf_op jit(solution)/shard_map/pallas_call | solution.py:213
  176.7 5.3 %collective-permute-start.14 = (bf16[128,128]{1,0:T(8,128)(2,1)S(1)}, bf16[128,128]{1,0:T(8,128)(2,1)S(1)}, u32[]{:S(2)}, u32[]{:S(2)}) collective-permute-start(bf16[128,128]{1,0:T(8,128)(2,1)S(1)} %get-tuple-element.105), channel_id=1, source_target_pairs={{0,504},{8,16},{16,8},{24,32},{32,24},{40,48},{48,40},{56,64},{64,... | collective-permute-start | bytes 98312 | tf_op jit(solution)/shard_map/ppermute | solution.py:227
  186.6 3.4 %shard_map.123 = (f32[128,128]{1,0:T(8,128)S(1)}, bf16[128,128]{1,0:T(8,128)(2,1)S(1)}, bf16[128,128]{1,0:T(8,128)(2,1)S(1)}) custom-call(f32[128,128]{1,0:T(8,128)S(1)} %get-tuple-element.104.base, bf16[128,128]{1,0:T(8,128)(2,1)S(1)} %collective-permute-done.14.first, bf16[128,128]{1,0:T(8,128)(2,1)S(1)} %collective-permute-done.15.second, ...), custom_call_target="tpu_custom_call" | custom-call | tf_op jit(solution)/shard_map/pallas_call | solution.py:213
  198.0 3.4 %shard_map.124 = (f32[128,128]{1,0:T(8,128)S(1)}, bf16[128,128]{1,0:T(8,128)(2,1)S(1)}, bf16[128,128]{1,0:T(8,128)(2,1)S(1)}) custom-call(f32[128,128]{1,0:T(8,128)S(1)} %get-tuple-element.107.base, bf16[128,128]{1,0:T(8,128)(2,1)S(1)} %collective-permute-done.16.first, bf16[128,128]{1,0:T(8,128)(2,1)S(1)} %collective-permute-done.17.second, ...), custom_call_target="tpu_custom_call" | custom-call | tf_op jit(solution)/shard_map/pallas_call | solution.py:213
  201.4 5.3 %collective-permute-start.18 = (bf16[128,128]{1,0:T(8,128)(2,1)S(1)}, bf16[128,128]{1,0:T(8,128)(2,1)S(1)}, u32[]{:S(2)}, u32[]{:S(2)}) collective-permute-start(bf16[128,128]{1,0:T(8,128)(2,1)S(1)} %get-tuple-element.111), channel_id=1, source_target_pairs={{0,504},{8,16},{16,8},{24,32},{32,24},{40,48},{48,40},{56,64},{64,... | collective-permute-start | bytes 98312 | tf_op jit(solution)/shard_map/ppermute | solution.py:227
  211.4 3.4 %shard_map.125 = (f32[128,128]{1,0:T(8,128)S(1)}, bf16[128,128]{1,0:T(8,128)(2,1)S(1)}, bf16[128,128]{1,0:T(8,128)(2,1)S(1)}) custom-call(f32[128,128]{1,0:T(8,128)S(1)} %get-tuple-element.110.base, bf16[128,128]{1,0:T(8,128)(2,1)S(1)} %collective-permute-done.18.first, bf16[128,128]{1,0:T(8,128)(2,1)S(1)} %collective-permute-done.19.second, ...), custom_call_target="tpu_custom_call" | custom-call | tf_op jit(solution)/shard_map/pallas_call | solution.py:213
  222.8 3.4 %shard_map.126 = (f32[128,128]{1,0:T(8,128)S(1)}, bf16[128,128]{1,0:T(8,128)(2,1)S(1)}, bf16[128,128]{1,0:T(8,128)(2,1)S(1)}) custom-call(f32[128,128]{1,0:T(8,128)S(1)} %get-tuple-element.113.base, bf16[128,128]{1,0:T(8,128)(2,1)S(1)} %collective-permute-done.20.first, bf16[128,128]{1,0:T(8,128)(2,1)S(1)} %collective-permute-done.21.second, ...), custom_call_target="tpu_custom_call" | custom-call | tf_op jit(solution)/shard_map/pallas_call | solution.py:213
  226.2 5.3 %collective-permute-start.22 = (bf16[128,128]{1,0:T(8,128)(2,1)S(1)}, bf16[128,128]{1,0:T(8,128)(2,1)S(1)}, u32[]{:S(2)}, u32[]{:S(2)}) collective-permute-start(bf16[128,128]{1,0:T(8,128)(2,1)S(1)} %get-tuple-element.117), channel_id=1, source_target_pairs={{0,504},{8,16},{16,8},{24,32},{32,24},{40,48},{48,40},{56,64},{64,... | collective-permute-start | bytes 98312 | tf_op jit(solution)/shard_map/ppermute | solution.py:227
  236.2 20.9 %all_to_all.57 = f32[8,16,128]{2,1,0:T(8,128)S(1)} all-to-all(f32[8,16,128]{2,1,0:T(8,128)S(1)} %bitcast.22), channel_id=1, replica_groups=mesh['region'=64,'depth'=8] {'depth'}, dimensions={0} | all-to-all | bytes 131072 | tf_op jit(solution)/shard_map/all_to_all | solution.py:233
  (91 shorter events, 91.1 us)
Async XLA Ops:
  6.5 108.0 %all-gather.2.cloned.1.call-start = ((), (), s32[]{:S(2)}) async-start(), calls=%async_computation.5 | async-start | bytes 18874368 | tf_op jit(solution)/shard_map/all_gather | solution.py:249
  14.0 17.0 %all-to-all-start = ((bf16[8,144,128]{2,1,0:T(8,128)(2,1)}), bf16[8,144,128]{2,1,0:T(8,128)(2,1)S(1)}, u32[]{:S(2)}, u32[]{:S(2)}) async-start(bf16[8,144,128]{2,1,0:T(8,128)(2,1)} %bitcast.7), calls=%async_computation | async-start | bytes 589824 | tf_op jit(solution)/shard_map/all_to_all | solution.py:233
  32.8 11.1 %collective-permute-start = (bf16[128,128]{1,0:T(8,128)(2,1)S(1)}, bf16[128,128]{1,0:T(8,128)(2,1)S(1)}, u32[]{:S(2)}, u32[]{:S(2)}) collective-permute-start(bf16[128,128]{1,0:T(8,128)(2,1)S(1)} %get-tuple-element.70), channel_id=1, source_target_pairs={{0,504},{8,16},{16,8},{24,32},{32,24},{40,48},{48,40},{56,64},{64,... | collective-permute-start | bytes 98312 | tf_op jit(solution)/shard_map/ppermute | solution.py:227
  42.0 5.1 %collective-permute-start.1 = (bf16[128,128]{1,0:T(8,128)(2,1)S(1)}, bf16[128,128]{1,0:T(8,128)(2,1)S(1)}, u32[]{:S(2)}, u32[]{:S(2)}) collective-permute-start(bf16[128,128]{1,0:T(8,128)(2,1)S(1)} %get-tuple-element.71), channel_id=1, source_target_pairs={{0,8},{8,0},{16,24},{24,16},{32,40},{40,32},{48,56},{56,48},{64,72... | collective-permute-start | bytes 98312 | tf_op jit(solution)/shard_map/ppermute | solution.py:228
  62.9 8.0 %collective-permute-start.2 = (bf16[128,128]{1,0:T(8,128)(2,1)S(1)}, bf16[128,128]{1,0:T(8,128)(2,1)S(1)}, u32[]{:S(2)}, u32[]{:S(2)}) collective-permute-start(bf16[128,128]{1,0:T(8,128)(2,1)S(1)} %get-tuple-element.78), channel_id=1, source_target_pairs={{0,504},{8,16},{16,8},{24,32},{32,24},{40,48},{48,40},{56,64},{64,... | collective-permute-start | bytes 98312 | tf_op jit(solution)/shard_map/ppermute | solution.py:227
  65.9 5.1 %collective-permute-start.3 = (bf16[128,128]{1,0:T(8,128)(2,1)S(1)}, bf16[128,128]{1,0:T(8,128)(2,1)S(1)}, u32[]{:S(2)}, u32[]{:S(2)}) collective-permute-start(bf16[128,128]{1,0:T(8,128)(2,1)S(1)} %get-tuple-element.79), channel_id=1, source_target_pairs={{0,8},{8,0},{16,24},{24,16},{32,40},{40,32},{48,56},{56,48},{64,72... | collective-permute-start | bytes 98312 | tf_op jit(solution)/shard_map/ppermute | solution.py:228
  86.7 8.0 %collective-permute-start.4 = (bf16[128,128]{1,0:T(8,128)(2,1)S(1)}, bf16[128,128]{1,0:T(8,128)(2,1)S(1)}, u32[]{:S(2)}, u32[]{:S(2)}) collective-permute-start(bf16[128,128]{1,0:T(8,128)(2,1)S(1)} %get-tuple-element.83), channel_id=1, source_target_pairs={{0,504},{8,16},{16,8},{24,32},{32,24},{40,48},{48,40},{56,64},{64,... | collective-permute-start | bytes 98312 | tf_op jit(solution)/shard_map/ppermute | solution.py:227
  92.3 5.1 %collective-permute-start.5 = (bf16[128,128]{1,0:T(8,128)(2,1)S(1)}, bf16[128,128]{1,0:T(8,128)(2,1)S(1)}, u32[]{:S(2)}, u32[]{:S(2)}) collective-permute-start(bf16[128,128]{1,0:T(8,128)(2,1)S(1)} %get-tuple-element.84), channel_id=1, source_target_pairs={{0,8},{8,0},{16,24},{24,16},{32,40},{40,32},{48,56},{56,48},{64,72... | collective-permute-start | bytes 98312 | tf_op jit(solution)/shard_map/ppermute | solution.py:228
  98.0 10.8 %all-to-all-start.3 = ((f32[8,16,128]{2,1,0:T(8,128)}), f32[8,16,128]{2,1,0:T(8,128)S(1)}, u32[]{:S(2)}, u32[]{:S(2)}) async-start(f32[8,16,128]{2,1,0:T(8,128)} %bitcast.13), calls=%async_computation.3 | async-start | bytes 131072 | tf_op jit(solution)/shard_map/all_to_all | solution.py:233
  123.8 10.1 %collective-permute-start.6 = (bf16[128,128]{1,0:T(8,128)(2,1)S(1)}, bf16[128,128]{1,0:T(8,128)(2,1)S(1)}, u32[]{:S(2)}, u32[]{:S(2)}) collective-permute-start(bf16[128,128]{1,0:T(8,128)(2,1)S(1)} %get-tuple-element.93), channel_id=1, source_target_pairs={{0,504},{8,16},{16,8},{24,32},{32,24},{40,48},{48,40},{56,64},{64,... | collective-permute-start | bytes 98312 | tf_op jit(solution)/shard_map/ppermute | solution.py:227
  131.9 4.7 %collective-permute-start.7 = (bf16[128,128]{1,0:T(8,128)(2,1)S(1)}, bf16[128,128]{1,0:T(8,128)(2,1)S(1)}, u32[]{:S(2)}, u32[]{:S(2)}) collective-permute-start(bf16[128,128]{1,0:T(8,128)(2,1)S(1)} %get-tuple-element.94), channel_id=1, source_target_pairs={{0,8},{8,0},{16,24},{24,16},{32,40},{40,32},{48,56},{56,48},{64,72... | collective-permute-start | bytes 98312 | tf_op jit(solution)/shard_map/ppermute | solution.py:228
  140.0 8.0 %collective-permute-start.8 = (bf16[128,128]{1,0:T(8,128)(2,1)S(1)}, bf16[128,128]{1,0:T(8,128)(2,1)S(1)}, u32[]{:S(2)}, u32[]{:S(2)}) collective-permute-start(bf16[128,128]{1,0:T(8,128)(2,1)S(1)} %get-tuple-element.96), channel_id=1, source_target_pairs={{0,504},{8,16},{16,8},{24,32},{32,24},{40,48},{48,40},{56,64},{64,... | collective-permute-start | bytes 98312 | tf_op jit(solution)/shard_map/ppermute | solution.py:227
  151.4 8.0 %collective-permute-start.10 = (bf16[128,128]{1,0:T(8,128)(2,1)S(1)}, bf16[128,128]{1,0:T(8,128)(2,1)S(1)}, u32[]{:S(2)}, u32[]{:S(2)}) collective-permute-start(bf16[128,128]{1,0:T(8,128)(2,1)S(1)} %get-tuple-element.99), channel_id=1, source_target_pairs={{0,504},{8,16},{16,8},{24,32},{32,24},{40,48},{48,40},{56,64},{64,... | collective-permute-start | bytes 98312 | tf_op jit(solution)/shard_map/ppermute | solution.py:227
  156.9 5.0 %collective-permute-start.11 = (bf16[128,128]{1,0:T(8,128)(2,1)S(1)}, bf16[128,128]{1,0:T(8,128)(2,1)S(1)}, u32[]{:S(2)}, u32[]{:S(2)}) collective-permute-start(bf16[128,128]{1,0:T(8,128)(2,1)S(1)} %get-tuple-element.100), channel_id=1, source_target_pairs={{0,8},{8,0},{16,24},{24,16},{32,40},{40,32},{48,56},{56,48},{64,72... | collective-permute-start | bytes 98312 | tf_op jit(solution)/shard_map/ppermute | solution.py:228
  165.2 8.0 %collective-permute-start.12 = (bf16[128,128]{1,0:T(8,128)(2,1)S(1)}, bf16[128,128]{1,0:T(8,128)(2,1)S(1)}, u32[]{:S(2)}, u32[]{:S(2)}) collective-permute-start(bf16[128,128]{1,0:T(8,128)(2,1)S(1)} %get-tuple-element.102), channel_id=1, source_target_pairs={{0,504},{8,16},{16,8},{24,32},{32,24},{40,48},{48,40},{56,64},{64,... | collective-permute-start | bytes 98312 | tf_op jit(solution)/shard_map/ppermute | solution.py:227
  168.3 5.0 %collective-permute-start.13 = (bf16[128,128]{1,0:T(8,128)(2,1)S(1)}, bf16[128,128]{1,0:T(8,128)(2,1)S(1)}, u32[]{:S(2)}, u32[]{:S(2)}) collective-permute-start(bf16[128,128]{1,0:T(8,128)(2,1)S(1)} %get-tuple-element.103), channel_id=1, source_target_pairs={{0,8},{8,0},{16,24},{24,16},{32,40},{40,32},{48,56},{56,48},{64,72... | collective-permute-start | bytes 98312 | tf_op jit(solution)/shard_map/ppermute | solution.py:228
  176.7 8.0 %collective-permute-start.14 = (bf16[128,128]{1,0:T(8,128)(2,1)S(1)}, bf16[128,128]{1,0:T(8,128)(2,1)S(1)}, u32[]{:S(2)}, u32[]{:S(2)}) collective-permute-start(bf16[128,128]{1,0:T(8,128)(2,1)S(1)} %get-tuple-element.105), channel_id=1, source_target_pairs={{0,504},{8,16},{16,8},{24,32},{32,24},{40,48},{48,40},{56,64},{64,... | collective-permute-start | bytes 98312 | tf_op jit(solution)/shard_map/ppermute | solution.py:227
  182.0 4.7 %collective-permute-start.15 = (bf16[128,128]{1,0:T(8,128)(2,1)S(1)}, bf16[128,128]{1,0:T(8,128)(2,1)S(1)}, u32[]{:S(2)}, u32[]{:S(2)}) collective-permute-start(bf16[128,128]{1,0:T(8,128)(2,1)S(1)} %get-tuple-element.106), channel_id=1, source_target_pairs={{0,8},{8,0},{16,24},{24,16},{32,40},{40,32},{48,56},{56,48},{64,72... | collective-permute-start | bytes 98312 | tf_op jit(solution)/shard_map/ppermute | solution.py:228
  190.0 8.0 %collective-permute-start.16 = (bf16[128,128]{1,0:T(8,128)(2,1)S(1)}, bf16[128,128]{1,0:T(8,128)(2,1)S(1)}, u32[]{:S(2)}, u32[]{:S(2)}) collective-permute-start(bf16[128,128]{1,0:T(8,128)(2,1)S(1)} %get-tuple-element.108), channel_id=1, source_target_pairs={{0,504},{8,16},{16,8},{24,32},{32,24},{40,48},{48,40},{56,64},{64,... | collective-permute-start | bytes 98312 | tf_op jit(solution)/shard_map/ppermute | solution.py:227
  193.4 4.7 %collective-permute-start.17 = (bf16[128,128]{1,0:T(8,128)(2,1)S(1)}, bf16[128,128]{1,0:T(8,128)(2,1)S(1)}, u32[]{:S(2)}, u32[]{:S(2)}) collective-permute-start(bf16[128,128]{1,0:T(8,128)(2,1)S(1)} %get-tuple-element.109), channel_id=1, source_target_pairs={{0,8},{8,0},{16,24},{24,16},{32,40},{40,32},{48,56},{56,48},{64,72... | collective-permute-start | bytes 98312 | tf_op jit(solution)/shard_map/ppermute | solution.py:228
  201.4 8.0 %collective-permute-start.18 = (bf16[128,128]{1,0:T(8,128)(2,1)S(1)}, bf16[128,128]{1,0:T(8,128)(2,1)S(1)}, u32[]{:S(2)}, u32[]{:S(2)}) collective-permute-start(bf16[128,128]{1,0:T(8,128)(2,1)S(1)} %get-tuple-element.111), channel_id=1, source_target_pairs={{0,504},{8,16},{16,8},{24,32},{32,24},{40,48},{48,40},{56,64},{64,... | collective-permute-start | bytes 98312 | tf_op jit(solution)/shard_map/ppermute | solution.py:227
  214.8 8.0 %collective-permute-start.20 = (bf16[128,128]{1,0:T(8,128)(2,1)S(1)}, bf16[128,128]{1,0:T(8,128)(2,1)S(1)}, u32[]{:S(2)}, u32[]{:S(2)}) collective-permute-start(bf16[128,128]{1,0:T(8,128)(2,1)S(1)} %get-tuple-element.114), channel_id=1, source_target_pairs={{0,504},{8,16},{16,8},{24,32},{32,24},{40,48},{48,40},{56,64},{64,... | collective-permute-start | bytes 98312 | tf_op jit(solution)/shard_map/ppermute | solution.py:227
  218.2 4.7 %collective-permute-start.21 = (bf16[128,128]{1,0:T(8,128)(2,1)S(1)}, bf16[128,128]{1,0:T(8,128)(2,1)S(1)}, u32[]{:S(2)}, u32[]{:S(2)}) collective-permute-start(bf16[128,128]{1,0:T(8,128)(2,1)S(1)} %get-tuple-element.115), channel_id=1, source_target_pairs={{0,8},{8,0},{16,24},{24,16},{32,40},{40,32},{48,56},{56,48},{64,72... | collective-permute-start | bytes 98312 | tf_op jit(solution)/shard_map/ppermute | solution.py:228
  226.2 8.0 %collective-permute-start.22 = (bf16[128,128]{1,0:T(8,128)(2,1)S(1)}, bf16[128,128]{1,0:T(8,128)(2,1)S(1)}, u32[]{:S(2)}, u32[]{:S(2)}) collective-permute-start(bf16[128,128]{1,0:T(8,128)(2,1)S(1)} %get-tuple-element.117), channel_id=1, source_target_pairs={{0,504},{8,16},{16,8},{24,32},{32,24},{40,48},{48,40},{56,64},{64,... | collective-permute-start | bytes 98312 | tf_op jit(solution)/shard_map/ppermute | solution.py:227
  (21 other events, 114.1 us)
Sparse Core Ops, SparseCore 0:
  9.9 104.6 all-gather.1

commit v7 on v6

--- a/solution.py
+++ b/solution.py
@@ -157,21 +157,20 @@
     write_place(lines_v[0:1], v_place)
 
 
-def tracer_products(rows, left, right, place, tiles, first, slots, scratch):
+def tracer_products(rows, left, right, place, tiles, slots, scratch):
     x_left, x_right, product = scratch
     count = left.shape[0]
     rows = rows.astype(BF)
     x_left[:count] = dot(left[...], rows).astype(BF)
     x_right[:count] = dot(right[...], rows).astype(BF)
     upper_rows = iota((8, CELLS), 0) < 2 * PAIR
-    blocks = tiles.shape[0] // GROUPS
     for depth in range(GROUPS):
         for octet in range(slots // 8):
             at = (depth * slots + octet * 8) * PAIR
             part = slice(at, at + 8 * PAIR)
             lhs = jnp.concatenate([x_left[part], x_right[part]], axis=1)
             for quad in range(2):
-                tile = depth * blocks + first + octet * 8 + quad * 4
+                tile = depth * slots + octet * 8 + quad * 4
                 upper = jnp.concatenate([tiles[tile], tiles[tile + 2]], axis=1)
                 lower = jnp.concatenate([tiles[tile + 1], tiles[tile + 3]], axis=1)
                 out = dot(lhs, jnp.concatenate([upper, lower], axis=0))[8 * quad : 8 * quad + 8]
@@ -179,11 +178,14 @@
     return placed(place, product[:count])
 
 
-def tracer_step(value, wet, v_left, v_right, v_place, l_left, l_right, l_place, tiles, base, to_first, to_second, *scratch):
+def tracer_step(
+    value, wet, v_left, v_right, v_place, l_left, l_right, l_place, v_tiles, l_tiles,
+    base, to_first, to_second, *scratch,
+):
     l_slots, v_slots = l_left.shape[0] // (GROUPS * PAIR), v_left.shape[0] // (GROUPS * PAIR)
     value = wet[...] * value
-    value = wet[...] * (value + tracer_products(value, v_left, v_right, v_place, tiles, l_slots, v_slots, scratch))
-    partial = tracer_products(value, l_left, l_right, l_place, tiles, 0, l_slots, scratch)
+    value = wet[...] * (value + tracer_products(value, v_left, v_right, v_place, v_tiles, v_slots, scratch))
+    partial = tracer_products(value, l_left, l_right, l_place, l_tiles, l_slots, scratch)
     to_first[...] = partial[:STATE].astype(BF)
     to_second[...] = partial[2 * STATE :].astype(BF)
     base[...] = value + partial[STATE : 2 * STATE]
@@ -246,9 +248,9 @@
     vertical_peers,
     vertical_targets,
 ):
-    gathered = lax.all_gather(
-        jnp.concatenate([lateral_tiles, vertical_tiles], axis=0), "depth", axis=0, tiled=True
-    )
+    gathered = [
+        lax.all_gather(tiles, "depth", axis=0, tiled=True) for tiles in (vertical_tiles, lateral_tiles)
+    ]
     l_slots, v_slots = lateral_tiles.shape[0], vertical_tiles.shape[0]
     lengths = column_lengths.reshape(1, CELLS)
     state = ((STATE, CELLS), F32)
@@ -312,7 +314,7 @@
             arrived, body = (value,), tracer_first_kernel
         else:
             arrived, body = (base, *received), tracer_kernel
-        base, to_first, to_second = call(body, [state, sent, sent], *arrived, *constants, gathered, scratch=scratch)
+        base, to_first, to_second = call(body, [state, sent, sent], *arrived, *constants, *gathered, scratch=scratch)
         received = swapped(to_first, to_second)
     (value,) = call(sum_kernel, [state], base, *received)
     (adjoint,) = call(close_kernel, [((LEVELS, TRACERS, CELLS), F32)], to_depth(value), wet)

time: 266 us -> 288 us (1.083)
  waiting for transfers between devices: 51.1 us -> 68.1 us
  local copies, waits for them, and re-layouts: 8.31 us -> 18 us
  other arithmetic: 3.13 us -> 0 us
    all_gather x1 -> x2, waiting for transfers between devices: 5.78 us -> 21.5 us  [local(): lax.all_gather(tiles, 'depth', axis=0, tiled=True)]
    unnamed x36 -> x42, local copies, waits for them, and re-layouts: 8.31 us -> 18 us
    concatenate x1 -> x0, other arithmetic: 3.13 us -> none  [local(): jnp.concatenate([lateral_tiles, vertical_tiles], axis=0)]
  transfers between devices with their start and end apart: 27 -> 28, of which waited for: 21 -> 20; matrix products, arithmetic and copies ran while one was open for 0% -> 0% of each run, Pallas kernels for 3% -> 3%
where the time goes in v7:
time: 288 us; the launch traced here: 286 us
  starting transfers between devices  99.9 us (35%)
  waiting for transfers between devices  68.1 us (24%)
  blocking collectives  46.8 us (16%)
  Pallas kernels  39.1 us (14%)
  local copies, waits for them, and re-layouts  18 us (6%)
  between operations  14.4 us (5%)
    ppermute x12, starting transfers between devices, swapped(): from_first = lax.ppermute(to_first, 'region', first)  61 us
    all_to_all x3, blocking collectives, to_depth(): lax.all_to_all(value, 'depth', split_axis=0, concat_axis=0, tiled=True)  46.8 us
    pallas_call x20, Pallas kernels, call(): pl.pallas_call(body, out_shape=[jax.ShapeDtypeStruct(shape, kind) for sha...  39.1 us
    ppermute x12, starting transfers between devices, swapped(): from_second = lax.ppermute(to_second, 'region', second)  23.4 us
    all_gather x2, waiting for transfers between devices, local(): lax.all_gather(tiles, 'depth', axis=0, tiled=True)  21.5 us
    unnamed x42, local copies, waits for them, and re-layouts  18 us
    ppermute x12, waiting for transfers between devices, swapped(): from_first = lax.ppermute(to_first, 'region', first)  17.1 us
    ppermute x12, waiting for transfers between devices, swapped(): from_second = lax.ppermute(to_second, 'region', second)  16.9 us
  transfers between devices with their start and end apart: 28, of which 20 were waited for; matrix products, arithmetic and copies ran while one was open for 0% of the time, Pallas kernels for 3%

profile of v7, /device:TPU:1, one launch (start us, length us, event | category | flops | bytes accessed | tf_op | source)
XLA Modules:
  0.0 286.4 jit_solution(13041157238078562747)
XLA Ops:
  19.0 10.2 %all-to-all-start = ((bf16[8,144,128]{2,1,0:T(8,128)(2,1)}), bf16[8,144,128]{2,1,0:T(8,128)(2,1)S(1)}, u32[]{:S(2)}, u32[]{:S(2)}) async-start(bf16[8,144,128]{2,1,0:T(8,128)(2,1)} %bitcast.7), calls=%async_computation | async-start | bytes 589824 | tf_op jit(solution)/shard_map/all_to_all | solution.py:235
  29.7 6.3 %all-to-all-done = bf16[8,144,128]{2,1,0:T(8,128)(2,1)S(1)} async-done(((bf16[8,144,128]{2,1,0:T(8,128)(2,1)}), bf16[8,144,128]{2,1,0:T(8,128)(2,1)S(1)}, u32[]{:S(2)}, u32[]{:S(2)}) %all-to-all-start) | async-done | bytes 294944 | tf_op jit(solution)/shard_map/all_to_all | solution.py:235
  37.7 10.1 %collective-permute-start = (bf16[128,128]{1,0:T(8,128)(2,1)S(1)}, bf16[128,128]{1,0:T(8,128)(2,1)S(1)}, u32[]{:S(2)}, u32[]{:S(2)}) collective-permute-start(bf16[128,128]{1,0:T(8,128)(2,1)S(1)} %get-tuple-element.70), channel_id=1, source_target_pairs={{0,504},{8,16},{16,8},{24,32},{32,24},{40,48},{48,40},{56,64},{64,... | collective-permute-start | bytes 98312 | tf_op jit(solution)/shard_map/ppermute | solution.py:229
  55.5 11.8 %all_to_all.55 = bf16[8,128,128]{2,1,0:T(8,128)(2,1)S(1)} all-to-all(bf16[8,128,128]{2,1,0:T(8,128)(2,1)S(1)} %bitcast.25), channel_id=1, replica_groups=mesh['region'=64,'depth'=8] {'depth'}, dimensions={0} | all-to-all | bytes 524288 | tf_op jit(solution)/shard_map/all_to_all | solution.py:235
  76.9 14.3 %all_to_all.56 = bf16[8,128,128]{2,1,0:T(8,128)(2,1)S(1)} all-to-all(bf16[8,128,128]{2,1,0:T(8,128)(2,1)S(1)} %bitcast.24), channel_id=1, replica_groups=mesh['region'=64,'depth'=8] {'depth'}, dimensions={0} | all-to-all | bytes 524288 | tf_op jit(solution)/shard_map/all_to_all | solution.py:235
  92.2 5.6 %collective-permute-start.4 = (bf16[128,128]{1,0:T(8,128)(2,1)S(1)}, bf16[128,128]{1,0:T(8,128)(2,1)S(1)}, u32[]{:S(2)}, u32[]{:S(2)}) collective-permute-start(bf16[128,128]{1,0:T(8,128)(2,1)S(1)} %get-tuple-element.83), channel_id=1, source_target_pairs={{0,504},{8,16},{16,8},{24,32},{32,24},{40,48},{48,40},{56,64},{64,... | collective-permute-start | bytes 98312 | tf_op jit(solution)/shard_map/ppermute | solution.py:229
  103.4 5.2 %all-to-all-start.3 = ((f32[8,16,128]{2,1,0:T(8,128)}), f32[8,16,128]{2,1,0:T(8,128)S(1)}, u32[]{:S(2)}, u32[]{:S(2)}) async-start(f32[8,16,128]{2,1,0:T(8,128)} %bitcast.13), calls=%async_computation.3 | async-start | bytes 131072 | tf_op jit(solution)/shard_map/all_to_all | solution.py:235
  109.3 4.9 %all-to-all-done.3 = f32[8,16,128]{2,1,0:T(8,128)S(1)} async-done(((f32[8,16,128]{2,1,0:T(8,128)}), f32[8,16,128]{2,1,0:T(8,128)S(1)}, u32[]{:S(2)}, u32[]{:S(2)}) %all-to-all-start.3) | async-done | bytes 65568 | tf_op jit(solution)/shard_map/all_to_all | solution.py:235
  114.2 21.5 %all-gather.5.cloned.1.call-done.refs_8_ = bf16[384,128,128]{2,1,0:T(8,128)(2,1)} async-done(((bf16[48,128,128]{2,1,0:T(8,128)(2,1)}), bf16[384,128,128]{2,1,0:T(8,128)(2,1)}) %all-gather.5.cloned.1.call-update) | async-done | bytes 12582928 | tf_op jit(solution)/shard_map/all_gather | solution.py:252
  135.7 4.6 %copy-done = bf16[384,128,128]{2,1,0:T(8,128)(2,1)S(1)} copy-done((bf16[384,128,128]{2,1,0:T(8,128)(2,1)S(1)}, bf16[384,128,128]{2,1,0:T(8,128)(2,1)}, u32[]{:S(2)}) %copy-start) | copy-done | bytes 12582936
  145.9 8.0 %collective-permute-start.6 = (bf16[128,128]{1,0:T(8,128)(2,1)S(1)}, bf16[128,128]{1,0:T(8,128)(2,1)S(1)}, u32[]{:S(2)}, u32[]{:S(2)}) collective-permute-start(bf16[128,128]{1,0:T(8,128)(2,1)S(1)} %get-tuple-element.93), channel_id=1, source_target_pairs={{0,504},{8,16},{16,8},{24,32},{32,24},{40,48},{48,40},{56,64},{64,... | collective-permute-start | bytes 98312 | tf_op jit(solution)/shard_map/ppermute | solution.py:229
  158.6 3.4 %shard_map.119 = (f32[128,128]{1,0:T(8,128)S(1)}, bf16[128,128]{1,0:T(8,128)(2,1)S(1)}, bf16[128,128]{1,0:T(8,128)(2,1)S(1)}) custom-call(f32[128,128]{1,0:T(8,128)S(1)} %get-tuple-element.92.base, bf16[128,128]{1,0:T(8,128)(2,1)S(1)} %collective-permute-done.6.first, bf16[128,128]{1,0:T(8,128)(2,1)S(1)} %collective-permute-done.7.second, ...), custom_call_target="tpu_custom_call" | custom-call | tf_op jit(solution)/shard_map/pallas_call | solution.py:215
  170.0 3.4 %shard_map.120 = (f32[128,128]{1,0:T(8,128)S(1)}, bf16[128,128]{1,0:T(8,128)(2,1)S(1)}, bf16[128,128]{1,0:T(8,128)(2,1)S(1)}) custom-call(f32[128,128]{1,0:T(8,128)S(1)} %get-tuple-element.95.base, bf16[128,128]{1,0:T(8,128)(2,1)S(1)} %collective-permute-done.8.first, bf16[128,128]{1,0:T(8,128)(2,1)S(1)} %collective-permute-done.9.second, ...), custom_call_target="tpu_custom_call" | custom-call | tf_op jit(solution)/shard_map/pallas_call | solution.py:215
  173.4 5.5 %collective-permute-start.10 = (bf16[128,128]{1,0:T(8,128)(2,1)S(1)}, bf16[128,128]{1,0:T(8,128)(2,1)S(1)}, u32[]{:S(2)}, u32[]{:S(2)}) collective-permute-start(bf16[128,128]{1,0:T(8,128)(2,1)S(1)} %get-tuple-element.99), channel_id=1, source_target_pairs={{0,504},{8,16},{16,8},{24,32},{32,24},{40,48},{48,40},{56,64},{64,... | collective-permute-start | bytes 98312 | tf_op jit(solution)/shard_map/ppermute | solution.py:229
  183.8 3.4 %shard_map.121 = (f32[128,128]{1,0:T(8,128)S(1)}, bf16[128,128]{1,0:T(8,128)(2,1)S(1)}, bf16[128,128]{1,0:T(8,128)(2,1)S(1)}) custom-call(f32[128,128]{1,0:T(8,128)S(1)} %get-tuple-element.98.base, bf16[128,128]{1,0:T(8,128)(2,1)S(1)} %collective-permute-done.10.first, bf16[128,128]{1,0:T(8,128)(2,1)S(1)} %collective-permute-done.11.second, ...), custom_call_target="tpu_custom_call" | custom-call | tf_op jit(solution)/shard_map/pallas_call | solution.py:215
  195.3 3.4 %shard_map.122 = (f32[128,128]{1,0:T(8,128)S(1)}, bf16[128,128]{1,0:T(8,128)(2,1)S(1)}, bf16[128,128]{1,0:T(8,128)(2,1)S(1)}) custom-call(f32[128,128]{1,0:T(8,128)S(1)} %get-tuple-element.101.base, bf16[128,128]{1,0:T(8,128)(2,1)S(1)} %collective-permute-done.12.first, bf16[128,128]{1,0:T(8,128)(2,1)S(1)} %collective-permute-done.13.second, ...), custom_call_target="tpu_custom_call" | custom-call | tf_op jit(solution)/shard_map/pallas_call | solution.py:215
  198.7 5.3 %collective-permute-start.14 = (bf16[128,128]{1,0:T(8,128)(2,1)S(1)}, bf16[128,128]{1,0:T(8,128)(2,1)S(1)}, u32[]{:S(2)}, u32[]{:S(2)}) collective-permute-start(bf16[128,128]{1,0:T(8,128)(2,1)S(1)} %get-tuple-element.105), channel_id=1, source_target_pairs={{0,504},{8,16},{16,8},{24,32},{32,24},{40,48},{48,40},{56,64},{64,... | collective-permute-start | bytes 98312 | tf_op jit(solution)/shard_map/ppermute | solution.py:229
  208.6 3.4 %shard_map.123 = (f32[128,128]{1,0:T(8,128)S(1)}, bf16[128,128]{1,0:T(8,128)(2,1)S(1)}, bf16[128,128]{1,0:T(8,128)(2,1)S(1)}) custom-call(f32[128,128]{1,0:T(8,128)S(1)} %get-tuple-element.104.base, bf16[128,128]{1,0:T(8,128)(2,1)S(1)} %collective-permute-done.14.first, bf16[128,128]{1,0:T(8,128)(2,1)S(1)} %collective-permute-done.15.second, ...), custom_call_target="tpu_custom_call" | custom-call | tf_op jit(solution)/shard_map/pallas_call | solution.py:215
  220.1 3.4 %shard_map.124 = (f32[128,128]{1,0:T(8,128)S(1)}, bf16[128,128]{1,0:T(8,128)(2,1)S(1)}, bf16[128,128]{1,0:T(8,128)(2,1)S(1)}) custom-call(f32[128,128]{1,0:T(8,128)S(1)} %get-tuple-element.107.base, bf16[128,128]{1,0:T(8,128)(2,1)S(1)} %collective-permute-done.16.first, bf16[128,128]{1,0:T(8,128)(2,1)S(1)} %collective-permute-done.17.second, ...), custom_call_target="tpu_custom_call" | custom-call | tf_op jit(solution)/shard_map/pallas_call | solution.py:215
  223.5 5.3 %collective-permute-start.18 = (bf16[128,128]{1,0:T(8,128)(2,1)S(1)}, bf16[128,128]{1,0:T(8,128)(2,1)S(1)}, u32[]{:S(2)}, u32[]{:S(2)}) collective-permute-start(bf16[128,128]{1,0:T(8,128)(2,1)S(1)} %get-tuple-element.111), channel_id=1, source_target_pairs={{0,504},{8,16},{16,8},{24,32},{32,24},{40,48},{48,40},{56,64},{64,... | collective-permute-start | bytes 98312 | tf_op jit(solution)/shard_map/ppermute | solution.py:229
  233.4 3.4 %shard_map.125 = (f32[128,128]{1,0:T(8,128)S(1)}, bf16[128,128]{1,0:T(8,128)(2,1)S(1)}, bf16[128,128]{1,0:T(8,128)(2,1)S(1)}) custom-call(f32[128,128]{1,0:T(8,128)S(1)} %get-tuple-element.110.base, bf16[128,128]{1,0:T(8,128)(2,1)S(1)} %collective-permute-done.18.first, bf16[128,128]{1,0:T(8,128)(2,1)S(1)} %collective-permute-done.19.second, ...), custom_call_target="tpu_custom_call" | custom-call | tf_op jit(solution)/shard_map/pallas_call | solution.py:215
  244.8 3.4 %shard_map.126 = (f32[128,128]{1,0:T(8,128)S(1)}, bf16[128,128]{1,0:T(8,128)(2,1)S(1)}, bf16[128,128]{1,0:T(8,128)(2,1)S(1)}) custom-call(f32[128,128]{1,0:T(8,128)S(1)} %get-tuple-element.113.base, bf16[128,128]{1,0:T(8,128)(2,1)S(1)} %collective-permute-done.20.first, bf16[128,128]{1,0:T(8,128)(2,1)S(1)} %collective-permute-done.21.second, ...), custom_call_target="tpu_custom_call" | custom-call | tf_op jit(solution)/shard_map/pallas_call | solution.py:215
  248.3 5.3 %collective-permute-start.22 = (bf16[128,128]{1,0:T(8,128)(2,1)S(1)}, bf16[128,128]{1,0:T(8,128)(2,1)S(1)}, u32[]{:S(2)}, u32[]{:S(2)}) collective-permute-start(bf16[128,128]{1,0:T(8,128)(2,1)S(1)} %get-tuple-element.117), channel_id=1, source_target_pairs={{0,504},{8,16},{16,8},{24,32},{32,24},{40,48},{48,40},{56,64},{64,... | collective-permute-start | bytes 98312 | tf_op jit(solution)/shard_map/ppermute | solution.py:229
  258.2 20.7 %all_to_all.57 = f32[8,16,128]{2,1,0:T(8,128)S(1)} all-to-all(f32[8,16,128]{2,1,0:T(8,128)S(1)} %bitcast.22), channel_id=1, replica_groups=mesh['region'=64,'depth'=8] {'depth'}, dimensions={0} | all-to-all | bytes 131072 | tf_op jit(solution)/shard_map/all_to_all | solution.py:235
  (99 shorter events, 100.1 us)
Async XLA Ops:
  6.5 107.7 %all-gather.3.cloned.1.call-start = ((), (), s32[]{:S(2)}) async-start(), calls=%async_computation.5 | async-start | bytes 4718592 | tf_op jit(solution)/shard_map/all_gather | solution.py:252
  7.3 128.5 %all-gather.5.cloned.1.call-start = ((), (), s32[]{:S(2)}) async-start(), calls=%async_computation.6 | async-start | bytes 14155776 | tf_op jit(solution)/shard_map/all_gather | solution.py:252
  19.0 17.0 %all-to-all-start = ((bf16[8,144,128]{2,1,0:T(8,128)(2,1)}), bf16[8,144,128]{2,1,0:T(8,128)(2,1)S(1)}, u32[]{:S(2)}, u32[]{:S(2)}) async-start(bf16[8,144,128]{2,1,0:T(8,128)(2,1)} %bitcast.7), calls=%async_computation | async-start | bytes 589824 | tf_op jit(solution)/shard_map/all_to_all | solution.py:235
  37.7 12.0 %collective-permute-start = (bf16[128,128]{1,0:T(8,128)(2,1)S(1)}, bf16[128,128]{1,0:T(8,128)(2,1)S(1)}, u32[]{:S(2)}, u32[]{:S(2)}) collective-permute-start(bf16[128,128]{1,0:T(8,128)(2,1)S(1)} %get-tuple-element.70), channel_id=1, source_target_pairs={{0,504},{8,16},{16,8},{24,32},{32,24},{40,48},{48,40},{56,64},{64,... | collective-permute-start | bytes 98312 | tf_op jit(solution)/shard_map/ppermute | solution.py:229
  47.8 5.1 %collective-permute-start.1 = (bf16[128,128]{1,0:T(8,128)(2,1)S(1)}, bf16[128,128]{1,0:T(8,128)(2,1)S(1)}, u32[]{:S(2)}, u32[]{:S(2)}) collective-permute-start(bf16[128,128]{1,0:T(8,128)(2,1)S(1)} %get-tuple-element.71), channel_id=1, source_target_pairs={{0,8},{8,0},{16,24},{24,16},{32,40},{40,32},{48,56},{56,48},{64,72... | collective-permute-start | bytes 98312 | tf_op jit(solution)/shard_map/ppermute | solution.py:230
  68.2 8.0 %collective-permute-start.2 = (bf16[128,128]{1,0:T(8,128)(2,1)S(1)}, bf16[128,128]{1,0:T(8,128)(2,1)S(1)}, u32[]{:S(2)}, u32[]{:S(2)}) collective-permute-start(bf16[128,128]{1,0:T(8,128)(2,1)S(1)} %get-tuple-element.78), channel_id=1, source_target_pairs={{0,504},{8,16},{16,8},{24,32},{32,24},{40,48},{48,40},{56,64},{64,... | collective-permute-start | bytes 98312 | tf_op jit(solution)/shard_map/ppermute | solution.py:229
  71.3 4.9 %collective-permute-start.3 = (bf16[128,128]{1,0:T(8,128)(2,1)S(1)}, bf16[128,128]{1,0:T(8,128)(2,1)S(1)}, u32[]{:S(2)}, u32[]{:S(2)}) collective-permute-start(bf16[128,128]{1,0:T(8,128)(2,1)S(1)} %get-tuple-element.79), channel_id=1, source_target_pairs={{0,8},{8,0},{16,24},{24,16},{32,40},{40,32},{48,56},{56,48},{64,72... | collective-permute-start | bytes 98312 | tf_op jit(solution)/shard_map/ppermute | solution.py:230
  92.2 8.0 %collective-permute-start.4 = (bf16[128,128]{1,0:T(8,128)(2,1)S(1)}, bf16[128,128]{1,0:T(8,128)(2,1)S(1)}, u32[]{:S(2)}, u32[]{:S(2)}) collective-permute-start(bf16[128,128]{1,0:T(8,128)(2,1)S(1)} %get-tuple-element.83), channel_id=1, source_target_pairs={{0,504},{8,16},{16,8},{24,32},{32,24},{40,48},{48,40},{56,64},{64,... | collective-permute-start | bytes 98312 | tf_op jit(solution)/shard_map/ppermute | solution.py:229
  97.7 5.1 %collective-permute-start.5 = (bf16[128,128]{1,0:T(8,128)(2,1)S(1)}, bf16[128,128]{1,0:T(8,128)(2,1)S(1)}, u32[]{:S(2)}, u32[]{:S(2)}) collective-permute-start(bf16[128,128]{1,0:T(8,128)(2,1)S(1)} %get-tuple-element.84), channel_id=1, source_target_pairs={{0,8},{8,0},{16,24},{24,16},{32,40},{40,32},{48,56},{56,48},{64,72... | collective-permute-start | bytes 98312 | tf_op jit(solution)/shard_map/ppermute | solution.py:230
  103.4 10.8 %all-to-all-start.3 = ((f32[8,16,128]{2,1,0:T(8,128)}), f32[8,16,128]{2,1,0:T(8,128)S(1)}, u32[]{:S(2)}, u32[]{:S(2)}) async-start(f32[8,16,128]{2,1,0:T(8,128)} %bitcast.13), calls=%async_computation.3 | async-start | bytes 131072 | tf_op jit(solution)/shard_map/all_to_all | solution.py:235
  145.9 9.9 %collective-permute-start.6 = (bf16[128,128]{1,0:T(8,128)(2,1)S(1)}, bf16[128,128]{1,0:T(8,128)(2,1)S(1)}, u32[]{:S(2)}, u32[]{:S(2)}) collective-permute-start(bf16[128,128]{1,0:T(8,128)(2,1)S(1)} %get-tuple-element.93), channel_id=1, source_target_pairs={{0,504},{8,16},{16,8},{24,32},{32,24},{40,48},{48,40},{56,64},{64,... | collective-permute-start | bytes 98312 | tf_op jit(solution)/shard_map/ppermute | solution.py:229
  153.9 4.7 %collective-permute-start.7 = (bf16[128,128]{1,0:T(8,128)(2,1)S(1)}, bf16[128,128]{1,0:T(8,128)(2,1)S(1)}, u32[]{:S(2)}, u32[]{:S(2)}) collective-permute-start(bf16[128,128]{1,0:T(8,128)(2,1)S(1)} %get-tuple-element.94), channel_id=1, source_target_pairs={{0,8},{8,0},{16,24},{24,16},{32,40},{40,32},{48,56},{56,48},{64,72... | collective-permute-start | bytes 98312 | tf_op jit(solution)/shard_map/ppermute | solution.py:230
  162.0 8.0 %collective-permute-start.8 = (bf16[128,128]{1,0:T(8,128)(2,1)S(1)}, bf16[128,128]{1,0:T(8,128)(2,1)S(1)}, u32[]{:S(2)}, u32[]{:S(2)}) collective-permute-start(bf16[128,128]{1,0:T(8,128)(2,1)S(1)} %get-tuple-element.96), channel_id=1, source_target_pairs={{0,504},{8,16},{16,8},{24,32},{32,24},{40,48},{48,40},{56,64},{64,... | collective-permute-start | bytes 98312 | tf_op jit(solution)/shard_map/ppermute | solution.py:229
  165.3 4.7 %collective-permute-start.9 = (bf16[128,128]{1,0:T(8,128)(2,1)S(1)}, bf16[128,128]{1,0:T(8,128)(2,1)S(1)}, u32[]{:S(2)}, u32[]{:S(2)}) collective-permute-start(bf16[128,128]{1,0:T(8,128)(2,1)S(1)} %get-tuple-element.97), channel_id=1, source_target_pairs={{0,8},{8,0},{16,24},{24,16},{32,40},{40,32},{48,56},{56,48},{64,72... | collective-permute-start | bytes 98312 | tf_op jit(solution)/shard_map/ppermute | solution.py:230
  173.4 8.0 %collective-permute-start.10 = (bf16[128,128]{1,0:T(8,128)(2,1)S(1)}, bf16[128,128]{1,0:T(8,128)(2,1)S(1)}, u32[]{:S(2)}, u32[]{:S(2)}) collective-permute-start(bf16[128,128]{1,0:T(8,128)(2,1)S(1)} %get-tuple-element.99), channel_id=1, source_target_pairs={{0,504},{8,16},{16,8},{24,32},{32,24},{40,48},{48,40},{56,64},{64,... | collective-permute-start | bytes 98312 | tf_op jit(solution)/shard_map/ppermute | solution.py:229
  178.9 5.0 %collective-permute-start.11 = (bf16[128,128]{1,0:T(8,128)(2,1)S(1)}, bf16[128,128]{1,0:T(8,128)(2,1)S(1)}, u32[]{:S(2)}, u32[]{:S(2)}) collective-permute-start(bf16[128,128]{1,0:T(8,128)(2,1)S(1)} %get-tuple-element.100), channel_id=1, source_target_pairs={{0,8},{8,0},{16,24},{24,16},{32,40},{40,32},{48,56},{56,48},{64,72... | collective-permute-start | bytes 98312 | tf_op jit(solution)/shard_map/ppermute | solution.py:230
  187.3 8.0 %collective-permute-start.12 = (bf16[128,128]{1,0:T(8,128)(2,1)S(1)}, bf16[128,128]{1,0:T(8,128)(2,1)S(1)}, u32[]{:S(2)}, u32[]{:S(2)}) collective-permute-start(bf16[128,128]{1,0:T(8,128)(2,1)S(1)} %get-tuple-element.102), channel_id=1, source_target_pairs={{0,504},{8,16},{16,8},{24,32},{32,24},{40,48},{48,40},{56,64},{64,... | collective-permute-start | bytes 98312 | tf_op jit(solution)/shard_map/ppermute | solution.py:229
  190.3 5.0 %collective-permute-start.13 = (bf16[128,128]{1,0:T(8,128)(2,1)S(1)}, bf16[128,128]{1,0:T(8,128)(2,1)S(1)}, u32[]{:S(2)}, u32[]{:S(2)}) collective-permute-start(bf16[128,128]{1,0:T(8,128)(2,1)S(1)} %get-tuple-element.103), channel_id=1, source_target_pairs={{0,8},{8,0},{16,24},{24,16},{32,40},{40,32},{48,56},{56,48},{64,72... | collective-permute-start | bytes 98312 | tf_op jit(solution)/shard_map/ppermute | solution.py:230
  198.7 8.0 %collective-permute-start.14 = (bf16[128,128]{1,0:T(8,128)(2,1)S(1)}, bf16[128,128]{1,0:T(8,128)(2,1)S(1)}, u32[]{:S(2)}, u32[]{:S(2)}) collective-permute-start(bf16[128,128]{1,0:T(8,128)(2,1)S(1)} %get-tuple-element.105), channel_id=1, source_target_pairs={{0,504},{8,16},{16,8},{24,32},{32,24},{40,48},{48,40},{56,64},{64,... | collective-permute-start | bytes 98312 | tf_op jit(solution)/shard_map/ppermute | solution.py:229
  212.1 8.0 %collective-permute-start.16 = (bf16[128,128]{1,0:T(8,128)(2,1)S(1)}, bf16[128,128]{1,0:T(8,128)(2,1)S(1)}, u32[]{:S(2)}, u32[]{:S(2)}) collective-permute-start(bf16[128,128]{1,0:T(8,128)(2,1)S(1)} %get-tuple-element.108), channel_id=1, source_target_pairs={{0,504},{8,16},{16,8},{24,32},{32,24},{40,48},{48,40},{56,64},{64,... | collective-permute-start | bytes 98312 | tf_op jit(solution)/shard_map/ppermute | solution.py:229
  223.5 8.0 %collective-permute-start.18 = (bf16[128,128]{1,0:T(8,128)(2,1)S(1)}, bf16[128,128]{1,0:T(8,128)(2,1)S(1)}, u32[]{:S(2)}, u32[]{:S(2)}) collective-permute-start(bf16[128,128]{1,0:T(8,128)(2,1)S(1)} %get-tuple-element.111), channel_id=1, source_target_pairs={{0,504},{8,16},{16,8},{24,32},{32,24},{40,48},{48,40},{56,64},{64,... | collective-permute-start | bytes 98312 | tf_op jit(solution)/shard_map/ppermute | solution.py:229
  236.9 8.0 %collective-permute-start.20 = (bf16[128,128]{1,0:T(8,128)(2,1)S(1)}, bf16[128,128]{1,0:T(8,128)(2,1)S(1)}, u32[]{:S(2)}, u32[]{:S(2)}) collective-permute-start(bf16[128,128]{1,0:T(8,128)(2,1)S(1)} %get-tuple-element.114), channel_id=1, source_target_pairs={{0,504},{8,16},{16,8},{24,32},{32,24},{40,48},{48,40},{56,64},{64,... | collective-permute-start | bytes 98312 | tf_op jit(solution)/shard_map/ppermute | solution.py:229
  248.3 8.0 %collective-permute-start.22 = (bf16[128,128]{1,0:T(8,128)(2,1)S(1)}, bf16[128,128]{1,0:T(8,128)(2,1)S(1)}, u32[]{:S(2)}, u32[]{:S(2)}) collective-permute-start(bf16[128,128]{1,0:T(8,128)(2,1)S(1)} %get-tuple-element.117), channel_id=1, source_target_pairs={{0,504},{8,16},{16,8},{24,32},{32,24},{40,48},{48,40},{56,64},{64,... | collective-permute-start | bytes 98312 | tf_op jit(solution)/shard_map/ppermute | solution.py:229
  253.6 4.7 %collective-permute-start.23 = (bf16[128,128]{1,0:T(8,128)(2,1)S(1)}, bf16[128,128]{1,0:T(8,128)(2,1)S(1)}, u32[]{:S(2)}, u32[]{:S(2)}) collective-permute-start(bf16[128,128]{1,0:T(8,128)(2,1)S(1)} %get-tuple-element.118), channel_id=1, source_target_pairs={{0,8},{8,0},{16,24},{24,16},{32,40},{40,32},{48,56},{56,48},{64,72... | collective-permute-start | bytes 98312 | tf_op jit(solution)/shard_map/ppermute | solution.py:230
  (25 other events, 169.9 us)
Sparse Core Ops, SparseCore 0:
  9.5 45.7 all-gather.2
  57.5 78.2 all-gather.4

commit v8 on v4

--- a/solution.py
+++ b/solution.py
@@ -76,9 +76,7 @@
 
 
 def placed(place, product):
-    high = product.astype(BF)
-    low = (product - high.astype(F32)).astype(BF)
-    return dot(place[...], high) + dot(place[...], low)
+    return dot(place[...], product.astype(BF))
 
 
 def open_kernel(
@@ -306,7 +304,6 @@
     rows = GROUPS * l_slots * PAIR
     scratch = [pltpu.VMEM((rows, CELLS), kind) for kind in (BF, BF, F32)]
     (value,) = call(sum_kernel, [state], base, *received)
-    value, gathered = lax.optimization_barrier((value, gathered))
     value = to_depth(value)
     for step in range(LEVEL_STEPS, STEPS):
         if step == LEVEL_STEPS:

time: 267 us -> 263 us (0.985)
  Pallas kernels: 39.3 us -> 35.8 us
    pallas_call x21, Pallas kernels: 39.3 us -> 35.8 us  [call(): pl.pallas_call(body, out_shape=[jax.ShapeDtypeStruct(shape, kind) for sha...]
where the time goes in v8:
time: 263 us; the launch traced here: 262 us
  starting transfers between devices  94.7 us (36%)
  blocking collectives  61.1 us (23%)
  waiting for transfers between devices  43.4 us (17%)
  Pallas kernels  35.8 us (14%)
  between operations  14.6 us (6%)
  local copies, waits for them, and re-layouts  9.1 us (3%)
  other arithmetic  3.12 us (1%)
    all_to_all x4, blocking collectives, to_depth(): lax.all_to_all(value, 'depth', split_axis=0, concat_axis=0, tiled=True)  61.1 us
    ppermute x12, starting transfers between devices, swapped(): from_first = lax.ppermute(to_first, 'region', first)  55.1 us
    pallas_call x21, Pallas kernels, call(): pl.pallas_call(body, out_shape=[jax.ShapeDtypeStruct(shape, kind) for sha...  35.8 us
    ppermute x12, starting transfers between devices, swapped(): from_second = lax.ppermute(to_second, 'region', second)  23.4 us
    ppermute x12, waiting for transfers between devices, swapped(): from_first = lax.ppermute(to_first, 'region', first)  19.7 us
    all_to_all x2, starting transfers between devices, to_depth(): lax.all_to_all(value, 'depth', split_axis=0, concat_axis=0, tiled=True)  16.2 us
    ppermute x12, waiting for transfers between devices, swapped(): from_second = lax.ppermute(to_second, 'region', second)  14.7 us
    unnamed x36, local copies, waits for them, and re-layouts  9.1 us
  transfers between devices with their start and end apart: 27, of which 20 were waited for; matrix products, arithmetic and copies ran while one was open for 0% of the time, Pallas kernels for 4%

profile of v8, /device:TPU:1, one launch (start us, length us, event | category | flops | bytes accessed | tf_op | source)
XLA Modules:
  0.0 261.8 jit_solution(13409863939949414320)
XLA Ops:
  6.5 3.1 %pad_maximum_fusion = bf16[64,128,128]{2,1,0:T(8,128)(2,1)} fusion(bf16[16,128,128]{2,1,0:T(8,128)(2,1)} %tiles.14, bf16[48,128,128]{2,1,0:T(8,128)(2,1)} %tiles.15), kind=kLoop, calls=%fused_computation | loop fusion | flops 1048576 | bytes 4194304 | tf_op jit(solution)/shard_map/concatenate | solution.py:248
  13.0 10.8 %all-to-all-start = ((bf16[8,144,128]{2,1,0:T(8,128)(2,1)}), bf16[8,144,128]{2,1,0:T(8,128)(2,1)}, u32[]{:S(2)}, u32[]{:S(2)}) async-start(bf16[8,144,128]{2,1,0:T(8,128)(2,1)} %bitcast.7), calls=%async_computation | async-start | bytes 589824 | tf_op jit(solution)/shard_map/all_to_all | solution.py:231
  25.1 5.7 %all-to-all-done = bf16[8,144,128]{2,1,0:T(8,128)(2,1)} async-done(((bf16[8,144,128]{2,1,0:T(8,128)(2,1)}), bf16[8,144,128]{2,1,0:T(8,128)(2,1)}, u32[]{:S(2)}, u32[]{:S(2)}) %all-to-all-start) | async-done | bytes 294944 | tf_op jit(solution)/shard_map/all_to_all | solution.py:231
  34.5 8.5 %collective-permute-start = (bf16[128,128]{1,0:T(8,128)(2,1)S(1)}, bf16[128,128]{1,0:T(8,128)(2,1)S(1)}, u32[]{:S(2)}, u32[]{:S(2)}) collective-permute-start(bf16[128,128]{1,0:T(8,128)(2,1)S(1)} %get-tuple-element.72), channel_id=1, source_target_pairs={{0,504},{8,16},{16,8},{24,32},{32,24},{40,48},{48,40},{56,64},{64,... | collective-permute-start | bytes 98312 | tf_op jit(solution)/shard_map/ppermute | solution.py:225
  45.0 3.1 %collective-permute-done.1.second = bf16[128,128]{1,0:T(8,128)(2,1)S(1)} collective-permute-done((bf16[128,128]{1,0:T(8,128)(2,1)S(1)}, bf16[128,128]{1,0:T(8,128)(2,1)S(1)}, u32[]{:S(2)}, u32[]{:S(2)}) %collective-permute-start.1) | collective-permute-done | bytes 32800 | tf_op jit(solution)/shard_map/ppermute | solution.py:226
  48.7 14.3 %all_to_all.66 = bf16[8,128,128]{2,1,0:T(8,128)(2,1)S(1)} all-to-all(bf16[8,128,128]{2,1,0:T(8,128)(2,1)S(1)} %bitcast.26), channel_id=1, replica_groups=mesh['region'=64,'depth'=8] {'depth'}, dimensions={0} | all-to-all | bytes 524288 | tf_op jit(solution)/shard_map/all_to_all | solution.py:231
  72.5 14.1 %all_to_all.67 = bf16[8,128,128]{2,1,0:T(8,128)(2,1)S(1)} all-to-all(bf16[8,128,128]{2,1,0:T(8,128)(2,1)S(1)} %bitcast.27), channel_id=1, replica_groups=mesh['region'=64,'depth'=8] {'depth'}, dimensions={0} | all-to-all | bytes 524288 | tf_op jit(solution)/shard_map/all_to_all | solution.py:231
  87.4 5.6 %collective-permute-start.4 = (bf16[128,128]{1,0:T(8,128)(2,1)S(1)}, bf16[128,128]{1,0:T(8,128)(2,1)S(1)}, u32[]{:S(2)}, u32[]{:S(2)}) collective-permute-start(bf16[128,128]{1,0:T(8,128)(2,1)S(1)} %get-tuple-element.85), channel_id=1, source_target_pairs={{0,504},{8,16},{16,8},{24,32},{32,24},{40,48},{48,40},{56,64},{64,... | collective-permute-start | bytes 98312 | tf_op jit(solution)/shard_map/ppermute | solution.py:225
  98.7 14.1 %all_to_all.68 = bf16[8,128,128]{2,1,0:T(8,128)(2,1)S(1)} all-to-all(bf16[8,128,128]{2,1,0:T(8,128)(2,1)S(1)} %bitcast.25), channel_id=1, replica_groups=mesh['region'=64,'depth'=8] {'depth'}, dimensions={0} | all-to-all | bytes 524288 | tf_op jit(solution)/shard_map/all_to_all | solution.py:231
  122.2 5.3 %all-to-all-start.4 = ((f32[8,16,128]{2,1,0:T(8,128)}), f32[8,16,128]{2,1,0:T(8,128)S(1)}, u32[]{:S(2)}, u32[]{:S(2)}) async-start(f32[8,16,128]{2,1,0:T(8,128)} %bitcast.15), calls=%async_computation.4 | async-start | bytes 131072 | tf_op jit(solution)/shard_map/all_to_all | solution.py:231
  129.2 3.2 %all-to-all-done.4 = f32[8,16,128]{2,1,0:T(8,128)S(1)} async-done(((f32[8,16,128]{2,1,0:T(8,128)}), f32[8,16,128]{2,1,0:T(8,128)S(1)}, u32[]{:S(2)}, u32[]{:S(2)}) %all-to-all-start.4) | async-done | bytes 65568 | tf_op jit(solution)/shard_map/all_to_all | solution.py:231
  132.4 5.8 %copy-done = bf16[512,128,128]{2,1,0:T(8,128)(2,1)S(1)} copy-done((bf16[512,128,128]{2,1,0:T(8,128)(2,1)S(1)}, bf16[512,128,128]{2,1,0:T(8,128)(2,1)}, u32[]{:S(2)}) %copy-start) | copy-done | bytes 16777240
  141.3 5.8 %collective-permute-start.8 = (bf16[128,128]{1,0:T(8,128)(2,1)S(1)}, bf16[128,128]{1,0:T(8,128)(2,1)S(1)}, u32[]{:S(2)}, u32[]{:S(2)}) collective-permute-start(bf16[128,128]{1,0:T(8,128)(2,1)S(1)} %get-tuple-element.100), channel_id=1, source_target_pairs={{0,504},{8,16},{16,8},{24,32},{32,24},{40,48},{48,40},{56,64},{64,... | collective-permute-start | bytes 98312 | tf_op jit(solution)/shard_map/ppermute | solution.py:225
  151.8 3.1 %shard_map.121 = (f32[128,128]{1,0:T(8,128)S(1)}, bf16[128,128]{1,0:T(8,128)(2,1)S(1)}, bf16[128,128]{1,0:T(8,128)(2,1)S(1)}) custom-call(f32[128,128]{1,0:T(8,128)S(1)} %get-tuple-element.99.base, bf16[128,128]{1,0:T(8,128)(2,1)S(1)} %collective-permute-done.8.first, bf16[128,128]{1,0:T(8,128)(2,1)S(1)} %collective-permute-done.9.second, ...), custom_call_target="tpu_custom_call" | custom-call | tf_op jit(solution)/shard_map/pallas_call | solution.py:211
  154.9 3.3 %collective-permute-start.10 = (bf16[128,128]{1,0:T(8,128)(2,1)S(1)}, bf16[128,128]{1,0:T(8,128)(2,1)S(1)}, u32[]{:S(2)}, u32[]{:S(2)}) collective-permute-start(bf16[128,128]{1,0:T(8,128)(2,1)S(1)} %get-tuple-element.103), channel_id=1, source_target_pairs={{0,504},{8,16},{16,8},{24,32},{32,24},{40,48},{48,40},{56,64},{64,... | collective-permute-start | bytes 98312 | tf_op jit(solution)/shard_map/ppermute | solution.py:225
  162.9 3.1 %shard_map.122 = (f32[128,128]{1,0:T(8,128)S(1)}, bf16[128,128]{1,0:T(8,128)(2,1)S(1)}, bf16[128,128]{1,0:T(8,128)(2,1)S(1)}) custom-call(f32[128,128]{1,0:T(8,128)S(1)} %get-tuple-element.102.base, bf16[128,128]{1,0:T(8,128)(2,1)S(1)} %collective-permute-done.10.first, bf16[128,128]{1,0:T(8,128)(2,1)S(1)} %collective-permute-done.11.second, ...), custom_call_target="tpu_custom_call" | custom-call | tf_op jit(solution)/shard_map/pallas_call | solution.py:211
  166.0 5.6 %collective-permute-start.12 = (bf16[128,128]{1,0:T(8,128)(2,1)S(1)}, bf16[128,128]{1,0:T(8,128)(2,1)S(1)}, u32[]{:S(2)}, u32[]{:S(2)}) collective-permute-start(bf16[128,128]{1,0:T(8,128)(2,1)S(1)} %get-tuple-element.106), channel_id=1, source_target_pairs={{0,504},{8,16},{16,8},{24,32},{32,24},{40,48},{48,40},{56,64},{64,... | collective-permute-start | bytes 98312 | tf_op jit(solution)/shard_map/ppermute | solution.py:225
  176.5 3.1 %shard_map.123 = (f32[128,128]{1,0:T(8,128)S(1)}, bf16[128,128]{1,0:T(8,128)(2,1)S(1)}, bf16[128,128]{1,0:T(8,128)(2,1)S(1)}) custom-call(f32[128,128]{1,0:T(8,128)S(1)} %get-tuple-element.105.base, bf16[128,128]{1,0:T(8,128)(2,1)S(1)} %collective-permute-done.12.first, bf16[128,128]{1,0:T(8,128)(2,1)S(1)} %collective-permute-done.13.second, ...), custom_call_target="tpu_custom_call" | custom-call | tf_op jit(solution)/shard_map/pallas_call | solution.py:211
  187.5 3.1 %shard_map.124 = (f32[128,128]{1,0:T(8,128)S(1)}, bf16[128,128]{1,0:T(8,128)(2,1)S(1)}, bf16[128,128]{1,0:T(8,128)(2,1)S(1)}) custom-call(f32[128,128]{1,0:T(8,128)S(1)} %get-tuple-element.108.base, bf16[128,128]{1,0:T(8,128)(2,1)S(1)} %collective-permute-done.14.first, bf16[128,128]{1,0:T(8,128)(2,1)S(1)} %collective-permute-done.15.second, ...), custom_call_target="tpu_custom_call" | custom-call | tf_op jit(solution)/shard_map/pallas_call | solution.py:211
  190.6 5.3 %collective-permute-start.16 = (bf16[128,128]{1,0:T(8,128)(2,1)S(1)}, bf16[128,128]{1,0:T(8,128)(2,1)S(1)}, u32[]{:S(2)}, u32[]{:S(2)}) collective-permute-start(bf16[128,128]{1,0:T(8,128)(2,1)S(1)} %get-tuple-element.112), channel_id=1, source_target_pairs={{0,504},{8,16},{16,8},{24,32},{32,24},{40,48},{48,40},{56,64},{64,... | collective-permute-start | bytes 98312 | tf_op jit(solution)/shard_map/ppermute | solution.py:225
  203.7 3.3 %collective-permute-start.18 = (bf16[128,128]{1,0:T(8,128)(2,1)S(1)}, bf16[128,128]{1,0:T(8,128)(2,1)S(1)}, u32[]{:S(2)}, u32[]{:S(2)}) collective-permute-start(bf16[128,128]{1,0:T(8,128)(2,1)S(1)} %get-tuple-element.115), channel_id=1, source_target_pairs={{0,504},{8,16},{16,8},{24,32},{32,24},{40,48},{48,40},{56,64},{64,... | collective-permute-start | bytes 98312 | tf_op jit(solution)/shard_map/ppermute | solution.py:225
  214.7 5.3 %collective-permute-start.20 = (bf16[128,128]{1,0:T(8,128)(2,1)S(1)}, bf16[128,128]{1,0:T(8,128)(2,1)S(1)}, u32[]{:S(2)}, u32[]{:S(2)}) collective-permute-start(bf16[128,128]{1,0:T(8,128)(2,1)S(1)} %get-tuple-element.118), channel_id=1, source_target_pairs={{0,504},{8,16},{16,8},{24,32},{32,24},{40,48},{48,40},{56,64},{64,... | collective-permute-start | bytes 98312 | tf_op jit(solution)/shard_map/ppermute | solution.py:225
  227.8 3.3 %collective-permute-start.22 = (bf16[128,128]{1,0:T(8,128)(2,1)S(1)}, bf16[128,128]{1,0:T(8,128)(2,1)S(1)}, u32[]{:S(2)}, u32[]{:S(2)}) collective-permute-start(bf16[128,128]{1,0:T(8,128)(2,1)S(1)} %get-tuple-element.121), channel_id=1, source_target_pairs={{0,504},{8,16},{16,8},{24,32},{32,24},{40,48},{48,40},{56,64},{64,... | collective-permute-start | bytes 98312 | tf_op jit(solution)/shard_map/ppermute | solution.py:225
  235.8 18.6 %all_to_all.69 = f32[8,16,128]{2,1,0:T(8,128)S(1)} all-to-all(f32[8,16,128]{2,1,0:T(8,128)S(1)} %bitcast.23), channel_id=1, replica_groups=mesh['region'=64,'depth'=8] {'depth'}, dimensions={0} | all-to-all | bytes 131072 | tf_op jit(solution)/shard_map/all_to_all | solution.py:231
  (93 shorter events, 90.7 us)
Async XLA Ops:
  6.5 125.9 %all-gather.2.cloned.1.call-start = ((), (), s32[]{:S(2)}) async-start(), calls=%async_computation.6 | async-start | bytes 18874368 | tf_op jit(solution)/shard_map/all_gather | solution.py:247
  13.0 17.8 %all-to-all-start = ((bf16[8,144,128]{2,1,0:T(8,128)(2,1)}), bf16[8,144,128]{2,1,0:T(8,128)(2,1)}, u32[]{:S(2)}, u32[]{:S(2)}) async-start(bf16[8,144,128]{2,1,0:T(8,128)(2,1)} %bitcast.7), calls=%async_computation | async-start | bytes 589824 | tf_op jit(solution)/shard_map/all_to_all | solution.py:231
  34.5 10.5 %collective-permute-start = (bf16[128,128]{1,0:T(8,128)(2,1)S(1)}, bf16[128,128]{1,0:T(8,128)(2,1)S(1)}, u32[]{:S(2)}, u32[]{:S(2)}) collective-permute-start(bf16[128,128]{1,0:T(8,128)(2,1)S(1)} %get-tuple-element.72), channel_id=1, source_target_pairs={{0,504},{8,16},{16,8},{24,32},{32,24},{40,48},{48,40},{56,64},{64,... | collective-permute-start | bytes 98312 | tf_op jit(solution)/shard_map/ppermute | solution.py:225
  43.0 5.1 %collective-permute-start.1 = (bf16[128,128]{1,0:T(8,128)(2,1)S(1)}, bf16[128,128]{1,0:T(8,128)(2,1)S(1)}, u32[]{:S(2)}, u32[]{:S(2)}) collective-permute-start(bf16[128,128]{1,0:T(8,128)(2,1)S(1)} %get-tuple-element.73), channel_id=1, source_target_pairs={{0,8},{8,0},{16,24},{24,16},{32,40},{40,32},{48,56},{56,48},{64,72... | collective-permute-start | bytes 98312 | tf_op jit(solution)/shard_map/ppermute | solution.py:226
  63.8 8.0 %collective-permute-start.2 = (bf16[128,128]{1,0:T(8,128)(2,1)S(1)}, bf16[128,128]{1,0:T(8,128)(2,1)S(1)}, u32[]{:S(2)}, u32[]{:S(2)}) collective-permute-start(bf16[128,128]{1,0:T(8,128)(2,1)S(1)} %get-tuple-element.80), channel_id=1, source_target_pairs={{0,504},{8,16},{16,8},{24,32},{32,24},{40,48},{48,40},{56,64},{64,... | collective-permute-start | bytes 98312 | tf_op jit(solution)/shard_map/ppermute | solution.py:225
  66.8 5.1 %collective-permute-start.3 = (bf16[128,128]{1,0:T(8,128)(2,1)S(1)}, bf16[128,128]{1,0:T(8,128)(2,1)S(1)}, u32[]{:S(2)}, u32[]{:S(2)}) collective-permute-start(bf16[128,128]{1,0:T(8,128)(2,1)S(1)} %get-tuple-element.81), channel_id=1, source_target_pairs={{0,8},{8,0},{16,24},{24,16},{32,40},{40,32},{48,56},{56,48},{64,72... | collective-permute-start | bytes 98312 | tf_op jit(solution)/shard_map/ppermute | solution.py:226
  87.4 8.0 %collective-permute-start.4 = (bf16[128,128]{1,0:T(8,128)(2,1)S(1)}, bf16[128,128]{1,0:T(8,128)(2,1)S(1)}, u32[]{:S(2)}, u32[]{:S(2)}) collective-permute-start(bf16[128,128]{1,0:T(8,128)(2,1)S(1)} %get-tuple-element.85), channel_id=1, source_target_pairs={{0,504},{8,16},{16,8},{24,32},{32,24},{40,48},{48,40},{56,64},{64,... | collective-permute-start | bytes 98312 | tf_op jit(solution)/shard_map/ppermute | solution.py:225
  93.0 5.1 %collective-permute-start.5 = (bf16[128,128]{1,0:T(8,128)(2,1)S(1)}, bf16[128,128]{1,0:T(8,128)(2,1)S(1)}, u32[]{:S(2)}, u32[]{:S(2)}) collective-permute-start(bf16[128,128]{1,0:T(8,128)(2,1)S(1)} %get-tuple-element.86), channel_id=1, source_target_pairs={{0,8},{8,0},{16,24},{24,16},{32,40},{40,32},{48,56},{56,48},{64,72... | collective-permute-start | bytes 98312 | tf_op jit(solution)/shard_map/ppermute | solution.py:226
  113.6 8.0 %collective-permute-start.6 = (bf16[128,128]{1,0:T(8,128)(2,1)S(1)}, bf16[128,128]{1,0:T(8,128)(2,1)S(1)}, u32[]{:S(2)}, u32[]{:S(2)}) collective-permute-start(bf16[128,128]{1,0:T(8,128)(2,1)S(1)} %get-tuple-element.90), channel_id=1, source_target_pairs={{0,504},{8,16},{16,8},{24,32},{32,24},{40,48},{48,40},{56,64},{64,... | collective-permute-start | bytes 98312 | tf_op jit(solution)/shard_map/ppermute | solution.py:225
  116.6 4.9 %collective-permute-start.7 = (bf16[128,128]{1,0:T(8,128)(2,1)S(1)}, bf16[128,128]{1,0:T(8,128)(2,1)S(1)}, u32[]{:S(2)}, u32[]{:S(2)}) collective-permute-start(bf16[128,128]{1,0:T(8,128)(2,1)S(1)} %get-tuple-element.91), channel_id=1, source_target_pairs={{0,8},{8,0},{16,24},{24,16},{32,40},{40,32},{48,56},{56,48},{64,72... | collective-permute-start | bytes 98312 | tf_op jit(solution)/shard_map/ppermute | solution.py:226
  122.2 10.2 %all-to-all-start.4 = ((f32[8,16,128]{2,1,0:T(8,128)}), f32[8,16,128]{2,1,0:T(8,128)S(1)}, u32[]{:S(2)}, u32[]{:S(2)}) async-start(f32[8,16,128]{2,1,0:T(8,128)} %bitcast.15), calls=%async_computation.4 | async-start | bytes 131072 | tf_op jit(solution)/shard_map/all_to_all | solution.py:231
  141.3 8.2 %collective-permute-start.8 = (bf16[128,128]{1,0:T(8,128)(2,1)S(1)}, bf16[128,128]{1,0:T(8,128)(2,1)S(1)}, u32[]{:S(2)}, u32[]{:S(2)}) collective-permute-start(bf16[128,128]{1,0:T(8,128)(2,1)S(1)} %get-tuple-element.100), channel_id=1, source_target_pairs={{0,504},{8,16},{16,8},{24,32},{32,24},{40,48},{48,40},{56,64},{64,... | collective-permute-start | bytes 98312 | tf_op jit(solution)/shard_map/ppermute | solution.py:225
  147.1 4.7 %collective-permute-start.9 = (bf16[128,128]{1,0:T(8,128)(2,1)S(1)}, bf16[128,128]{1,0:T(8,128)(2,1)S(1)}, u32[]{:S(2)}, u32[]{:S(2)}) collective-permute-start(bf16[128,128]{1,0:T(8,128)(2,1)S(1)} %get-tuple-element.101), channel_id=1, source_target_pairs={{0,8},{8,0},{16,24},{24,16},{32,40},{40,32},{48,56},{56,48},{64,72... | collective-permute-start | bytes 98312 | tf_op jit(solution)/shard_map/ppermute | solution.py:226
  154.9 8.0 %collective-permute-start.10 = (bf16[128,128]{1,0:T(8,128)(2,1)S(1)}, bf16[128,128]{1,0:T(8,128)(2,1)S(1)}, u32[]{:S(2)}, u32[]{:S(2)}) collective-permute-start(bf16[128,128]{1,0:T(8,128)(2,1)S(1)} %get-tuple-element.103), channel_id=1, source_target_pairs={{0,504},{8,16},{16,8},{24,32},{32,24},{40,48},{48,40},{56,64},{64,... | collective-permute-start | bytes 98312 | tf_op jit(solution)/shard_map/ppermute | solution.py:225
  158.2 4.7 %collective-permute-start.11 = (bf16[128,128]{1,0:T(8,128)(2,1)S(1)}, bf16[128,128]{1,0:T(8,128)(2,1)S(1)}, u32[]{:S(2)}, u32[]{:S(2)}) collective-permute-start(bf16[128,128]{1,0:T(8,128)(2,1)S(1)} %get-tuple-element.104), channel_id=1, source_target_pairs={{0,8},{8,0},{16,24},{24,16},{32,40},{40,32},{48,56},{56,48},{64,72... | collective-permute-start | bytes 98312 | tf_op jit(solution)/shard_map/ppermute | solution.py:226
  166.0 8.0 %collective-permute-start.12 = (bf16[128,128]{1,0:T(8,128)(2,1)S(1)}, bf16[128,128]{1,0:T(8,128)(2,1)S(1)}, u32[]{:S(2)}, u32[]{:S(2)}) collective-permute-start(bf16[128,128]{1,0:T(8,128)(2,1)S(1)} %get-tuple-element.106), channel_id=1, source_target_pairs={{0,504},{8,16},{16,8},{24,32},{32,24},{40,48},{48,40},{56,64},{64,... | collective-permute-start | bytes 98312 | tf_op jit(solution)/shard_map/ppermute | solution.py:225
  171.5 5.0 %collective-permute-start.13 = (bf16[128,128]{1,0:T(8,128)(2,1)S(1)}, bf16[128,128]{1,0:T(8,128)(2,1)S(1)}, u32[]{:S(2)}, u32[]{:S(2)}) collective-permute-start(bf16[128,128]{1,0:T(8,128)(2,1)S(1)} %get-tuple-element.107), channel_id=1, source_target_pairs={{0,8},{8,0},{16,24},{24,16},{32,40},{40,32},{48,56},{56,48},{64,72... | collective-permute-start | bytes 98312 | tf_op jit(solution)/shard_map/ppermute | solution.py:226
  179.6 8.0 %collective-permute-start.14 = (bf16[128,128]{1,0:T(8,128)(2,1)S(1)}, bf16[128,128]{1,0:T(8,128)(2,1)S(1)}, u32[]{:S(2)}, u32[]{:S(2)}) collective-permute-start(bf16[128,128]{1,0:T(8,128)(2,1)S(1)} %get-tuple-element.109), channel_id=1, source_target_pairs={{0,504},{8,16},{16,8},{24,32},{32,24},{40,48},{48,40},{56,64},{64,... | collective-permute-start | bytes 98312 | tf_op jit(solution)/shard_map/ppermute | solution.py:225
  182.6 5.0 %collective-permute-start.15 = (bf16[128,128]{1,0:T(8,128)(2,1)S(1)}, bf16[128,128]{1,0:T(8,128)(2,1)S(1)}, u32[]{:S(2)}, u32[]{:S(2)}) collective-permute-start(bf16[128,128]{1,0:T(8,128)(2,1)S(1)} %get-tuple-element.110), channel_id=1, source_target_pairs={{0,8},{8,0},{16,24},{24,16},{32,40},{40,32},{48,56},{56,48},{64,72... | collective-permute-start | bytes 98312 | tf_op jit(solution)/shard_map/ppermute | solution.py:226
  190.6 8.0 %collective-permute-start.16 = (bf16[128,128]{1,0:T(8,128)(2,1)S(1)}, bf16[128,128]{1,0:T(8,128)(2,1)S(1)}, u32[]{:S(2)}, u32[]{:S(2)}) collective-permute-start(bf16[128,128]{1,0:T(8,128)(2,1)S(1)} %get-tuple-element.112), channel_id=1, source_target_pairs={{0,504},{8,16},{16,8},{24,32},{32,24},{40,48},{48,40},{56,64},{64,... | collective-permute-start | bytes 98312 | tf_op jit(solution)/shard_map/ppermute | solution.py:225
  203.7 8.0 %collective-permute-start.18 = (bf16[128,128]{1,0:T(8,128)(2,1)S(1)}, bf16[128,128]{1,0:T(8,128)(2,1)S(1)}, u32[]{:S(2)}, u32[]{:S(2)}) collective-permute-start(bf16[128,128]{1,0:T(8,128)(2,1)S(1)} %get-tuple-element.115), channel_id=1, source_target_pairs={{0,504},{8,16},{16,8},{24,32},{32,24},{40,48},{48,40},{56,64},{64,... | collective-permute-start | bytes 98312 | tf_op jit(solution)/shard_map/ppermute | solution.py:225
  207.0 4.7 %collective-permute-start.19 = (bf16[128,128]{1,0:T(8,128)(2,1)S(1)}, bf16[128,128]{1,0:T(8,128)(2,1)S(1)}, u32[]{:S(2)}, u32[]{:S(2)}) collective-permute-start(bf16[128,128]{1,0:T(8,128)(2,1)S(1)} %get-tuple-element.116), channel_id=1, source_target_pairs={{0,8},{8,0},{16,24},{24,16},{32,40},{40,32},{48,56},{56,48},{64,72... | collective-permute-start | bytes 98312 | tf_op jit(solution)/shard_map/ppermute | solution.py:226
  214.7 8.0 %collective-permute-start.20 = (bf16[128,128]{1,0:T(8,128)(2,1)S(1)}, bf16[128,128]{1,0:T(8,128)(2,1)S(1)}, u32[]{:S(2)}, u32[]{:S(2)}) collective-permute-start(bf16[128,128]{1,0:T(8,128)(2,1)S(1)} %get-tuple-element.118), channel_id=1, source_target_pairs={{0,504},{8,16},{16,8},{24,32},{32,24},{40,48},{48,40},{56,64},{64,... | collective-permute-start | bytes 98312 | tf_op jit(solution)/shard_map/ppermute | solution.py:225
  227.8 8.0 %collective-permute-start.22 = (bf16[128,128]{1,0:T(8,128)(2,1)S(1)}, bf16[128,128]{1,0:T(8,128)(2,1)S(1)}, u32[]{:S(2)}, u32[]{:S(2)}) collective-permute-start(bf16[128,128]{1,0:T(8,128)(2,1)S(1)} %get-tuple-element.121), channel_id=1, source_target_pairs={{0,504},{8,16},{16,8},{24,32},{32,24},{40,48},{48,40},{56,64},{64,... | collective-permute-start | bytes 98312 | tf_op jit(solution)/shard_map/ppermute | solution.py:225
  (21 other events, 96.1 us)
Sparse Core Ops, SparseCore 0:
  9.9 106.7 all-gather.1
